TPU v7x, 512 devices: a whole 4x4x16 slice. The times are simulated.
512 devices in a mesh: row: 4 (over x), col: 16 (over z), depth: 8 (over y, core).
Axes of the slice: x: 4, y: 4, z: 16, core: 2. Of those that a mesh axis runs over, the one named last changes fastest.
Arguments:
- tokens: bfloat16 [512, 8192], P(('row', 'depth'), 'col'), may hold values from -6 to 6
- cotangent: bfloat16 [512, 8192], P(('row', 'depth'), 'col'), may hold values from -6 to 6
- gate_weight: bfloat16 [8192, 14336], P('col', ('row', 'depth')), may hold values from -0.0625 to 0.0625
- up_weight: bfloat16 [8192, 14336], P('col', ('row', 'depth')), may hold values from -0.0625 to 0.0625
- down_weight: bfloat16 [14336, 8192], P(('row', 'depth'), 'col'), may hold values from -0.046875 to 0.046875
Outputs:
- layer_out: bfloat16 [512, 8192], P(('row', 'depth'), 'col')
- tokens_grad: bfloat16 [512, 8192], P(('row', 'depth'), 'col')
- gate_grad: bfloat16 [8192, 14336], P('col', ('row', 'depth'))
- up_grad: bfloat16 [8192, 14336], P('col', ('row', 'depth'))
- down_grad: bfloat16 [14336, 8192], P(('row', 'depth'), 'col')
All inputs are finite; a program needn't handle non-finite values.
Results may differ from a plain program's by a relative error of at most 0.0049.
Values may be sent and summed in bfloat16 or wider, within the bound.
No kernel may reach another device: no remote copies, remote signals or barrier semaphores. Data moves between devices by JAX's collectives and lax.ppermute only.
A program may use at most 64 MiB of HBM per device.

v0:
```python
import math

import jax
import jax.numpy as jnp
from jax import lax
from jax.sharding import PartitionSpec as P


def swish_pair(gate_sum, up_sum):
    sigmoid_gate = jax.nn.sigmoid(gate_sum)
    return (gate_sum * sigmoid_gate * up_sum).astype(jnp.bfloat16)


def swish_grads(hidden_cot, gate_sum, up_sum):
    sigmoid_gate = jax.nn.sigmoid(gate_sum)
    gate_cot = hidden_cot * up_sum * sigmoid_gate * (1.0 + gate_sum * (1.0 - sigmoid_gate))
    up_cot = hidden_cot * gate_sum * sigmoid_gate
    return (gate_cot.astype(jnp.bfloat16), up_cot.astype(jnp.bfloat16))


def product(left, right):
    return jnp.dot(left, right, preferred_element_type=jnp.float32)


def contract_last(left, right):
    return jnp.einsum("ik,jk->ij", left, right, preferred_element_type=jnp.float32)


def contract_first(left, right):
    return jnp.einsum("ki,kj->ij", left, right, preferred_element_type=jnp.float32)


def shards(tokens, cotangent, gate_weight, up_weight, down_weight):
    gathered = lax.all_gather(tokens, ("row", "depth"), axis=0, tiled=True)
    total_rows = gathered.shape[0]
    grad_scale = 1.0 / math.sqrt(total_rows)
    gate_sum, up_sum = lax.psum(
        (product(gathered, gate_weight), product(gathered, up_weight)), "col"
    )
    hidden = swish_pair(gate_sum, up_sum)
    layer_out = lax.psum_scatter(
        product(hidden, down_weight), ("row", "depth"), scatter_dimension=0, tiled=True
    ).astype(jnp.bfloat16)
    cot_rows = lax.all_gather(cotangent, ("row", "depth"), axis=0, tiled=True)
    hidden_cot = lax.psum(contract_last(cot_rows, down_weight), "col")
    down_grad = (contract_first(hidden, cot_rows) * grad_scale).astype(jnp.bfloat16)
    gate_cot, up_cot = swish_grads(hidden_cot, gate_sum, up_sum)
    gate_grad = (contract_first(gathered, gate_cot) * grad_scale).astype(jnp.bfloat16)
    up_grad = (contract_first(gathered, up_cot) * grad_scale).astype(jnp.bfloat16)
    tokens_grad = lax.psum_scatter(
        contract_last(gate_cot, gate_weight) + contract_last(up_cot, up_weight),
        ("row", "depth"),
        scatter_dimension=0,
        tiled=True,
    ).astype(jnp.bfloat16)
    return (layer_out, tokens_grad, gate_grad, up_grad, down_grad)


def solution(mesh):
    in_specs = (
        P(("row", "depth"), "col"),
        P(("row", "depth"), "col"),
        P("col", ("row", "depth")),
        P("col", ("row", "depth")),
        P(("row", "depth"), "col"),
    )
    out_specs = (
        P(("row", "depth"), "col"),
        P(("row", "depth"), "col"),
        P("col", ("row", "depth")),
        P("col", ("row", "depth")),
        P(("row", "depth"), "col"),
    )
    return jax.shard_map(shards, mesh=mesh, in_specs=in_specs, out_specs=out_specs, check_vma=False)
```

profile of v0, /device:TPU:1, one launch (start us, length us, event | category | flops | bytes accessed | tf_op | source)
XLA Modules:
  0.0 424.7 jit_solution(10049198963592003500)
XLA Ops:
  7.2 0.0 copy-start
  7.2 0.0 copy-start.4
  7.2 0.0 copy-start.1
  7.2 0.0 all-reduce.3.cloned.1.call-start
  7.2 29.3 %all_gather.6 = bf16[512,512]{1,0:T(8,128)(2,1)S(1)} all-gather(bf16[16,512]{1,0:T(8,128)(2,1)} %param.5), channel_id=1, replica_groups=mesh['row'=4,'col'=16,'depth'=8] {'row','depth'}, dimensions={0}, use_global_device_ids=true | all-gather | bytes 540672 | tf_op jit(solution)/shard_map/all_gather | solution.py:34
  36.6 0.0 copy-done.4
  36.6 24.2 %all_gather.7 = bf16[512,512]{1,0:T(8,128)(2,1)S(1)} all-gather(bf16[16,512]{1,0:T(8,128)(2,1)S(1)} %copy-done.4), channel_id=1, replica_groups=mesh['row'=4,'col'=16,'depth'=8] {'row','depth'}, dimensions={0}, use_global_device_ids=true | all-gather | bytes 540672 | tf_op jit(solution)/shard_map/all_gather | solution.py:44
  60.8 0.0 copy-done.1
  60.8 1.4 fusion.6
  62.2 0.0 copy-done
  62.2 0.0 copy-start.2
  62.2 1.4 fusion.5
  63.5 0.0 copy-done.2
  63.5 1.4 fusion.8
  64.9 0.0 all-reduce.3.cloned.1.call-update
  65.0 0.0 reduce-scatter.5.cloned.1.call-start
  65.0 138.3 %all-reduce.3.cloned.1.call-done = (f32[512,448]{0,1:T(8,128)}, f32[512,448]{0,1:T(8,128)}, f32[512,448]{0,1:T(8,128)}) async-done(((f32[512,448]{0,1:T(8,128)}, f32[512,448]{0,1:T(8,128)}, f32[512,448]{0,1:T(8,128)}), (f32[512,448]{0,1:T(8,128)}, f32[512,448]{0,1:T(8,128)}, f32[512,448]{0,1:T(8,128)})) %all-reduce.3.cloned.1.call-update) | async-done | bytes 2752528 | tf_op jit(solution)/shard_map/psum | solution.py:37
  203.4 3.1 multiply_convert_fusion
  206.4 0.5 fusion.9
  206.9 1.5 convolution_add_fusion
  208.4 0.0 copy-start.3
  208.4 0.0 reduce-scatter.5.cloned.1.call-update
  208.4 0.0 reduce-scatter.3.cloned.1.call-start
  208.5 0.9 copy-done.3
  209.4 1.4 fusion.7
  210.8 0.0 reduce-scatter.3.cloned.1.call-update
  210.9 1.2 fusion.2
  212.0 1.2 fusion.3
  213.2 1.2 fusion.4
  214.4 98.0 %reduce-scatter.5.cloned.1.call-done = f32[16,512]{1,0:T(8,128)} async-done(((f32[512,512]{1,0:T(8,128)}), f32[16,512]{1,0:T(8,128)}) %reduce-scatter.5.cloned.1.call-update) | async-done | bytes 32784 | tf_op jit(solution)/shard_map/reduce_scatter | solution.py:50
  312.4 1.4 convert_element_type.34
  313.8 103.1 %reduce-scatter.3.cloned.1.call-done = f32[16,512]{1,0:T(8,128)} async-done(((f32[512,512]{1,0:T(8,128)}), f32[16,512]{1,0:T(8,128)}) %reduce-scatter.3.cloned.1.call-update) | async-done | bytes 32784 | tf_op jit(solution)/shard_map/reduce_scatter | solution.py:41
  416.8 1.4 convert_element_type.31
Async XLA Ops:
  7.2 55.0 %copy-start = (bf16[512,448]{0,1:T(8,128)(2,1)S(1)}, bf16[512,448]{0,1:T(8,128)(2,1)}, u32[]{:S(2)}) copy-start(bf16[512,448]{0,1:T(8,128)(2,1)} %param.7) | copy-start | bytes 1376260
  7.2 29.4 %copy-start.4 = (bf16[16,512]{1,0:T(8,128)(2,1)S(1)}, bf16[16,512]{1,0:T(8,128)(2,1)}, u32[]{:S(2)}) copy-start(bf16[16,512]{1,0:T(8,128)(2,1)} %param.6) | copy-start | bytes 49156
  7.2 53.6 %copy-start.1 = (bf16[512,448]{0,1:T(8,128)(2,1)S(1)}, bf16[512,448]{0,1:T(8,128)(2,1)}, u32[]{:S(2)}) copy-start(bf16[512,448]{0,1:T(8,128)(2,1)} %param.8) | copy-start | bytes 1376260
  7.2 196.2 %all-reduce.3.cloned.1.call-start = ((), (), s32[]{:S(2)}) async-start(), calls=%async_computation.4 | async-start | bytes 5505024 | tf_op jit(solution)/shard_map/psum | solution.py:37
  62.2 1.4 copy-start.2
  65.0 247.4 %reduce-scatter.5.cloned.1.call-start = ((), (), s32[]{:S(2)}) async-start(), calls=%async_computation.3 | async-start | bytes 1081344 | tf_op jit(solution)/shard_map/reduce_scatter | solution.py:50
  208.4 1.0 copy-start.3
  208.4 208.4 %reduce-scatter.3.cloned.1.call-start = ((), (), s32[]{:S(2)}) async-start(), calls=%async_computation.2 | async-start | bytes 1081344 | tf_op jit(solution)/shard_map/reduce_scatter | solution.py:41
Sparse Core Ops, SparseCore 0:
  65.1 138.2 all-reduce.2
  208.5 103.8 reduce-scatter.4
  316.8 100.0 reduce-scatter.2
where the time goes:
time: 426 us; the launch traced here: 425 us
  waiting for transfers between devices  339 us (80%)
  blocking collectives  53.5 us (13%)
  between operations  13.8 us (3%)
  matrix products  11.1 us (3%)
  other arithmetic  5.79 us (1%)
    psum x1, waiting for transfers between devices, shards(): lax.psum((product(gathered, gate_weight), product(gathered, up_weight)),...  138 us
    reduce_scatter x1, waiting for transfers between devices, shards(): lax.psum_scatter(product(hidden, down_weight), ('row', 'depth'), scatter_...  103 us
    reduce_scatter x1, waiting for transfers between devices, shards(): lax.psum_scatter(contract_last(gate_cot, gate_weight) + contract_last(up_...  98 us
    all_gather x1, blocking collectives, shards(): gathered = lax.all_gather(tokens, ('row', 'depth'), axis=0, tiled=True)  29.3 us
    all_gather x1, blocking collectives, shards(): cot_rows = lax.all_gather(cotangent, ('row', 'depth'), axis=0, tiled=True)  24.2 us
  transfers between devices with their start and end apart: 3, of which 3 were waited for; matrix products, arithmetic and copies ran while one was open for 1% of the time, Pallas kernels for 0%

commit v1 on v0

v1 whole, which is shorter than its diff:
```python
import math

import jax
import jax.numpy as jnp
from jax import lax
from jax.experimental import pallas as pl
from jax.experimental.pallas import tpu as pltpu
from jax.sharding import PartitionSpec as P

BF = jnp.bfloat16
F32 = jnp.float32
GROUP = ("row", "depth")
NEAR = (0, -1, 1, 2)


def nt(left, right):
    return lax.dot_general(left, right, (((1,), (1,)), ((), ())), preferred_element_type=F32)


def nn(left, right):
    return lax.dot_general(left, right, (((1,), (0,)), ((), ())), preferred_element_type=F32)


def tn(left, right):
    return lax.dot_general(left, right, (((0,), (0,)), ((), ())), preferred_element_type=F32)


def call(body, out_shapes, n_scalar, n_array, scratch=()):
    return pl.pallas_call(
        body,
        out_shape=[jax.ShapeDtypeStruct(s, d) for s, d in out_shapes],
        in_specs=[pl.BlockSpec(memory_space=pltpu.SMEM)] * n_scalar
        + [pl.BlockSpec(memory_space=pltpu.VMEM)] * n_array,
        out_specs=[pl.BlockSpec(memory_space=pltpu.VMEM)] * len(out_shapes),
        scratch_shapes=list(scratch),
        compiler_params=pltpu.CompilerParams(vmem_limit_bytes=40 * 1024 * 1024),
    )


def partial_sums(index, gathered, gate_t, up_t, down, own, first, second, third, ordered, pair):
    ff = gate_t.shape[0]
    width = gate_t.shape[1]
    pair[0:ff, :] = gate_t[...]
    pair[ff : 2 * ff, :] = up_t[...]
    chunk = ordered.shape[0] // 16
    per = chunk // gathered.shape[1]
    for at in range(16):
        rows = gathered[pl.ds(index[at] * per, per)]
        ordered[at * chunk : (at + 1) * chunk, :] = rows.reshape(chunk, 2 * width)
    block = 4 * chunk
    for at, out in enumerate((own, first, second, third)):
        rows = ordered[at * block : (at + 1) * block, :]
        out[:, 0 : 2 * ff] = nt(rows[:, :width], pair[...]).astype(out.dtype)
        out[:, 2 * ff :] = nt(rows[:, width:], down[...]).astype(out.dtype)


def near_sum(place, own, first, second, third, keep, near, far, back):
    chunk = keep.shape[0]

    def total(at):
        rows = pl.ds(pl.multiple_of(place[at] * chunk, chunk), chunk)
        return own[rows, :] + (
            first[rows, :].astype(F32) + second[rows, :].astype(F32) + third[rows, :].astype(F32)
        )

    keep[...] = total(0)
    near[...] = total(1).astype(BF)
    far[...] = total(2).astype(BF)
    back[...] = total(3).astype(BF)


def swish(keep, near, far, back, out):
    ff = out.shape[1] // 3
    total = keep[...] + (near[...].astype(F32) + far[...].astype(F32) + back[...].astype(F32))
    gate_sum = total[:, :ff]
    up_sum = total[:, ff : 2 * ff]
    hidden_cot = total[:, 2 * ff :]
    sig = jax.nn.sigmoid(gate_sum)
    gate_cot = hidden_cot * up_sum * sig * (1.0 + gate_sum * (1.0 - sig))
    up_cot = hidden_cot * gate_sum * sig
    out[:, :ff] = gate_cot.astype(BF)
    out[:, ff : 2 * ff] = up_cot.astype(BF)
    out[:, 2 * ff :] = (gate_sum * sig * up_sum).astype(BF)


def outward(index, c0, c1, c2, c3, gate_t, up_t, down, out, pair):
    ff = gate_t.shape[0]
    width = gate_t.shape[1]
    pair[0:ff, :] = gate_t[...]
    pair[ff : 2 * ff, :] = up_t[...]
    chunk = out.shape[1]
    for at, c in enumerate((c0, c1, c2, c3)):
        layer = nn(c[:, 2 * ff :], down[...]).astype(BF)
        back = nn(c[:, : 2 * ff], pair[...]).astype(BF)
        for j in range(4):
            slot = index[at * 4 + j]
            out[slot, :, :width] = layer[j * chunk : (j + 1) * chunk, :]
            out[slot, :, width:] = back[j * chunk : (j + 1) * chunk, :]


def weight_grads(c0, c1, c2, c3, ordered, gate_g, up_g, down_g, allc):
    ff, width = gate_g.shape
    block = c0.shape[0]
    scale = 1.0 / math.sqrt(ordered.shape[0])
    for at, c in enumerate((c0, c1, c2, c3)):
        allc[at * block : (at + 1) * block, :] = c[...]
    both = tn(allc[:, : 2 * ff], ordered[:, :width]) * scale
    gate_g[...] = both[:ff, :].astype(BF)
    up_g[...] = both[ff:, :].astype(BF)
    down_g[...] = (tn(allc[:, 2 * ff :], ordered[:, width:]) * scale).astype(BF)


def shards(mesh, tokens, cotangent, gate_weight, up_weight, down_weight):
    cols, depth = mesh.shape["col"], mesh.shape["depth"]
    ranks = mesh.shape["row"] * depth
    ff, width = down_weight.shape
    rows = tokens.shape[0]
    total = rows * ranks
    chunk = total // cols
    block = 4 * chunk

    def shift(x, step):
        pairs = []
        for z in range(cols):
            for d in range(depth):
                to = (z + (step if d % 2 == 0 else -step)) % cols
                pairs.append((z * depth + d, to * depth + d))
        return lax.ppermute(x, ("col", "depth"), pairs)

    z = lax.axis_index("col")
    sign = 1 - 2 * (lax.axis_index("depth") % 2)
    four = jnp.arange(4, dtype=jnp.int32)
    classes = (z - sign * jnp.array(NEAR, jnp.int32) + 16) % 4
    index = (classes[:, None] + 4 * four[None, :]).reshape(16).astype(jnp.int32)
    place = ((z // 4 + sign * four + 4) % 4).astype(jnp.int32)

    mine = jnp.concatenate([tokens, cotangent], axis=1)
    gathered = lax.all_to_all(
        jnp.broadcast_to(mine[None], (ranks, rows, 2 * width)), GROUP, 0, 0, tiled=True
    )
    gate_t, up_t = gate_weight.T, up_weight.T
    wide = 3 * ff
    own, first, second, third, ordered = call(
        partial_sums,
        [((block, wide), F32)] + [((block, wide), BF)] * 3 + [((total, 2 * width), BF)],
        1,
        4,
        [pltpu.VMEM((2 * ff, width), BF)],
    )(index, gathered, gate_t, up_t, down_weight)
    third = shift(third, -NEAR[3])
    first = shift(first, -NEAR[1])
    second = shift(second, -NEAR[2])
    keep, near, far, back = call(
        near_sum, [((chunk, wide), F32)] + [((chunk, wide), BF)] * 3, 1, 4
    )(place, own, first, second, third)
    far = shift(far, 8)
    near = shift(near, 4)
    back = shift(back, -4)
    (act,) = call(swish, [((chunk, wide), BF)], 0, 4)(keep, near, far, back)
    strided = [[i + 4 * j for j in range(4)] for i in range(4)]
    c0 = lax.all_gather(act, "col", axis=0, tiled=True, axis_index_groups=strided)
    c3 = shift(c0, NEAR[3])
    c1 = shift(c0, NEAR[1])
    c2 = shift(c0, NEAR[2])
    (out,) = call(
        outward,
        [((16, chunk, 2 * width), BF)],
        1,
        7,
        [pltpu.VMEM((2 * ff, width), BF)],
    )(index, c0, c1, c2, c3, gate_t, up_t, down_weight)
    parts = lax.all_to_all(out.reshape(ranks, rows, 2 * width), GROUP, 0, 0, tiled=True)
    summed = jnp.sum(parts.astype(F32), axis=0).astype(BF)
    gate_g, up_g, down_g = call(
        weight_grads, [((ff, width), BF)] * 3, 0, 5, [pltpu.VMEM((total, wide), BF)]
    )(c0, c1, c2, c3, ordered)
    return (summed[:, :width], summed[:, width:], gate_g.T, up_g.T, down_g)


def solution(mesh):
    tok = P(GROUP, "col")
    wide = P("col", GROUP)

    def run(*args):
        return shards(mesh, *args)

    return jax.shard_map(
        run,
        mesh=mesh,
        in_specs=(tok, tok, wide, wide, tok),
        out_specs=(tok, tok, wide, wide, tok),
        check_vma=False,
    )
```

time: 426 us -> 157 us (0.37)
  waiting for transfers between devices: 339 us -> 64.6 us
  starting transfers between devices: 0.12 us -> 58 us
  blocking collectives: 53.5 us -> 19.2 us
  between operations: 13.8 us -> 0.8 us
  matrix products: 11.1 us -> 0 us
  Pallas kernels: 0 us -> 8.04 us
    reduce_scatter x2 -> x0, waiting for transfers between devices: 201 us -> none  [the longest x1 103 us: shards(): lax.psum_scatter(product(hidden, down_weight), ('row', 'depth'), scatter_...]
    psum x1 -> x0, waiting for transfers between devices: 138 us -> none  [shards(): lax.psum((product(gathered, gate_weight), product(gathered, up_weight)),...]
    ppermute x0 -> x9, starting transfers between devices: none -> 41.5 us  [shift(): return lax.ppermute(x, ('col', 'depth'), pairs)]
    all_gather x2 -> x1, blocking collectives: 53.5 us -> 19.2 us  [shards(): lax.all_gather(act, 'col', axis=0, tiled=True, axis_index_groups=strided)]
    ppermute x0 -> x9, waiting for transfers between devices: none -> 33.2 us  [shift(): return lax.ppermute(x, ('col', 'depth'), pairs)]
    all_to_all x0 -> x2, waiting for transfers between devices: none -> 31.4 us  [the longest x1 16.2 us: shards(): lax.all_to_all(jnp.broadcast_to(mine[None], (ranks, rows, 2 * width)), GR...]
    all_to_all x0 -> x2, starting transfers between devices: none -> 16.5 us  [the longest x1 10.6 us: shards(): lax.all_to_all(jnp.broadcast_to(mine[None], (ranks, rows, 2 * width)), GR...]
    dot_general x9 -> x0, matrix products: 11.1 us -> none  [the longest x3 4.19 us: product(): return jnp.dot(left, right, preferred_element_type=jnp.float32)]
  transfers between devices with their start and end apart: 3 -> 11, of which waited for: 3 -> 9; matrix products, arithmetic and copies ran while one was open for 1% -> 0% of each run, Pallas kernels for 0% -> 1%
where the time goes in v1:
time: 157 us; the launch traced here: 156 us
  waiting for transfers between devices  64.6 us (41%)
  starting transfers between devices  58 us (37%)
  blocking collectives  19.2 us (12%)
  Pallas kernels  8.04 us (5%)
  local copies, waits for them, and re-layouts  3.46 us (2%)
  other arithmetic  2.23 us (1%)
    ppermute x9, starting transfers between devices, shift(): return lax.ppermute(x, ('col', 'depth'), pairs)  41.5 us
    ppermute x9, waiting for transfers between devices, shift(): return lax.ppermute(x, ('col', 'depth'), pairs)  33.2 us
    all_gather x1, blocking collectives, shards(): lax.all_gather(act, 'col', axis=0, tiled=True, axis_index_groups=strided)  19.2 us
    all_to_all x1, waiting for transfers between devices, shards(): lax.all_to_all(jnp.broadcast_to(mine[None], (ranks, rows, 2 * width)), GR...  16.2 us
    all_to_all x1, waiting for transfers between devices, shards(): lax.all_to_all(out.reshape(ranks, rows, 2 * width), GROUP, 0, 0, tiled=True)  15.3 us
    all_to_all x1, starting transfers between devices, shards(): lax.all_to_all(jnp.broadcast_to(mine[None], (ranks, rows, 2 * width)), GR...  10.6 us
    all_to_all x1, starting transfers between devices, shards(): lax.all_to_all(out.reshape(ranks, rows, 2 * width), GROUP, 0, 0, tiled=True)  5.94 us
  transfers between devices with their start and end apart: 11, of which 9 were waited for; matrix products, arithmetic and copies ran while one was open for 0% of the time, Pallas kernels for 1%

profile of v1, /device:TPU:1, one launch (start us, length us, event | category | flops | bytes accessed | tf_op | source)
XLA Modules:
  0.0 156.3 jit_solution(4812268908947802053)
XLA Ops:
  0.6 0.7 pad_maximum_fusion
  1.4 1.1 broadcast_in_dim.2
  2.5 0.0 copy-start
  2.5 0.0 copy-start.1
  2.5 0.0 copy-start.2
  2.5 10.6 %all-to-all-start = ((bf16[32,16,1024]{2,1,0:T(8,128)(2,1)}), bf16[32,16,1024]{2,1,0:T(8,128)(2,1)S(1)}, u32[]{:S(2)}, u32[]{:S(2)}) async-start(bf16[32,16,1024]{2,1,0:T(8,128)(2,1)} %broadcast_in_dim.2), calls=%async_computation | async-start | bytes 2097152 | tf_op jit(solution)/shard_map/all_to_all | solution.py:138
  13.1 0.0 copy-start.5
  13.1 0.6 copy-done.5
  13.8 0.1 broadcast_add_fusion
  13.9 0.1 add.50.index
  13.9 16.2 %all-to-all-done.gathered = bf16[32,16,1024]{2,1,0:T(8,128)(2,1)S(1)} async-done(((bf16[32,16,1024]{2,1,0:T(8,128)(2,1)}), bf16[32,16,1024]{2,1,0:T(8,128)(2,1)S(1)}, u32[]{:S(2)}, u32[]{:S(2)}) %all-to-all-start) | async-done | bytes 1048608 | tf_op jit(solution)/shard_map/all_to_all | solution.py:138
  30.1 0.0 copy-done
  30.1 0.0 copy-done.1
  30.1 0.0 copy-done.2
  30.1 3.0 %shard_map.101 = (f32[128,1344]{1,0:T(8,128)S(1)}, bf16[128,1344]{1,0:T(8,128)(2,1)}, bf16[128,1344]{1,0:T(8,128)(2,1)}, bf16[128,1344]{1,0:T(8,128)(2,1)}, bf16[512,1024]{1,0:T(8,128)(2,1)S(1)}) custom-call(s32[16]{0:T(128)S(1)} %add.50.index, bf16[32,16,1024]{2,1,0:T(8,128)(2,1)S(1)} %all-to-all-done.gathered, bf16[448,512]{1,0:T(8,128)(2,1)S(1)} %bitcast.5, ...), custom_call_target="tpu_custom_call" | custom-call | tf_op jit(solution)/shard_map/pallas_call | solution.py:143
  33.1 0.0 copy-start.3
  33.1 1.0 copy-done.3
  34.1 9.2 %collective-permute-start = (bf16[128,1344]{1,0:T(8,128)(2,1)}, bf16[128,1344]{1,0:T(8,128)(2,1)S(1)}, u32[]{:S(2)}, u32[]{:S(2)}) collective-permute-start(bf16[128,1344]{1,0:T(8,128)(2,1)} %get-tuple-element.18), channel_id=1, source_target_pairs={{0,8},{1,121},{2,10},{3,123},{4,12},{5,125},{6,14},{7,127},{8,16},... | collective-permute-start | bytes 1032200 | tf_op jit(solution)/shard_map/ppermute | solution.py:128
  43.2 1.9 %collective-permute-start.1 = (bf16[128,1344]{1,0:T(8,128)(2,1)}, bf16[128,1344]{1,0:T(8,128)(2,1)S(1)}, u32[]{:S(2)}, u32[]{:S(2)}) collective-permute-start(bf16[128,1344]{1,0:T(8,128)(2,1)} %get-tuple-element.19), channel_id=1, source_target_pairs={{0,120},{1,9},{2,122},{3,11},{4,124},{5,13},{6,126},{7,15},{8,0},{... | collective-permute-start | bytes 1032200 | tf_op jit(solution)/shard_map/ppermute | solution.py:128
  45.2 1.9 %collective-permute-start.2 = (bf16[128,1344]{1,0:T(8,128)(2,1)}, bf16[128,1344]{1,0:T(8,128)(2,1)S(1)}, u32[]{:S(2)}, u32[]{:S(2)}) collective-permute-start(bf16[128,1344]{1,0:T(8,128)(2,1)} %get-tuple-element.20), channel_id=1, source_target_pairs={{0,112},{1,17},{2,114},{3,19},{4,116},{5,21},{6,118},{7,23},{8,120... | collective-permute-start | bytes 1032200 | tf_op jit(solution)/shard_map/ppermute | solution.py:128
  47.1 2.1 %collective-permute-done.first = bf16[128,1344]{1,0:T(8,128)(2,1)S(1)} collective-permute-done((bf16[128,1344]{1,0:T(8,128)(2,1)}, bf16[128,1344]{1,0:T(8,128)(2,1)S(1)}, u32[]{:S(2)}, u32[]{:S(2)}) %collective-permute-start) | collective-permute-done | bytes 344096 | tf_op jit(solution)/shard_map/ppermute | solution.py:128
  49.2 3.8 %collective-permute-done.1.second = bf16[128,1344]{1,0:T(8,128)(2,1)S(1)} collective-permute-done((bf16[128,1344]{1,0:T(8,128)(2,1)}, bf16[128,1344]{1,0:T(8,128)(2,1)S(1)}, u32[]{:S(2)}, u32[]{:S(2)}) %collective-permute-start.1) | collective-permute-done | bytes 344096 | tf_op jit(solution)/shard_map/ppermute | solution.py:128
  53.0 6.3 %collective-permute-done.2.third = bf16[128,1344]{1,0:T(8,128)(2,1)S(1)} collective-permute-done((bf16[128,1344]{1,0:T(8,128)(2,1)}, bf16[128,1344]{1,0:T(8,128)(2,1)S(1)}, u32[]{:S(2)}, u32[]{:S(2)}) %collective-permute-start.2) | collective-permute-done | bytes 344096 | tf_op jit(solution)/shard_map/ppermute | solution.py:128
  59.2 0.7 shard_map.102
  59.9 4.5 %collective-permute-start.3 = (bf16[32,1344]{1,0:T(8,128)(2,1)S(1)}, bf16[32,1344]{1,0:T(8,128)(2,1)S(1)}, u32[]{:S(2)}, u32[]{:S(2)}) collective-permute-start(bf16[32,1344]{1,0:T(8,128)(2,1)S(1)} %get-tuple-element.22), channel_id=1, source_target_pairs={{0,32},{1,97},{2,34},{3,99},{4,36},{5,101},{6,38},{7,103},{8,40},{... | collective-permute-start | bytes 258056 | tf_op jit(solution)/shard_map/ppermute | solution.py:128
  64.5 6.0 %collective-permute-start.4 = (bf16[32,1344]{1,0:T(8,128)(2,1)S(1)}, bf16[32,1344]{1,0:T(8,128)(2,1)S(1)}, u32[]{:S(2)}, u32[]{:S(2)}) collective-permute-start(bf16[32,1344]{1,0:T(8,128)(2,1)S(1)} %get-tuple-element.23), channel_id=1, source_target_pairs={{0,64},{1,65},{2,66},{3,67},{4,68},{5,69},{6,70},{7,71},{8,72},{9,... | collective-permute-start | bytes 258056 | tf_op jit(solution)/shard_map/ppermute | solution.py:128
  70.5 7.3 %collective-permute-start.5 = (bf16[32,1344]{1,0:T(8,128)(2,1)S(1)}, bf16[32,1344]{1,0:T(8,128)(2,1)S(1)}, u32[]{:S(2)}, u32[]{:S(2)}) collective-permute-start(bf16[32,1344]{1,0:T(8,128)(2,1)S(1)} %get-tuple-element.24), channel_id=1, source_target_pairs={{0,96},{1,33},{2,98},{3,35},{4,100},{5,37},{6,102},{7,39},{8,104},... | collective-permute-start | bytes 258056 | tf_op jit(solution)/shard_map/ppermute | solution.py:128
  77.7 0.0 collective-permute-done.3.near
  77.8 5.1 %collective-permute-done.4.far = bf16[32,1344]{1,0:T(8,128)(2,1)S(1)} collective-permute-done((bf16[32,1344]{1,0:T(8,128)(2,1)S(1)}, bf16[32,1344]{1,0:T(8,128)(2,1)S(1)}, u32[]{:S(2)}, u32[]{:S(2)}) %collective-permute-start.4) | collective-permute-done | bytes 86048 | tf_op jit(solution)/shard_map/ppermute | solution.py:128
  82.9 2.7 %collective-permute-done.5.back = bf16[32,1344]{1,0:T(8,128)(2,1)S(1)} collective-permute-done((bf16[32,1344]{1,0:T(8,128)(2,1)S(1)}, bf16[32,1344]{1,0:T(8,128)(2,1)S(1)}, u32[]{:S(2)}, u32[]{:S(2)}) %collective-permute-start.5) | collective-permute-done | bytes 86048 | tf_op jit(solution)/shard_map/ppermute | solution.py:128
  85.6 0.1 shard_map.103
  85.7 19.2 %all_gather.3.c0 = bf16[128,1344]{1,0:T(8,128)(2,1)S(1)} all-gather(bf16[32,1344]{1,0:T(8,128)(2,1)S(1)} %shard_map.103), channel_id=1, replica_groups={{0,32,64,96},{8,40,72,104},{16,48,80,112},{24,56,88,120},{1,33,65,97},{..., dimensions={0}, use_global_device_ids=true | all-gather | bytes 430080 | tf_op jit(solution)/shard_map/all_gather | solution.py:161
  104.9 2.8 %collective-permute-start.8 = (bf16[128,1344]{1,0:T(8,128)(2,1)S(1)}, bf16[128,1344]{1,0:T(8,128)(2,1)S(1)}, u32[]{:S(2)}, u32[]{:S(2)}) collective-permute-start(bf16[128,1344]{1,0:T(8,128)(2,1)S(1)} %all_gather.3.c0), channel_id=1, source_target_pairs={{0,16},{1,113},{2,18},{3,115},{4,20},{5,117},{6,22},{7,119},{8,24}... | collective-permute-start | bytes 1032200 | tf_op jit(solution)/shard_map/ppermute | solution.py:128
  107.7 4.8 %collective-permute-start.7 = (bf16[128,1344]{1,0:T(8,128)(2,1)S(1)}, bf16[128,1344]{1,0:T(8,128)(2,1)S(1)}, u32[]{:S(2)}, u32[]{:S(2)}) collective-permute-start(bf16[128,1344]{1,0:T(8,128)(2,1)S(1)} %all_gather.3.c0), channel_id=1, source_target_pairs={{0,8},{1,121},{2,10},{3,123},{4,12},{5,125},{6,14},{7,127},{8,16},... | collective-permute-start | bytes 1032200 | tf_op jit(solution)/shard_map/ppermute | solution.py:128
  112.5 3.1 %collective-permute-start.6 = (bf16[128,1344]{1,0:T(8,128)(2,1)S(1)}, bf16[128,1344]{1,0:T(8,128)(2,1)S(1)}, u32[]{:S(2)}, u32[]{:S(2)}) collective-permute-start(bf16[128,1344]{1,0:T(8,128)(2,1)S(1)} %all_gather.3.c0), channel_id=1, source_target_pairs={{0,120},{1,9},{2,122},{3,11},{4,124},{5,13},{6,126},{7,15},{8,0},{... | collective-permute-start | bytes 1032200 | tf_op jit(solution)/shard_map/ppermute | solution.py:128
  115.6 0.0 collective-permute-done.8.c3
  115.6 7.9 %collective-permute-done.7.c2 = bf16[128,1344]{1,0:T(8,128)(2,1)S(1)} collective-permute-done((bf16[128,1344]{1,0:T(8,128)(2,1)S(1)}, bf16[128,1344]{1,0:T(8,128)(2,1)S(1)}, u32[]{:S(2)}, u32[]{:S(2)}) %collective-permute-start.7) | collective-permute-done | bytes 344096 | tf_op jit(solution)/shard_map/ppermute | solution.py:128
  123.6 5.3 %collective-permute-done.6.c1 = bf16[128,1344]{1,0:T(8,128)(2,1)S(1)} collective-permute-done((bf16[128,1344]{1,0:T(8,128)(2,1)S(1)}, bf16[128,1344]{1,0:T(8,128)(2,1)S(1)}, u32[]{:S(2)}, u32[]{:S(2)}) %collective-permute-start.6) | collective-permute-done | bytes 344096 | tf_op jit(solution)/shard_map/ppermute | solution.py:128
  128.9 2.5 %shard_map.104 = bf16[16,32,1024]{2,1,0:T(8,128)(2,1)} custom-call(s32[16]{0:T(128)S(1)} %add.50.index, bf16[128,1344]{1,0:T(8,128)(2,1)S(1)} %all_gather.3.c0, bf16[128,1344]{1,0:T(8,128)(2,1)S(1)} %collective-permute-done.6.c1, bf16[128,1344]{1,0:T(8,128)(2,1)S(1)} %collective-permute-done.7.c2, bf16[128,1344]{1,0:T(8,128)(2,1)S(1)} %collective-permute-done.8.c3, ...), custom_call_target="tpu_custom_call" | custom-call | tf_op jit(solution)/shard_map/pallas_call | solution.py:165
  131.4 0.0 copy-start.4
  131.4 5.9 %all-to-all-start.1 = ((bf16[32,16,1024]{2,1,0:T(8,128)(2,1)}), bf16[32,16,1024]{2,1,0:T(8,128)(2,1)}, u32[]{:S(2)}, u32[]{:S(2)}) async-start(bf16[32,16,1024]{2,1,0:T(8,128)(2,1)} %bitcast.2), calls=%async_computation.1 | async-start | bytes 2097152 | tf_op jit(solution)/shard_map/all_to_all | solution.py:172
  137.3 0.0 copy-done.4
  137.3 1.7 %shard_map.105 = (bf16[448,512]{1,0:T(8,128)(2,1)}, bf16[448,512]{1,0:T(8,128)(2,1)}, bf16[448,512]{1,0:T(8,128)(2,1)}) custom-call(bf16[128,1344]{1,0:T(8,128)(2,1)S(1)} %all_gather.3.c0, bf16[128,1344]{1,0:T(8,128)(2,1)S(1)} %collective-permute-done.6.c1, bf16[128,1344]{1,0:T(8,128)(2,1)S(1)} %collective-permute-done.7.c2, ...), custom_call_target="tpu_custom_call" | custom-call | tf_op jit(solution)/shard_map/pallas_call | solution.py:174
  139.0 15.3 %all-to-all-done.1 = bf16[32,16,1024]{2,1,0:T(8,128)(2,1)} async-done(((bf16[32,16,1024]{2,1,0:T(8,128)(2,1)}), bf16[32,16,1024]{2,1,0:T(8,128)(2,1)}, u32[]{:S(2)}, u32[]{:S(2)}) %all-to-all-start.1) | async-done | bytes 1048608 | tf_op jit(solution)/shard_map/all_to_all | solution.py:172
  154.3 1.4 reduce_sum.12
  155.7 0.6 fusion.2
  (2 shorter events, 0.0 us)
Async XLA Ops:
  2.5 27.6 %copy-start = (bf16[512,448]{0,1:T(8,128)(2,1)S(1)}, bf16[512,448]{0,1:T(8,128)(2,1)}, u32[]{:S(2)}) copy-start(bf16[512,448]{0,1:T(8,128)(2,1)} %param.8) | copy-start | bytes 1376260
  2.5 27.6 %copy-start.1 = (bf16[512,448]{0,1:T(8,128)(2,1)S(1)}, bf16[512,448]{0,1:T(8,128)(2,1)}, u32[]{:S(2)}) copy-start(bf16[512,448]{0,1:T(8,128)(2,1)} %param.9) | copy-start | bytes 1376260
  2.5 27.6 %copy-start.2 = (bf16[448,512]{1,0:T(8,128)(2,1)S(1)}, bf16[448,512]{1,0:T(8,128)(2,1)}, u32[]{:S(2)}) copy-start(bf16[448,512]{1,0:T(8,128)(2,1)} %down.3) | copy-start | bytes 1376260
  2.5 27.6 %all-to-all-start = ((bf16[32,16,1024]{2,1,0:T(8,128)(2,1)}), bf16[32,16,1024]{2,1,0:T(8,128)(2,1)S(1)}, u32[]{:S(2)}, u32[]{:S(2)}) async-start(bf16[32,16,1024]{2,1,0:T(8,128)(2,1)} %broadcast_in_dim.2), calls=%async_computation | async-start | bytes 2097152 | tf_op jit(solution)/shard_map/all_to_all | solution.py:138
  13.1 0.7 copy-start.5
  33.1 1.0 copy-start.3
  34.1 15.1 %collective-permute-start = (bf16[128,1344]{1,0:T(8,128)(2,1)}, bf16[128,1344]{1,0:T(8,128)(2,1)S(1)}, u32[]{:S(2)}, u32[]{:S(2)}) collective-permute-start(bf16[128,1344]{1,0:T(8,128)(2,1)} %get-tuple-element.18), channel_id=1, source_target_pairs={{0,8},{1,121},{2,10},{3,123},{4,12},{5,125},{6,14},{7,127},{8,16},... | collective-permute-start | bytes 1032200 | tf_op jit(solution)/shard_map/ppermute | solution.py:128
  43.2 9.7 %collective-permute-start.1 = (bf16[128,1344]{1,0:T(8,128)(2,1)}, bf16[128,1344]{1,0:T(8,128)(2,1)S(1)}, u32[]{:S(2)}, u32[]{:S(2)}) collective-permute-start(bf16[128,1344]{1,0:T(8,128)(2,1)} %get-tuple-element.19), channel_id=1, source_target_pairs={{0,120},{1,9},{2,122},{3,11},{4,124},{5,13},{6,126},{7,15},{8,0},{... | collective-permute-start | bytes 1032200 | tf_op jit(solution)/shard_map/ppermute | solution.py:128
  45.2 14.1 %collective-permute-start.2 = (bf16[128,1344]{1,0:T(8,128)(2,1)}, bf16[128,1344]{1,0:T(8,128)(2,1)S(1)}, u32[]{:S(2)}, u32[]{:S(2)}) collective-permute-start(bf16[128,1344]{1,0:T(8,128)(2,1)} %get-tuple-element.20), channel_id=1, source_target_pairs={{0,112},{1,17},{2,114},{3,19},{4,116},{5,21},{6,118},{7,23},{8,120... | collective-permute-start | bytes 1032200 | tf_op jit(solution)/shard_map/ppermute | solution.py:128
  59.9 17.8 %collective-permute-start.3 = (bf16[32,1344]{1,0:T(8,128)(2,1)S(1)}, bf16[32,1344]{1,0:T(8,128)(2,1)S(1)}, u32[]{:S(2)}, u32[]{:S(2)}) collective-permute-start(bf16[32,1344]{1,0:T(8,128)(2,1)S(1)} %get-tuple-element.22), channel_id=1, source_target_pairs={{0,32},{1,97},{2,34},{3,99},{4,36},{5,101},{6,38},{7,103},{8,40},{... | collective-permute-start | bytes 258056 | tf_op jit(solution)/shard_map/ppermute | solution.py:128
  64.5 18.4 %collective-permute-start.4 = (bf16[32,1344]{1,0:T(8,128)(2,1)S(1)}, bf16[32,1344]{1,0:T(8,128)(2,1)S(1)}, u32[]{:S(2)}, u32[]{:S(2)}) collective-permute-start(bf16[32,1344]{1,0:T(8,128)(2,1)S(1)} %get-tuple-element.23), channel_id=1, source_target_pairs={{0,64},{1,65},{2,66},{3,67},{4,68},{5,69},{6,70},{7,71},{8,72},{9,... | collective-permute-start | bytes 258056 | tf_op jit(solution)/shard_map/ppermute | solution.py:128
  70.5 15.1 %collective-permute-start.5 = (bf16[32,1344]{1,0:T(8,128)(2,1)S(1)}, bf16[32,1344]{1,0:T(8,128)(2,1)S(1)}, u32[]{:S(2)}, u32[]{:S(2)}) collective-permute-start(bf16[32,1344]{1,0:T(8,128)(2,1)S(1)} %get-tuple-element.24), channel_id=1, source_target_pairs={{0,96},{1,33},{2,98},{3,35},{4,100},{5,37},{6,102},{7,39},{8,104},... | collective-permute-start | bytes 258056 | tf_op jit(solution)/shard_map/ppermute | solution.py:128
  104.9 10.8 %collective-permute-start.8 = (bf16[128,1344]{1,0:T(8,128)(2,1)S(1)}, bf16[128,1344]{1,0:T(8,128)(2,1)S(1)}, u32[]{:S(2)}, u32[]{:S(2)}) collective-permute-start(bf16[128,1344]{1,0:T(8,128)(2,1)S(1)} %all_gather.3.c0), channel_id=1, source_target_pairs={{0,16},{1,113},{2,18},{3,115},{4,20},{5,117},{6,22},{7,119},{8,24}... | collective-permute-start | bytes 1032200 | tf_op jit(solution)/shard_map/ppermute | solution.py:128
  107.7 15.9 %collective-permute-start.7 = (bf16[128,1344]{1,0:T(8,128)(2,1)S(1)}, bf16[128,1344]{1,0:T(8,128)(2,1)S(1)}, u32[]{:S(2)}, u32[]{:S(2)}) collective-permute-start(bf16[128,1344]{1,0:T(8,128)(2,1)S(1)} %all_gather.3.c0), channel_id=1, source_target_pairs={{0,8},{1,121},{2,10},{3,123},{4,12},{5,125},{6,14},{7,127},{8,16},... | collective-permute-start | bytes 1032200 | tf_op jit(solution)/shard_map/ppermute | solution.py:128
  112.5 16.4 %collective-permute-start.6 = (bf16[128,1344]{1,0:T(8,128)(2,1)S(1)}, bf16[128,1344]{1,0:T(8,128)(2,1)S(1)}, u32[]{:S(2)}, u32[]{:S(2)}) collective-permute-start(bf16[128,1344]{1,0:T(8,128)(2,1)S(1)} %all_gather.3.c0), channel_id=1, source_target_pairs={{0,120},{1,9},{2,122},{3,11},{4,124},{5,13},{6,126},{7,15},{8,0},{... | collective-permute-start | bytes 1032200 | tf_op jit(solution)/shard_map/ppermute | solution.py:128
  131.4 5.9 %copy-start.4 = (bf16[512,1024]{1,0:T(8,128)(2,1)S(1)}, bf16[512,1024]{1,0:T(8,128)(2,1)}, u32[]{:S(2)}) copy-start(bf16[512,1024]{1,0:T(8,128)(2,1)} %copy-done.3) | copy-start | bytes 3145732
  131.4 22.9 %all-to-all-start.1 = ((bf16[32,16,1024]{2,1,0:T(8,128)(2,1)}), bf16[32,16,1024]{2,1,0:T(8,128)(2,1)}, u32[]{:S(2)}, u32[]{:S(2)}) async-start(bf16[32,16,1024]{2,1,0:T(8,128)(2,1)} %bitcast.2), calls=%async_computation.1 | async-start | bytes 2097152 | tf_op jit(solution)/shard_map/all_to_all | solution.py:172

commit v2 on v1

v2 whole, which is shorter than its diff:
```python
import math

import jax
import jax.numpy as jnp
from jax import lax
from jax.experimental import pallas as pl
from jax.experimental.pallas import tpu as pltpu
from jax.sharding import PartitionSpec as P

BF = jnp.bfloat16
F32 = jnp.float32
GROUP = ("row", "depth")
NEAR = (0, -1, 1, 2)


def nt(left, right):
    return lax.dot_general(left, right, (((1,), (1,)), ((), ())), preferred_element_type=F32)


def nn(left, right):
    return lax.dot_general(left, right, (((1,), (0,)), ((), ())), preferred_element_type=F32)


def tn(left, right):
    return lax.dot_general(left, right, (((0,), (0,)), ((), ())), preferred_element_type=F32)


def call(body, out_shapes, n_scalar, n_array, scratch=(), mib=8):
    return pl.pallas_call(
        body,
        out_shape=[jax.ShapeDtypeStruct(s, d) for s, d in out_shapes],
        in_specs=[pl.BlockSpec(memory_space=pltpu.SMEM)] * n_scalar
        + [pl.BlockSpec(memory_space=pltpu.VMEM)] * n_array,
        out_specs=[pl.BlockSpec(memory_space=pltpu.VMEM)] * len(out_shapes),
        scratch_shapes=list(scratch),
        compiler_params=pltpu.CompilerParams(vmem_limit_bytes=mib * 1024 * 1024),
    )


def coded(x):
    return (x * jnp.abs(x)).astype(BF)


def decoded(x):
    wide = x.astype(F32)
    root = jnp.sqrt(jnp.abs(wide))
    return jnp.where(wide < 0, -root, root)


def spread(tokens, cotangent, out):
    width = tokens.shape[1]
    both = jnp.concatenate([tokens[...], cotangent[...]], axis=1)
    for at in range(out.shape[0]):
        out[at] = both


def partial_sums(index, gathered, pair, down, third, first, second, own, ordered):
    width = pair.shape[1]
    both = pair.shape[0]
    chunk = ordered.shape[0] // 16
    per = chunk // gathered.shape[1]
    block = 4 * chunk
    for at, out in ((3, third), (1, first), (2, second), (0, own)):
        for j in range(4):
            slot = at * 4 + j
            rows = gathered[pl.ds(index[slot] * per, per)]
            ordered[slot * chunk : (slot + 1) * chunk, :] = rows.reshape(chunk, 2 * width)
        rows = ordered[at * block : (at + 1) * block, :]
        gate_up = nt(rows[:, :width], pair[...])
        cot = nt(rows[:, width:], down[...])
        out[:, 0:both] = gate_up if at == 0 else coded(gate_up)
        out[:, both:] = cot if at == 0 else coded(cot)


def near_sum(place, own, first, second, third, far, near, back, keep):
    chunk = keep.shape[0]

    def total(at):
        rows = pl.ds(pl.multiple_of(place[at] * chunk, chunk), chunk)
        return own[rows, :] + (decoded(first[rows, :]) + decoded(second[rows, :]) + decoded(third[rows, :]))

    far[...] = coded(total(2))
    near[...] = coded(total(1))
    back[...] = coded(total(3))
    keep[...] = total(0)


def swish(keep, near, far, back, out):
    ff = out.shape[1] // 3
    total = keep[...] + (decoded(near[...]) + decoded(far[...]) + decoded(back[...]))
    gate_sum = total[:, :ff]
    up_sum = total[:, ff : 2 * ff]
    hidden_cot = total[:, 2 * ff :]
    sig = jax.nn.sigmoid(gate_sum)
    gate_cot = hidden_cot * up_sum * sig * (1.0 + gate_sum * (1.0 - sig))
    up_cot = hidden_cot * gate_sum * sig
    out[:, :ff] = gate_cot.astype(BF)
    out[:, ff : 2 * ff] = up_cot.astype(BF)
    out[:, 2 * ff :] = (gate_sum * sig * up_sum).astype(BF)


def outward_rows(c, pair, down):
    both = pair.shape[0]
    return nn(c[:, both:], down[...]).astype(BF), nn(c[:, :both], pair[...]).astype(BF)


def outward_own(c0, pair, down, out):
    width = pair.shape[1]
    layer, back = outward_rows(c0, pair, down)
    out[:, :width] = layer
    out[:, width:] = back


def outward(index, own, c1, c2, c3, pair, down, out):
    width = pair.shape[1]
    chunk = out.shape[1]
    for j in range(4):
        out[index[j]] = own[j * chunk : (j + 1) * chunk, :]
    for at, c in ((1, c1), (2, c2), (3, c3)):
        layer, back = outward_rows(c, pair, down)
        for j in range(4):
            slot = index[at * 4 + j]
            out[slot, :, :width] = layer[j * chunk : (j + 1) * chunk, :]
            out[slot, :, width:] = back[j * chunk : (j + 1) * chunk, :]


def weight_grads(c0, c1, c2, c3, ordered, gate_g, up_g, down_g, allc):
    ff, width = gate_g.shape
    block = c0.shape[0]
    scale = 1.0 / math.sqrt(ordered.shape[0])
    for at, c in enumerate((c0, c1, c2, c3)):
        allc[at * block : (at + 1) * block, :] = c[...]
    both = tn(allc[:, : 2 * ff], ordered[:, :width]) * scale
    gate_g[...] = both[:ff, :].astype(BF)
    up_g[...] = both[ff:, :].astype(BF)
    down_g[...] = (tn(allc[:, 2 * ff :], ordered[:, width:]) * scale).astype(BF)


def last_sum(parts, layer_out, tokens_grad):
    width = layer_out.shape[1]
    total = parts[0].astype(F32)
    for at in range(1, parts.shape[0]):
        total = total + parts[at].astype(F32)
    layer_out[...] = total[:, :width].astype(BF)
    tokens_grad[...] = total[:, width:].astype(BF)


def shards(mesh, tokens, cotangent, gate_weight, up_weight, down_weight):
    cols, depth = mesh.shape["col"], mesh.shape["depth"]
    ranks = mesh.shape["row"] * depth
    ff, width = down_weight.shape
    rows = tokens.shape[0]
    total = rows * ranks
    chunk = total // cols
    block = 4 * chunk
    wide = 3 * ff

    def shift(x, step):
        pairs = []
        for z in range(cols):
            for d in range(depth):
                to = (z + (step if d % 2 == 0 else -step)) % cols
                pairs.append((z * depth + d, to * depth + d))
        return lax.ppermute(x, ("col", "depth"), pairs)

    z = lax.axis_index("col")
    sign = 1 - 2 * (lax.axis_index("depth") % 2)
    four = jnp.arange(4, dtype=jnp.int32)
    classes = (z - sign * jnp.array(NEAR, jnp.int32) + 16) % 4
    index = (classes[:, None] + 4 * four[None, :]).reshape(16).astype(jnp.int32)
    place = ((z // 4 + sign * four + 4) % 4).astype(jnp.int32)

    (mine,) = call(spread, [((ranks, rows, 2 * width), BF)], 0, 2)(tokens, cotangent)
    gathered = lax.all_to_all(mine, GROUP, 0, 0, tiled=True)
    pair = jnp.concatenate([gate_weight.T, up_weight.T], axis=0)
    third, first, second, own, ordered = call(
        partial_sums,
        [((block, wide), BF)] * 3 + [((block, wide), F32), ((total, 2 * width), BF)],
        1,
        3,
        mib=12,
    )(index, gathered, pair, down_weight)
    third = shift(third, -NEAR[3])
    first = shift(first, -NEAR[1])
    second = shift(second, -NEAR[2])
    far, near, back, keep = call(
        near_sum, [((chunk, wide), BF)] * 3 + [((chunk, wide), F32)], 1, 4
    )(place, own, first, second, third)
    far = shift(far, 8)
    near = shift(near, 4)
    back = shift(back, -4)
    (act,) = call(swish, [((chunk, wide), BF)], 0, 4)(keep, near, far, back)
    strided = [[i + 4 * j for j in range(4)] for i in range(4)]
    c0 = lax.all_gather(act, "col", axis=0, tiled=True, axis_index_groups=strided)
    c3 = shift(c0, NEAR[3])
    c1 = shift(c0, NEAR[1])
    c2 = shift(c0, NEAR[2])
    (own_out,) = call(outward_own, [((block, 2 * width), BF)], 0, 3)(c0, pair, down_weight)
    (out,) = call(outward, [((16, chunk, 2 * width), BF)], 1, 6)(
        index, own_out, c1, c2, c3, pair, down_weight
    )
    parts = lax.all_to_all(out.reshape(ranks, rows, 2 * width), GROUP, 0, 0, tiled=True)
    layer_out, tokens_grad = call(last_sum, [((rows, width), BF)] * 2, 0, 1)(parts)
    gate_g, up_g, down_g = call(
        weight_grads, [((ff, width), BF)] * 3, 0, 5, [pltpu.VMEM((total, wide), BF)], mib=12
    )(c0, c1, c2, c3, ordered)
    return (layer_out, tokens_grad, gate_g.T, up_g.T, down_g)


def solution(mesh):
    tok = P(GROUP, "col")
    wide = P("col", GROUP)

    def run(*args):
        return shards(mesh, *args)

    return jax.shard_map(
        run,
        mesh=mesh,
        in_specs=(tok, tok, wide, wide, tok),
        out_specs=(tok, tok, wide, wide, tok),
        check_vma=False,
    )
```

time: 157 us -> 157 us (level)
  Pallas kernels: 8.04 us -> 11.1 us
  other arithmetic: 2.23 us -> 0.16 us
    pallas_call x3 -> x6, Pallas kernels: 6.22 us -> 9.1 us  [the longest x1 3.02 us: shards(): call(partial_sums, [((block, wide), BF)] * 3 + [((block, wide), F32), ((t...]
    unnamed x12 -> x16, local copies, waits for them, and re-layouts: 1.64 us -> 3.63 us
where the time goes in v2:
time: 157 us
  waiting for transfers between devices  63.1 us (40%)
  starting transfers between devices  57.8 us (37%)
  blocking collectives  20.1 us (13%)
  Pallas kernels  11.1 us (7%)
  local copies, waits for them, and re-layouts  3.71 us (2%)
    ppermute x9, starting transfers between devices, shift(): return lax.ppermute(x, ('col', 'depth'), pairs)  41.3 us
    ppermute x9, waiting for transfers between devices, shift(): return lax.ppermute(x, ('col', 'depth'), pairs)  32.3 us
    all_gather x1, blocking collectives, shards(): lax.all_gather(act, 'col', axis=0, tiled=True, axis_index_groups=strided)  20.1 us
    all_to_all x1, waiting for transfers between devices, shards(): gathered = lax.all_to_all(mine, GROUP, 0, 0, tiled=True)  16.7 us
    all_to_all x1, waiting for transfers between devices, shards(): lax.all_to_all(out.reshape(ranks, rows, 2 * width), GROUP, 0, 0, tiled=True)  14.1 us
    all_to_all x1, starting transfers between devices, shards(): gathered = lax.all_to_all(mine, GROUP, 0, 0, tiled=True)  10.6 us
    all_to_all x1, starting transfers between devices, shards(): lax.all_to_all(out.reshape(ranks, rows, 2 * width), GROUP, 0, 0, tiled=True)  5.88 us
    unnamed x16, local copies, waits for them, and re-layouts  3.63 us
  transfers between devices with their start and end apart: 11, of which 9 were waited for; matrix products, arithmetic and copies ran while one was open for 0% of the time, Pallas kernels for 1%

profile of v2, /device:TPU:1, one launch (start us, length us, event | category | flops | bytes accessed | tf_op | source)
XLA Modules:
  0.0 156.7 jit_solution(14922385431874368236)
XLA Ops:
  0.6 0.0 copy-start.3
  0.6 0.7 copy-done.3
  1.3 0.0 copy-start.4
  1.4 0.7 copy-done.4
  2.1 1.1 shard_map.101
  3.2 0.0 copy-start.7
  3.2 0.0 copy-start.5
  3.2 0.0 copy-start.6
  3.2 10.6 %all-to-all-start = ((bf16[32,16,1024]{2,1,0:T(8,128)(2,1)}), bf16[32,16,1024]{2,1,0:T(8,128)(2,1)S(1)}, u32[]{:S(2)}, u32[]{:S(2)}) async-start(bf16[32,16,1024]{2,1,0:T(8,128)(2,1)} %shard_map.101), calls=%async_computation | async-start | bytes 2097152 | tf_op jit(solution)/shard_map/all_to_all | solution.py:174
  13.8 0.0 copy-start
  13.8 0.0 copy-done.7
  13.8 0.1 broadcast_add_fusion
  13.9 0.1 add.50.index
  14.0 0.0 copy-done.5
  14.0 0.0 copy-done.6
  14.0 0.1 pad_maximum_fusion.pair
  14.1 16.7 %all-to-all-done.gathered = bf16[32,16,1024]{2,1,0:T(8,128)(2,1)S(1)} async-done(((bf16[32,16,1024]{2,1,0:T(8,128)(2,1)}), bf16[32,16,1024]{2,1,0:T(8,128)(2,1)S(1)}, u32[]{:S(2)}, u32[]{:S(2)}) %all-to-all-start) | async-done | bytes 1048608 | tf_op jit(solution)/shard_map/all_to_all | solution.py:174
  30.8 0.0 copy-done
  30.8 3.0 %shard_map.102 = (bf16[128,1344]{1,0:T(8,128)(2,1)}, bf16[128,1344]{1,0:T(8,128)(2,1)}, bf16[128,1344]{1,0:T(8,128)(2,1)}, f32[128,1344]{1,0:T(8,128)S(1)}, bf16[512,1024]{1,0:T(8,128)(2,1)S(1)}) custom-call(s32[16]{0:T(128)S(1)} %add.50.index, bf16[32,16,1024]{2,1,0:T(8,128)(2,1)S(1)} %all-to-all-done.gathered, bf16[896,512]{1,0:T(8,128)(2,1)S(1)} %pad_maximum_fusion.pair, ...), custom_call_target="tpu_custom_call" | custom-call | tf_op jit(solution)/shard_map/pallas_call | solution.py:176
  33.8 0.0 copy-start.1
  33.8 1.0 copy-done.1
  34.8 9.2 %collective-permute-start = (bf16[128,1344]{1,0:T(8,128)(2,1)}, bf16[128,1344]{1,0:T(8,128)(2,1)S(1)}, u32[]{:S(2)}, u32[]{:S(2)}) collective-permute-start(bf16[128,1344]{1,0:T(8,128)(2,1)} %get-tuple-element.20), channel_id=1, source_target_pairs={{0,8},{1,121},{2,10},{3,123},{4,12},{5,125},{6,14},{7,127},{8,16},... | collective-permute-start | bytes 1032200 | tf_op jit(solution)/shard_map/ppermute | solution.py:164
  44.0 1.9 %collective-permute-start.1 = (bf16[128,1344]{1,0:T(8,128)(2,1)}, bf16[128,1344]{1,0:T(8,128)(2,1)S(1)}, u32[]{:S(2)}, u32[]{:S(2)}) collective-permute-start(bf16[128,1344]{1,0:T(8,128)(2,1)} %get-tuple-element.21), channel_id=1, source_target_pairs={{0,120},{1,9},{2,122},{3,11},{4,124},{5,13},{6,126},{7,15},{8,0},{... | collective-permute-start | bytes 1032200 | tf_op jit(solution)/shard_map/ppermute | solution.py:164
  45.9 1.9 %collective-permute-start.2 = (bf16[128,1344]{1,0:T(8,128)(2,1)}, bf16[128,1344]{1,0:T(8,128)(2,1)S(1)}, u32[]{:S(2)}, u32[]{:S(2)}) collective-permute-start(bf16[128,1344]{1,0:T(8,128)(2,1)} %get-tuple-element.22), channel_id=1, source_target_pairs={{0,112},{1,17},{2,114},{3,19},{4,116},{5,21},{6,118},{7,23},{8,120... | collective-permute-start | bytes 1032200 | tf_op jit(solution)/shard_map/ppermute | solution.py:164
  47.8 2.0 %collective-permute-done.first = bf16[128,1344]{1,0:T(8,128)(2,1)S(1)} collective-permute-done((bf16[128,1344]{1,0:T(8,128)(2,1)}, bf16[128,1344]{1,0:T(8,128)(2,1)S(1)}, u32[]{:S(2)}, u32[]{:S(2)}) %collective-permute-start) | collective-permute-done | bytes 344096 | tf_op jit(solution)/shard_map/ppermute | solution.py:164
  49.9 3.8 %collective-permute-done.1.second = bf16[128,1344]{1,0:T(8,128)(2,1)S(1)} collective-permute-done((bf16[128,1344]{1,0:T(8,128)(2,1)}, bf16[128,1344]{1,0:T(8,128)(2,1)S(1)}, u32[]{:S(2)}, u32[]{:S(2)}) %collective-permute-start.1) | collective-permute-done | bytes 344096 | tf_op jit(solution)/shard_map/ppermute | solution.py:164
  53.7 6.3 %collective-permute-done.2.third = bf16[128,1344]{1,0:T(8,128)(2,1)S(1)} collective-permute-done((bf16[128,1344]{1,0:T(8,128)(2,1)}, bf16[128,1344]{1,0:T(8,128)(2,1)S(1)}, u32[]{:S(2)}, u32[]{:S(2)}) %collective-permute-start.2) | collective-permute-done | bytes 344096 | tf_op jit(solution)/shard_map/ppermute | solution.py:164
  59.9 1.5 shard_map.103
  61.4 4.5 %collective-permute-start.3 = (bf16[32,1344]{1,0:T(8,128)(2,1)S(1)}, bf16[32,1344]{1,0:T(8,128)(2,1)S(1)}, u32[]{:S(2)}, u32[]{:S(2)}) collective-permute-start(bf16[32,1344]{1,0:T(8,128)(2,1)S(1)} %get-tuple-element.24), channel_id=1, source_target_pairs={{0,32},{1,97},{2,34},{3,99},{4,36},{5,101},{6,38},{7,103},{8,40},{... | collective-permute-start | bytes 258056 | tf_op jit(solution)/shard_map/ppermute | solution.py:164
  66.0 6.0 %collective-permute-start.4 = (bf16[32,1344]{1,0:T(8,128)(2,1)S(1)}, bf16[32,1344]{1,0:T(8,128)(2,1)S(1)}, u32[]{:S(2)}, u32[]{:S(2)}) collective-permute-start(bf16[32,1344]{1,0:T(8,128)(2,1)S(1)} %get-tuple-element.25), channel_id=1, source_target_pairs={{0,64},{1,65},{2,66},{3,67},{4,68},{5,69},{6,70},{7,71},{8,72},{9,... | collective-permute-start | bytes 258056 | tf_op jit(solution)/shard_map/ppermute | solution.py:164
  72.0 7.3 %collective-permute-start.5 = (bf16[32,1344]{1,0:T(8,128)(2,1)S(1)}, bf16[32,1344]{1,0:T(8,128)(2,1)S(1)}, u32[]{:S(2)}, u32[]{:S(2)}) collective-permute-start(bf16[32,1344]{1,0:T(8,128)(2,1)S(1)} %get-tuple-element.26), channel_id=1, source_target_pairs={{0,96},{1,33},{2,98},{3,35},{4,100},{5,37},{6,102},{7,39},{8,104},... | collective-permute-start | bytes 258056 | tf_op jit(solution)/shard_map/ppermute | solution.py:164
  79.2 0.0 collective-permute-done.3.near
  79.2 5.1 %collective-permute-done.4.far = bf16[32,1344]{1,0:T(8,128)(2,1)S(1)} collective-permute-done((bf16[32,1344]{1,0:T(8,128)(2,1)S(1)}, bf16[32,1344]{1,0:T(8,128)(2,1)S(1)}, u32[]{:S(2)}, u32[]{:S(2)}) %collective-permute-start.4) | collective-permute-done | bytes 86048 | tf_op jit(solution)/shard_map/ppermute | solution.py:164
  84.3 2.7 %collective-permute-done.5.back = bf16[32,1344]{1,0:T(8,128)(2,1)S(1)} collective-permute-done((bf16[32,1344]{1,0:T(8,128)(2,1)S(1)}, bf16[32,1344]{1,0:T(8,128)(2,1)S(1)}, u32[]{:S(2)}, u32[]{:S(2)}) %collective-permute-start.5) | collective-permute-done | bytes 86048 | tf_op jit(solution)/shard_map/ppermute | solution.py:164
  87.1 0.3 shard_map.104
  87.4 20.1 %all_gather.3.c0 = bf16[128,1344]{1,0:T(8,128)(2,1)S(1)} all-gather(bf16[32,1344]{1,0:T(8,128)(2,1)S(1)} %shard_map.104), channel_id=1, replica_groups={{0,32,64,96},{8,40,72,104},{16,48,80,112},{24,56,88,120},{1,33,65,97},{..., dimensions={0}, use_global_device_ids=true | all-gather | bytes 430080 | tf_op jit(solution)/shard_map/all_gather | solution.py:194
  107.5 2.8 %collective-permute-start.6 = (bf16[128,1344]{1,0:T(8,128)(2,1)S(1)}, bf16[128,1344]{1,0:T(8,128)(2,1)S(1)}, u32[]{:S(2)}, u32[]{:S(2)}) collective-permute-start(bf16[128,1344]{1,0:T(8,128)(2,1)S(1)} %all_gather.3.c0), channel_id=1, source_target_pairs={{0,120},{1,9},{2,122},{3,11},{4,124},{5,13},{6,126},{7,15},{8,0},{... | collective-permute-start | bytes 1032200 | tf_op jit(solution)/shard_map/ppermute | solution.py:164
  110.2 4.7 %collective-permute-start.7 = (bf16[128,1344]{1,0:T(8,128)(2,1)S(1)}, bf16[128,1344]{1,0:T(8,128)(2,1)S(1)}, u32[]{:S(2)}, u32[]{:S(2)}) collective-permute-start(bf16[128,1344]{1,0:T(8,128)(2,1)S(1)} %all_gather.3.c0), channel_id=1, source_target_pairs={{0,8},{1,121},{2,10},{3,123},{4,12},{5,125},{6,14},{7,127},{8,16},... | collective-permute-start | bytes 1032200 | tf_op jit(solution)/shard_map/ppermute | solution.py:164
  114.9 3.1 %collective-permute-start.8 = (bf16[128,1344]{1,0:T(8,128)(2,1)S(1)}, bf16[128,1344]{1,0:T(8,128)(2,1)S(1)}, u32[]{:S(2)}, u32[]{:S(2)}) collective-permute-start(bf16[128,1344]{1,0:T(8,128)(2,1)S(1)} %all_gather.3.c0), channel_id=1, source_target_pairs={{0,16},{1,113},{2,18},{3,115},{4,20},{5,117},{6,22},{7,119},{8,24}... | collective-permute-start | bytes 1032200 | tf_op jit(solution)/shard_map/ppermute | solution.py:164
  118.0 0.4 shard_map.105.own
  118.4 0.0 collective-permute-done.6.c1
  118.4 5.2 %collective-permute-done.7.c2 = bf16[128,1344]{1,0:T(8,128)(2,1)S(1)} collective-permute-done((bf16[128,1344]{1,0:T(8,128)(2,1)S(1)}, bf16[128,1344]{1,0:T(8,128)(2,1)S(1)}, u32[]{:S(2)}, u32[]{:S(2)}) %collective-permute-start.7) | collective-permute-done | bytes 344096 | tf_op jit(solution)/shard_map/ppermute | solution.py:164
  123.7 7.1 %collective-permute-done.8.c3 = bf16[128,1344]{1,0:T(8,128)(2,1)S(1)} collective-permute-done((bf16[128,1344]{1,0:T(8,128)(2,1)S(1)}, bf16[128,1344]{1,0:T(8,128)(2,1)S(1)}, u32[]{:S(2)}, u32[]{:S(2)}) %collective-permute-start.8) | collective-permute-done | bytes 344096 | tf_op jit(solution)/shard_map/ppermute | solution.py:164
  130.8 2.3 %shard_map.106 = bf16[16,32,1024]{2,1,0:T(8,128)(2,1)} custom-call(s32[16]{0:T(128)S(1)} %add.50.index, bf16[128,1024]{1,0:T(8,128)(2,1)S(1)} %shard_map.105.own, bf16[128,1344]{1,0:T(8,128)(2,1)S(1)} %collective-permute-done.6.c1, bf16[128,1344]{1,0:T(8,128)(2,1)S(1)} %collective-permute-done.7.c2, bf16[128,1344]{1,0:T(8,128)(2,1)S(1)} %collective-permute-done.8.c3, ...), custom_call_target="tpu_custom_call" | custom-call | tf_op jit(solution)/shard_map/pallas_call | solution.py:199
  133.1 5.9 %all-to-all-start.1 = ((bf16[32,16,1024]{2,1,0:T(8,128)(2,1)}), bf16[32,16,1024]{2,1,0:T(8,128)(2,1)S(1)}, u32[]{:S(2)}, u32[]{:S(2)}) async-start(bf16[32,16,1024]{2,1,0:T(8,128)(2,1)} %bitcast.2), calls=%async_computation.1 | async-start | bytes 2097152 | tf_op jit(solution)/shard_map/all_to_all | solution.py:202
  139.0 0.0 copy-start.2
  139.0 1.2 copy-done.2
  140.2 1.7 %shard_map.108 = (bf16[448,512]{1,0:T(8,128)(2,1)}, bf16[448,512]{1,0:T(8,128)(2,1)}, bf16[448,512]{1,0:T(8,128)(2,1)}) custom-call(bf16[128,1344]{1,0:T(8,128)(2,1)S(1)} %all_gather.3.c0, bf16[128,1344]{1,0:T(8,128)(2,1)S(1)} %collective-permute-done.6.c1, bf16[128,1344]{1,0:T(8,128)(2,1)S(1)} %collective-permute-done.7.c2, ...), custom_call_target="tpu_custom_call" | custom-call | tf_op jit(solution)/shard_map/pallas_call | solution.py:204
  141.9 14.1 %all-to-all-done.1.parts = bf16[32,16,1024]{2,1,0:T(8,128)(2,1)S(1)} async-done(((bf16[32,16,1024]{2,1,0:T(8,128)(2,1)}), bf16[32,16,1024]{2,1,0:T(8,128)(2,1)S(1)}, u32[]{:S(2)}, u32[]{:S(2)}) %all-to-all-start.1) | async-done | bytes 1048608 | tf_op jit(solution)/shard_map/all_to_all | solution.py:202
  156.0 0.8 shard_map.107
  (2 shorter events, 0.0 us)
Async XLA Ops:
  0.6 0.7 copy-start.3
  1.3 0.7 copy-start.4
  3.2 10.6 %copy-start.7 = (s32[4]{0:T(128)S(1)}, s32[4]{0:T(128)}, u32[]{:S(2)}) copy-start(s32[4]{0:T(128)} %constant.59.clone) | copy-start | bytes 52
  3.2 10.8 %copy-start.5 = (bf16[512,448]{0,1:T(8,128)(2,1)S(1)}, bf16[512,448]{0,1:T(8,128)(2,1)}, u32[]{:S(2)}) copy-start(bf16[512,448]{0,1:T(8,128)(2,1)} %param.9) | copy-start | bytes 1376260
  3.2 10.8 %copy-start.6 = (bf16[512,448]{0,1:T(8,128)(2,1)S(1)}, bf16[512,448]{0,1:T(8,128)(2,1)}, u32[]{:S(2)}) copy-start(bf16[512,448]{0,1:T(8,128)(2,1)} %param.8) | copy-start | bytes 1376260
  3.2 27.6 %all-to-all-start = ((bf16[32,16,1024]{2,1,0:T(8,128)(2,1)}), bf16[32,16,1024]{2,1,0:T(8,128)(2,1)S(1)}, u32[]{:S(2)}, u32[]{:S(2)}) async-start(bf16[32,16,1024]{2,1,0:T(8,128)(2,1)} %shard_map.101), calls=%async_computation | async-start | bytes 2097152 | tf_op jit(solution)/shard_map/all_to_all | solution.py:174
  13.8 17.0 %copy-start = (bf16[448,512]{1,0:T(8,128)(2,1)S(1)}, bf16[448,512]{1,0:T(8,128)(2,1)}, u32[]{:S(2)}) copy-start(bf16[448,512]{1,0:T(8,128)(2,1)} %down.5) | copy-start | bytes 1376260
  33.8 1.0 copy-start.1
  34.8 15.1 %collective-permute-start = (bf16[128,1344]{1,0:T(8,128)(2,1)}, bf16[128,1344]{1,0:T(8,128)(2,1)S(1)}, u32[]{:S(2)}, u32[]{:S(2)}) collective-permute-start(bf16[128,1344]{1,0:T(8,128)(2,1)} %get-tuple-element.20), channel_id=1, source_target_pairs={{0,8},{1,121},{2,10},{3,123},{4,12},{5,125},{6,14},{7,127},{8,16},... | collective-permute-start | bytes 1032200 | tf_op jit(solution)/shard_map/ppermute | solution.py:164
  44.0 9.7 %collective-permute-start.1 = (bf16[128,1344]{1,0:T(8,128)(2,1)}, bf16[128,1344]{1,0:T(8,128)(2,1)S(1)}, u32[]{:S(2)}, u32[]{:S(2)}) collective-permute-start(bf16[128,1344]{1,0:T(8,128)(2,1)} %get-tuple-element.21), channel_id=1, source_target_pairs={{0,120},{1,9},{2,122},{3,11},{4,124},{5,13},{6,126},{7,15},{8,0},{... | collective-permute-start | bytes 1032200 | tf_op jit(solution)/shard_map/ppermute | solution.py:164
  45.9 14.1 %collective-permute-start.2 = (bf16[128,1344]{1,0:T(8,128)(2,1)}, bf16[128,1344]{1,0:T(8,128)(2,1)S(1)}, u32[]{:S(2)}, u32[]{:S(2)}) collective-permute-start(bf16[128,1344]{1,0:T(8,128)(2,1)} %get-tuple-element.22), channel_id=1, source_target_pairs={{0,112},{1,17},{2,114},{3,19},{4,116},{5,21},{6,118},{7,23},{8,120... | collective-permute-start | bytes 1032200 | tf_op jit(solution)/shard_map/ppermute | solution.py:164
  61.4 17.8 %collective-permute-start.3 = (bf16[32,1344]{1,0:T(8,128)(2,1)S(1)}, bf16[32,1344]{1,0:T(8,128)(2,1)S(1)}, u32[]{:S(2)}, u32[]{:S(2)}) collective-permute-start(bf16[32,1344]{1,0:T(8,128)(2,1)S(1)} %get-tuple-element.24), channel_id=1, source_target_pairs={{0,32},{1,97},{2,34},{3,99},{4,36},{5,101},{6,38},{7,103},{8,40},{... | collective-permute-start | bytes 258056 | tf_op jit(solution)/shard_map/ppermute | solution.py:164
  66.0 18.4 %collective-permute-start.4 = (bf16[32,1344]{1,0:T(8,128)(2,1)S(1)}, bf16[32,1344]{1,0:T(8,128)(2,1)S(1)}, u32[]{:S(2)}, u32[]{:S(2)}) collective-permute-start(bf16[32,1344]{1,0:T(8,128)(2,1)S(1)} %get-tuple-element.25), channel_id=1, source_target_pairs={{0,64},{1,65},{2,66},{3,67},{4,68},{5,69},{6,70},{7,71},{8,72},{9,... | collective-permute-start | bytes 258056 | tf_op jit(solution)/shard_map/ppermute | solution.py:164
  72.0 15.1 %collective-permute-start.5 = (bf16[32,1344]{1,0:T(8,128)(2,1)S(1)}, bf16[32,1344]{1,0:T(8,128)(2,1)S(1)}, u32[]{:S(2)}, u32[]{:S(2)}) collective-permute-start(bf16[32,1344]{1,0:T(8,128)(2,1)S(1)} %get-tuple-element.26), channel_id=1, source_target_pairs={{0,96},{1,33},{2,98},{3,35},{4,100},{5,37},{6,102},{7,39},{8,104},... | collective-permute-start | bytes 258056 | tf_op jit(solution)/shard_map/ppermute | solution.py:164
  107.5 10.9 %collective-permute-start.6 = (bf16[128,1344]{1,0:T(8,128)(2,1)S(1)}, bf16[128,1344]{1,0:T(8,128)(2,1)S(1)}, u32[]{:S(2)}, u32[]{:S(2)}) collective-permute-start(bf16[128,1344]{1,0:T(8,128)(2,1)S(1)} %all_gather.3.c0), channel_id=1, source_target_pairs={{0,120},{1,9},{2,122},{3,11},{4,124},{5,13},{6,126},{7,15},{8,0},{... | collective-permute-start | bytes 1032200 | tf_op jit(solution)/shard_map/ppermute | solution.py:164
  110.2 13.4 %collective-permute-start.7 = (bf16[128,1344]{1,0:T(8,128)(2,1)S(1)}, bf16[128,1344]{1,0:T(8,128)(2,1)S(1)}, u32[]{:S(2)}, u32[]{:S(2)}) collective-permute-start(bf16[128,1344]{1,0:T(8,128)(2,1)S(1)} %all_gather.3.c0), channel_id=1, source_target_pairs={{0,8},{1,121},{2,10},{3,123},{4,12},{5,125},{6,14},{7,127},{8,16},... | collective-permute-start | bytes 1032200 | tf_op jit(solution)/shard_map/ppermute | solution.py:164
  114.9 15.8 %collective-permute-start.8 = (bf16[128,1344]{1,0:T(8,128)(2,1)S(1)}, bf16[128,1344]{1,0:T(8,128)(2,1)S(1)}, u32[]{:S(2)}, u32[]{:S(2)}) collective-permute-start(bf16[128,1344]{1,0:T(8,128)(2,1)S(1)} %all_gather.3.c0), channel_id=1, source_target_pairs={{0,16},{1,113},{2,18},{3,115},{4,20},{5,117},{6,22},{7,119},{8,24}... | collective-permute-start | bytes 1032200 | tf_op jit(solution)/shard_map/ppermute | solution.py:164
  133.1 22.9 %all-to-all-start.1 = ((bf16[32,16,1024]{2,1,0:T(8,128)(2,1)}), bf16[32,16,1024]{2,1,0:T(8,128)(2,1)S(1)}, u32[]{:S(2)}, u32[]{:S(2)}) async-start(bf16[32,16,1024]{2,1,0:T(8,128)(2,1)} %bitcast.2), calls=%async_computation.1 | async-start | bytes 2097152 | tf_op jit(solution)/shard_map/all_to_all | solution.py:202
  139.0 1.2 copy-start.2

commit v3 on v2

--- a/solution.py
+++ b/solution.py
@@ -1,3 +1,4 @@
+import functools
 import math
 
 import jax
@@ -25,13 +26,16 @@
     return lax.dot_general(left, right, (((0,), (0,)), ((), ())), preferred_element_type=F32)
 
 
-def call(body, out_shapes, n_scalar, n_array, scratch=(), mib=8):
+def call(body, out_shapes, n_scalar, n_array, scratch=(), mib=8, outside=(), outside_out=()):
+    def place(at, away):
+        return pl.BlockSpec(memory_space=pl.ANY if at in away else pltpu.VMEM)
+
     return pl.pallas_call(
         body,
         out_shape=[jax.ShapeDtypeStruct(s, d) for s, d in out_shapes],
         in_specs=[pl.BlockSpec(memory_space=pltpu.SMEM)] * n_scalar
-        + [pl.BlockSpec(memory_space=pltpu.VMEM)] * n_array,
-        out_specs=[pl.BlockSpec(memory_space=pltpu.VMEM)] * len(out_shapes),
+        + [place(at, outside) for at in range(n_array)],
+        out_specs=[place(at, outside_out) for at in range(len(out_shapes))],
         scratch_shapes=list(scratch),
         compiler_params=pltpu.CompilerParams(vmem_limit_bytes=mib * 1024 * 1024),
     )
@@ -47,32 +51,43 @@
     return jnp.where(wide < 0, -root, root)
 
 
-def spread(tokens, cotangent, out):
+def spread(tokens, cotangent, out, both, sems):
     width = tokens.shape[1]
-    both = jnp.concatenate([tokens[...], cotangent[...]], axis=1)
+    left = pltpu.make_async_copy(tokens, both.at[:, :width], sems.at[0])
+    right = pltpu.make_async_copy(cotangent, both.at[:, width:], sems.at[1])
+    left.start()
+    right.start()
+    left.wait()
+    right.wait()
     for at in range(out.shape[0]):
-        out[at] = both
-
-
-def partial_sums(index, gathered, pair, down, third, first, second, own, ordered):
+        out[at] = both[...]
+
+
+def partial_sums(index, mine, other, pair, down, third, first, second, own, kept, ordered, sems):
     width = pair.shape[1]
     both = pair.shape[0]
-    chunk = ordered.shape[0] // 16
-    per = chunk // gathered.shape[1]
+    rows = mine.shape[1]
+    chunk = 2 * rows
     block = 4 * chunk
+    copies = []
     for at, out in ((3, third), (1, first), (2, second), (0, own)):
         for j in range(4):
             slot = at * 4 + j
-            rows = gathered[pl.ds(index[slot] * per, per)]
-            ordered[slot * chunk : (slot + 1) * chunk, :] = rows.reshape(chunk, 2 * width)
-        rows = ordered[at * block : (at + 1) * block, :]
-        gate_up = nt(rows[:, :width], pair[...])
-        cot = nt(rows[:, width:], down[...])
+            ordered[slot * chunk : slot * chunk + rows, :] = mine[index[slot]]
+            ordered[slot * chunk + rows : (slot + 1) * chunk, :] = other[index[slot]]
+        here = pl.ds(at * block, block)
+        copies.append(pltpu.make_async_copy(ordered.at[here], kept.at[here], sems.at[at]))
+        copies[-1].start()
+        block_rows = ordered[at * block : (at + 1) * block, :]
+        gate_up = nt(block_rows[:, :width], pair[...])
+        cot = nt(block_rows[:, width:], down[...])
         out[:, 0:both] = gate_up if at == 0 else coded(gate_up)
         out[:, both:] = cot if at == 0 else coded(cot)
-
-
-def near_sum(place, own, first, second, third, far, near, back, keep):
+    for copy in copies:
+        copy.wait()
+
+
+def near_sum(place, own, third, first, second, far, near, back, keep):
     chunk = keep.shape[0]
 
     def total(at):
@@ -85,7 +100,7 @@
     keep[...] = total(0)
 
 
-def swish(keep, near, far, back, out):
+def swish(keep, far, near, back, out):
     ff = out.shape[1] // 3
     total = keep[...] + (decoded(near[...]) + decoded(far[...]) + decoded(back[...]))
     gate_sum = total[:, :ff]
@@ -99,29 +114,24 @@
     out[:, 2 * ff :] = (gate_sum * sig * up_sum).astype(BF)
 
 
-def outward_rows(c, pair, down):
+def outward(half, index, c3, c1, c2, c0, pair, down, out, picked):
+    width = pair.shape[1]
     both = pair.shape[0]
-    return nn(c[:, both:], down[...]).astype(BF), nn(c[:, :both], pair[...]).astype(BF)
-
-
-def outward_own(c0, pair, down, out):
-    width = pair.shape[1]
-    layer, back = outward_rows(c0, pair, down)
-    out[:, :width] = layer
-    out[:, width:] = back
-
-
-def outward(index, own, c1, c2, c3, pair, down, out):
-    width = pair.shape[1]
-    chunk = out.shape[1]
-    for j in range(4):
-        out[index[j]] = own[j * chunk : (j + 1) * chunk, :]
-    for at, c in ((1, c1), (2, c2), (3, c3)):
-        layer, back = outward_rows(c, pair, down)
+    rows = out.shape[1]
+    for at, c in ((3, c3), (1, c1), (2, c2), (0, c0)):
         for j in range(4):
-            slot = index[at * 4 + j]
-            out[slot, :, :width] = layer[j * chunk : (j + 1) * chunk, :]
-            out[slot, :, width:] = back[j * chunk : (j + 1) * chunk, :]
+            slot = at * 4 + j
+            first = j * 2 * rows + half * rows
+            picked[slot * rows : (slot + 1) * rows, :] = c[first : first + rows, :]
+    layer = nn(picked[:, both:], down[...]).astype(out.dtype)
+    back = nn(picked[:, :both], pair[...]).astype(out.dtype)
+    for slot in range(16):
+        out[index[slot], :, :width] = layer[slot * rows : (slot + 1) * rows, :]
+        out[index[slot], :, width:] = back[slot * rows : (slot + 1) * rows, :]
+
+
+def core_sum(keep, arrived, out):
+    out[...] = (keep[...] + arrived[...].astype(F32)).astype(BF)
 
 
 def weight_grads(c0, c1, c2, c3, ordered, gate_g, up_g, down_g, allc):
@@ -170,36 +180,63 @@
     index = (classes[:, None] + 4 * four[None, :]).reshape(16).astype(jnp.int32)
     place = ((z // 4 + sign * four + 4) % 4).astype(jnp.int32)
 
-    (mine,) = call(spread, [((ranks, rows, 2 * width), BF)], 0, 2)(tokens, cotangent)
-    gathered = lax.all_to_all(mine, GROUP, 0, 0, tiled=True)
+    cores = 2
+    chips = ranks // cores
+    same_core = [[c + cores * a for a in range(chips)] for c in range(cores)]
+
+    def swap(x):
+        return lax.ppermute(x, "depth", [(d, d ^ 1) for d in range(depth)])
+
+    def exchange(x):
+        return lax.all_to_all(x, GROUP, 0, 0, tiled=True, axis_index_groups=same_core)
+
+    (sent,) = call(
+        spread,
+        [((chips, rows, 2 * width), BF)],
+        0,
+        2,
+        [pltpu.VMEM((rows, 2 * width), BF), pltpu.SemaphoreType.DMA((2,))],
+        outside=(0, 1),
+    )(tokens, cotangent)
+    mine = exchange(sent)
+    other = swap(mine)
     pair = jnp.concatenate([gate_weight.T, up_weight.T], axis=0)
     third, first, second, own, ordered = call(
         partial_sums,
         [((block, wide), BF)] * 3 + [((block, wide), F32), ((total, 2 * width), BF)],
         1,
-        3,
+        4,
+        [pltpu.VMEM((total, 2 * width), BF), pltpu.SemaphoreType.DMA((4,))],
         mib=12,
-    )(index, gathered, pair, down_weight)
+        outside_out=(4,),
+    )(index, mine, other, pair, down_weight)
     third = shift(third, -NEAR[3])
     first = shift(first, -NEAR[1])
     second = shift(second, -NEAR[2])
     far, near, back, keep = call(
         near_sum, [((chunk, wide), BF)] * 3 + [((chunk, wide), F32)], 1, 4
-    )(place, own, first, second, third)
+    )(place, own, third, first, second)
     far = shift(far, 8)
     near = shift(near, 4)
     back = shift(back, -4)
-    (act,) = call(swish, [((chunk, wide), BF)], 0, 4)(keep, near, far, back)
+    (act,) = call(swish, [((chunk, wide), BF)], 0, 4)(keep, far, near, back)
     strided = [[i + 4 * j for j in range(4)] for i in range(4)]
     c0 = lax.all_gather(act, "col", axis=0, tiled=True, axis_index_groups=strided)
     c3 = shift(c0, NEAR[3])
     c1 = shift(c0, NEAR[1])
     c2 = shift(c0, NEAR[2])
-    (own_out,) = call(outward_own, [((block, 2 * width), BF)], 0, 3)(c0, pair, down_weight)
-    (out,) = call(outward, [((16, chunk, 2 * width), BF)], 1, 6)(
-        index, own_out, c1, c2, c3, pair, down_weight
-    )
-    parts = lax.all_to_all(out.reshape(ranks, rows, 2 * width), GROUP, 0, 0, tiled=True)
+    def half_out(half, dtype):
+        return call(
+            functools.partial(outward, half),
+            [((chips, rows, 2 * width), dtype)],
+            1,
+            6,
+            [pltpu.VMEM((total // cores, wide), BF)],
+        )(index, c3, c1, c2, c0, pair, down_weight)[0]
+
+    arrived = swap(half_out(1, BF))
+    (summed,) = call(core_sum, [((chips, rows, 2 * width), BF)], 0, 2)(half_out(0, F32), arrived)
+    parts = exchange(summed)
     layer_out, tokens_grad = call(last_sum, [((rows, width), BF)] * 2, 0, 1)(parts)
     gate_g, up_g, down_g = call(
         weight_grads, [((ff, width), BF)] * 3, 0, 5, [pltpu.VMEM((total, wide), BF)], mib=12

time: 157 us -> 152 us (0.968)
  waiting for transfers between devices: 63.1 us -> 44.5 us
  starting transfers between devices: 57.8 us -> 65.6 us
  blocking collectives: 20.1 us -> 23.1 us
    all_to_all x2, waiting for transfers between devices: 30.8 us -> 16.3 us  [exchange(): lax.all_to_all(x, GROUP, 0, 0, tiled=True, axis_index_groups=same_core)]
    ppermute x0 -> x2, starting transfers between devices: none -> 10.6 us  [swap(): return lax.ppermute(x, 'depth', [(d, d ^ 1) for d in range(depth)])]
    all_to_all x2, starting transfers between devices: 16.5 us -> 11.2 us  [exchange(): lax.all_to_all(x, GROUP, 0, 0, tiled=True, axis_index_groups=same_core)]
    ppermute x9, waiting for transfers between devices: 32.3 us -> 27.5 us  [shift(): return lax.ppermute(x, ('col', 'depth'), pairs)]
    all_gather x1, blocking collectives: 20.1 us -> 23.1 us  [shards(): lax.all_gather(act, 'col', axis=0, tiled=True, axis_index_groups=strided)]
    ppermute x9, starting transfers between devices: 41.3 us -> 43.8 us  [shift(): return lax.ppermute(x, ('col', 'depth'), pairs)]
    pallas_call x4 -> x5, Pallas kernels: 4.15 us -> 4.31 us  [the longest x2 2.21 us: half_out(): call(functools.partial(outward, half), [((chips, rows, 2 * width), dtype)...]
    unnamed x16 -> x14, local copies, waits for them, and re-layouts: 3.63 us -> 3.68 us
  transfers between devices with their start and end apart: 11 -> 13, of which waited for: 9 -> 10; matrix products, arithmetic and copies ran while one was open for 0% -> 1% of each run, Pallas kernels for 1% -> 2%
where the time goes in v3:
time: 152 us; the launch traced here: 151 us
  starting transfers between devices  65.6 us (43%)
  waiting for transfers between devices  44.5 us (29%)
  blocking collectives  23.1 us (15%)
  Pallas kernels  12.1 us (8%)
  local copies, waits for them, and re-layouts  3.76 us (2%)
    ppermute x9, starting transfers between devices, shift(): return lax.ppermute(x, ('col', 'depth'), pairs)  43.8 us
    ppermute x9, waiting for transfers between devices, shift(): return lax.ppermute(x, ('col', 'depth'), pairs)  27.5 us
    all_gather x1, blocking collectives, shards(): lax.all_gather(act, 'col', axis=0, tiled=True, axis_index_groups=strided)  23.1 us
    all_to_all x2, waiting for transfers between devices, exchange(): lax.all_to_all(x, GROUP, 0, 0, tiled=True, axis_index_groups=same_core)  16.3 us
    all_to_all x2, starting transfers between devices, exchange(): lax.all_to_all(x, GROUP, 0, 0, tiled=True, axis_index_groups=same_core)  11.2 us
    ppermute x2, starting transfers between devices, swap(): return lax.ppermute(x, 'depth', [(d, d ^ 1) for d in range(depth)])  10.6 us
    pallas_call x1, Pallas kernels, shards(): call(partial_sums, [((block, wide), BF)] * 3 + [((block, wide), F32), ((t...  3.95 us
    unnamed x14, local copies, waits for them, and re-layouts  3.68 us
  transfers between devices with their start and end apart: 13, of which 10 were waited for; matrix products, arithmetic and copies ran while one was open for 1% of the time, Pallas kernels for 2%

profile of v3, /device:TPU:1, one launch (start us, length us, event | category | flops | bytes accessed | tf_op | source)
XLA Modules:
  0.0 151.2 jit_solution(2075934414096359605)
XLA Ops:
  0.6 0.0 copy-start.6
  0.6 0.0 copy-start.3
  0.7 0.7 copy-done.3
  1.4 0.0 copy-start.4
  1.4 0.7 copy-done.4
  2.1 0.0 copy-start.5
  2.1 0.9 shard_map.101
  3.0 7.6 %all-to-all-start = ((bf16[16,16,1024]{2,1,0:T(8,128)(2,1)}), bf16[16,16,1024]{2,1,0:T(8,128)(2,1)S(1)}, u32[]{:S(2)}, u32[]{:S(2)}) async-start(bf16[16,16,1024]{2,1,0:T(8,128)(2,1)} %shard_map.101), calls=%async_computation | async-start | bytes 1048576 | tf_op jit(solution)/shard_map/all_to_all | solution.py:191
  10.6 0.0 copy-start
  10.6 9.0 %all-to-all-done.mine = bf16[16,16,1024]{2,1,0:T(8,128)(2,1)S(1)} async-done(((bf16[16,16,1024]{2,1,0:T(8,128)(2,1)}), bf16[16,16,1024]{2,1,0:T(8,128)(2,1)S(1)}, u32[]{:S(2)}, u32[]{:S(2)}) %all-to-all-start) | async-done | bytes 524320 | tf_op jit(solution)/shard_map/all_to_all | solution.py:191
  19.6 5.8 %collective-permute-start = (bf16[16,16,1024]{2,1,0:T(8,128)(2,1)S(1)}, bf16[16,16,1024]{2,1,0:T(8,128)(2,1)S(1)}, u32[]{:S(2)}, u32[]{:S(2)}) collective-permute-start(bf16[16,16,1024]{2,1,0:T(8,128)(2,1)S(1)} %all-to-all-done.mine), channel_id=1, source_target_pairs={{0,1},{1,0},{2,3},{3,2},{4,5},{5,4},{6,7},{7,6},{8,9},{9,8},{10,11... | collective-permute-start | bytes 1572872 | tf_op jit(solution)/shard_map/ppermute | solution.py:188
  25.4 0.0 copy-done.6
  25.4 0.1 broadcast_add_fusion
  25.5 0.1 add.50.index
  25.6 0.0 copy-done.5
  25.6 1.1 pad_maximum_fusion.pair
  26.7 0.2 collective-permute-done.other
  26.9 0.0 copy-done
  26.9 3.9 %shard_map.102 = (bf16[128,1344]{1,0:T(8,128)(2,1)}, bf16[128,1344]{1,0:T(8,128)(2,1)}, bf16[128,1344]{1,0:T(8,128)(2,1)}, f32[128,1344]{1,0:T(8,128)S(1)}, bf16[512,1024]{1,0:T(8,128)(2,1)S(1)}) custom-call(s32[16]{0:T(128)S(1)} %add.50.index, bf16[16,16,1024]{2,1,0:T(8,128)(2,1)S(1)} %all-to-all-done.mine, ...), custom_call_target="tpu_custom_call" | custom-call | tf_op jit(solution)/shard_map/pallas_call | solution.py:204
  30.9 0.0 copy-start.1
  30.9 1.0 copy-done.1
  31.9 4.4 %collective-permute-start.1 = (bf16[128,1344]{1,0:T(8,128)(2,1)}, bf16[128,1344]{1,0:T(8,128)(2,1)S(1)}, u32[]{:S(2)}, u32[]{:S(2)}) collective-permute-start(bf16[128,1344]{1,0:T(8,128)(2,1)} %get-tuple-element.20), channel_id=1, source_target_pairs={{0,112},{1,17},{2,114},{3,19},{4,116},{5,21},{6,118},{7,23},{8,120... | collective-permute-start | bytes 1032200 | tf_op jit(solution)/shard_map/ppermute | solution.py:174
  36.3 8.1 %collective-permute-start.2 = (bf16[128,1344]{1,0:T(8,128)(2,1)}, bf16[128,1344]{1,0:T(8,128)(2,1)S(1)}, u32[]{:S(2)}, u32[]{:S(2)}) collective-permute-start(bf16[128,1344]{1,0:T(8,128)(2,1)} %get-tuple-element.21), channel_id=1, source_target_pairs={{0,8},{1,121},{2,10},{3,123},{4,12},{5,125},{6,14},{7,127},{8,16},... | collective-permute-start | bytes 1032200 | tf_op jit(solution)/shard_map/ppermute | solution.py:174
  44.4 1.9 %collective-permute-start.3 = (bf16[128,1344]{1,0:T(8,128)(2,1)}, bf16[128,1344]{1,0:T(8,128)(2,1)S(1)}, u32[]{:S(2)}, u32[]{:S(2)}) collective-permute-start(bf16[128,1344]{1,0:T(8,128)(2,1)} %get-tuple-element.22), channel_id=1, source_target_pairs={{0,120},{1,9},{2,122},{3,11},{4,124},{5,13},{6,126},{7,15},{8,0},{... | collective-permute-start | bytes 1032200 | tf_op jit(solution)/shard_map/ppermute | solution.py:174
  46.4 3.2 %collective-permute-done.1.third = bf16[128,1344]{1,0:T(8,128)(2,1)S(1)} collective-permute-done((bf16[128,1344]{1,0:T(8,128)(2,1)}, bf16[128,1344]{1,0:T(8,128)(2,1)S(1)}, u32[]{:S(2)}, u32[]{:S(2)}) %collective-permute-start.1) | collective-permute-done | bytes 344096 | tf_op jit(solution)/shard_map/ppermute | solution.py:174
  49.6 7.2 %collective-permute-done.2.first = bf16[128,1344]{1,0:T(8,128)(2,1)S(1)} collective-permute-done((bf16[128,1344]{1,0:T(8,128)(2,1)}, bf16[128,1344]{1,0:T(8,128)(2,1)S(1)}, u32[]{:S(2)}, u32[]{:S(2)}) %collective-permute-start.2) | collective-permute-done | bytes 344096 | tf_op jit(solution)/shard_map/ppermute | solution.py:174
  56.8 2.3 %collective-permute-done.3.second = bf16[128,1344]{1,0:T(8,128)(2,1)S(1)} collective-permute-done((bf16[128,1344]{1,0:T(8,128)(2,1)}, bf16[128,1344]{1,0:T(8,128)(2,1)S(1)}, u32[]{:S(2)}, u32[]{:S(2)}) %collective-permute-start.3) | collective-permute-done | bytes 344096 | tf_op jit(solution)/shard_map/ppermute | solution.py:174
  59.1 1.5 shard_map.103
  60.6 9.4 %collective-permute-start.4 = (bf16[32,1344]{1,0:T(8,128)(2,1)S(1)}, bf16[32,1344]{1,0:T(8,128)(2,1)S(1)}, u32[]{:S(2)}, u32[]{:S(2)}) collective-permute-start(bf16[32,1344]{1,0:T(8,128)(2,1)S(1)} %get-tuple-element.24), channel_id=1, source_target_pairs={{0,64},{1,65},{2,66},{3,67},{4,68},{5,69},{6,70},{7,71},{8,72},{9,... | collective-permute-start | bytes 258056 | tf_op jit(solution)/shard_map/ppermute | solution.py:174
  70.0 1.9 %collective-permute-start.5 = (bf16[32,1344]{1,0:T(8,128)(2,1)S(1)}, bf16[32,1344]{1,0:T(8,128)(2,1)S(1)}, u32[]{:S(2)}, u32[]{:S(2)}) collective-permute-start(bf16[32,1344]{1,0:T(8,128)(2,1)S(1)} %get-tuple-element.25), channel_id=1, source_target_pairs={{0,32},{1,97},{2,34},{3,99},{4,36},{5,101},{6,38},{7,103},{8,40},{... | collective-permute-start | bytes 258056 | tf_op jit(solution)/shard_map/ppermute | solution.py:174
  71.9 7.3 %collective-permute-start.6 = (bf16[32,1344]{1,0:T(8,128)(2,1)S(1)}, bf16[32,1344]{1,0:T(8,128)(2,1)S(1)}, u32[]{:S(2)}, u32[]{:S(2)}) collective-permute-start(bf16[32,1344]{1,0:T(8,128)(2,1)S(1)} %get-tuple-element.26), channel_id=1, source_target_pairs={{0,96},{1,33},{2,98},{3,35},{4,100},{5,37},{6,102},{7,39},{8,104},... | collective-permute-start | bytes 258056 | tf_op jit(solution)/shard_map/ppermute | solution.py:174
  79.2 0.0 collective-permute-done.4.far
  79.2 4.6 %collective-permute-done.5.near = bf16[32,1344]{1,0:T(8,128)(2,1)S(1)} collective-permute-done((bf16[32,1344]{1,0:T(8,128)(2,1)S(1)}, bf16[32,1344]{1,0:T(8,128)(2,1)S(1)}, u32[]{:S(2)}, u32[]{:S(2)}) %collective-permute-start.5) | collective-permute-done | bytes 86048 | tf_op jit(solution)/shard_map/ppermute | solution.py:174
  83.8 0.0 collective-permute-done.6.back
  83.9 0.3 shard_map.104
  84.2 23.1 %all_gather.3.c0 = bf16[128,1344]{1,0:T(8,128)(2,1)S(1)} all-gather(bf16[32,1344]{1,0:T(8,128)(2,1)S(1)} %shard_map.104), channel_id=1, replica_groups={{0,32,64,96},{8,40,72,104},{16,48,80,112},{24,56,88,120},{1,33,65,97},{..., dimensions={0}, use_global_device_ids=true | all-gather | bytes 430080 | tf_op jit(solution)/shard_map/all_gather | solution.py:224
  107.3 2.9 %collective-permute-start.7 = (bf16[128,1344]{1,0:T(8,128)(2,1)S(1)}, bf16[128,1344]{1,0:T(8,128)(2,1)S(1)}, u32[]{:S(2)}, u32[]{:S(2)}) collective-permute-start(bf16[128,1344]{1,0:T(8,128)(2,1)S(1)} %all_gather.3.c0), channel_id=1, source_target_pairs={{0,16},{1,113},{2,18},{3,115},{4,20},{5,117},{6,22},{7,119},{8,24}... | collective-permute-start | bytes 1032200 | tf_op jit(solution)/shard_map/ppermute | solution.py:174
  110.2 5.9 %collective-permute-start.8 = (bf16[128,1344]{1,0:T(8,128)(2,1)S(1)}, bf16[128,1344]{1,0:T(8,128)(2,1)S(1)}, u32[]{:S(2)}, u32[]{:S(2)}) collective-permute-start(bf16[128,1344]{1,0:T(8,128)(2,1)S(1)} %all_gather.3.c0), channel_id=1, source_target_pairs={{0,120},{1,9},{2,122},{3,11},{4,124},{5,13},{6,126},{7,15},{8,0},{... | collective-permute-start | bytes 1032200 | tf_op jit(solution)/shard_map/ppermute | solution.py:174
  116.1 1.9 %collective-permute-start.9 = (bf16[128,1344]{1,0:T(8,128)(2,1)S(1)}, bf16[128,1344]{1,0:T(8,128)(2,1)S(1)}, u32[]{:S(2)}, u32[]{:S(2)}) collective-permute-start(bf16[128,1344]{1,0:T(8,128)(2,1)S(1)} %all_gather.3.c0), channel_id=1, source_target_pairs={{0,8},{1,121},{2,10},{3,123},{4,12},{5,125},{6,14},{7,127},{8,16},... | collective-permute-start | bytes 1032200 | tf_op jit(solution)/shard_map/ppermute | solution.py:174
  118.1 0.0 collective-permute-done.7.c3
  118.1 9.8 %collective-permute-done.8.c1 = bf16[128,1344]{1,0:T(8,128)(2,1)S(1)} collective-permute-done((bf16[128,1344]{1,0:T(8,128)(2,1)S(1)}, bf16[128,1344]{1,0:T(8,128)(2,1)S(1)}, u32[]{:S(2)}, u32[]{:S(2)}) %collective-permute-start.8) | collective-permute-done | bytes 344096 | tf_op jit(solution)/shard_map/ppermute | solution.py:174
  127.9 0.4 collective-permute-done.9.c2
  128.3 1.1 shard_map.106
  129.4 4.9 %collective-permute-start.10 = (bf16[16,16,1024]{2,1,0:T(8,128)(2,1)S(1)}, bf16[16,16,1024]{2,1,0:T(8,128)(2,1)S(1)}, u32[]{:S(2)}, u32[]{:S(2)}) collective-permute-start(bf16[16,16,1024]{2,1,0:T(8,128)(2,1)S(1)} %shard_map.106), channel_id=1, source_target_pairs={{0,1},{1,0},{2,3},{3,2},{4,5},{5,4},{6,7},{7,6},{8,9},{9,8},{10,11... | collective-permute-start | bytes 1572872 | tf_op jit(solution)/shard_map/ppermute | solution.py:188
  134.3 1.1 shard_map.105.keep
  135.4 0.4 collective-permute-done.10.arrived
  135.8 0.9 shard_map.107
  136.7 3.6 %all-to-all-start.1 = ((bf16[16,16,1024]{2,1,0:T(8,128)(2,1)}), bf16[16,16,1024]{2,1,0:T(8,128)(2,1)S(1)}, u32[]{:S(2)}, u32[]{:S(2)}) async-start(bf16[16,16,1024]{2,1,0:T(8,128)(2,1)} %shard_map.107), calls=%async_computation.1 | async-start | bytes 1048576 | tf_op jit(solution)/shard_map/all_to_all | solution.py:191
  140.3 0.0 copy-start.2
  140.3 1.2 copy-done.2
  141.5 1.7 %shard_map.109 = (bf16[448,512]{1,0:T(8,128)(2,1)}, bf16[448,512]{1,0:T(8,128)(2,1)}, bf16[448,512]{1,0:T(8,128)(2,1)}) custom-call(bf16[128,1344]{1,0:T(8,128)(2,1)S(1)} %all_gather.3.c0, bf16[128,1344]{1,0:T(8,128)(2,1)S(1)} %collective-permute-done.8.c1, bf16[128,1344]{1,0:T(8,128)(2,1)S(1)} %collective-permute-done.9.c2, ...), custom_call_target="tpu_custom_call" | custom-call | tf_op jit(solution)/shard_map/pallas_call | solution.py:241
  143.2 7.3 %all-to-all-done.1.parts = bf16[16,16,1024]{2,1,0:T(8,128)(2,1)S(1)} async-done(((bf16[16,16,1024]{2,1,0:T(8,128)(2,1)}), bf16[16,16,1024]{2,1,0:T(8,128)(2,1)S(1)}, u32[]{:S(2)}, u32[]{:S(2)}) %all-to-all-start.1) | async-done | bytes 524320 | tf_op jit(solution)/shard_map/all_to_all | solution.py:191
  150.5 0.7 shard_map.108
  (2 shorter events, 0.0 us)
Async XLA Ops:
  0.6 24.8 %copy-start.6 = (s32[4]{0:T(128)S(1)}, s32[4]{0:T(128)}, u32[]{:S(2)}) copy-start(s32[4]{0:T(128)} %constant.59.clone) | copy-start | bytes 52
  0.6 0.7 copy-start.3
  1.4 0.7 copy-start.4
  2.1 23.5 %copy-start.5 = (bf16[512,448]{0,1:T(8,128)(2,1)S(1)}, bf16[512,448]{0,1:T(8,128)(2,1)}, u32[]{:S(2)}) copy-start(bf16[512,448]{0,1:T(8,128)(2,1)} %param.9) | copy-start | bytes 1376260
  3.0 16.7 %all-to-all-start = ((bf16[16,16,1024]{2,1,0:T(8,128)(2,1)}), bf16[16,16,1024]{2,1,0:T(8,128)(2,1)S(1)}, u32[]{:S(2)}, u32[]{:S(2)}) async-start(bf16[16,16,1024]{2,1,0:T(8,128)(2,1)} %shard_map.101), calls=%async_computation | async-start | bytes 1048576 | tf_op jit(solution)/shard_map/all_to_all | solution.py:191
  10.6 16.3 %copy-start = (bf16[448,512]{1,0:T(8,128)(2,1)S(1)}, bf16[448,512]{1,0:T(8,128)(2,1)}, u32[]{:S(2)}) copy-start(bf16[448,512]{1,0:T(8,128)(2,1)} %down.5) | copy-start | bytes 1376260
  19.6 7.3 %collective-permute-start = (bf16[16,16,1024]{2,1,0:T(8,128)(2,1)S(1)}, bf16[16,16,1024]{2,1,0:T(8,128)(2,1)S(1)}, u32[]{:S(2)}, u32[]{:S(2)}) collective-permute-start(bf16[16,16,1024]{2,1,0:T(8,128)(2,1)S(1)} %all-to-all-done.mine), channel_id=1, source_target_pairs={{0,1},{1,0},{2,3},{3,2},{4,5},{5,4},{6,7},{7,6},{8,9},{9,8},{10,11... | collective-permute-start | bytes 1572872 | tf_op jit(solution)/shard_map/ppermute | solution.py:188
  30.9 1.0 copy-start.1
  31.9 17.7 %collective-permute-start.1 = (bf16[128,1344]{1,0:T(8,128)(2,1)}, bf16[128,1344]{1,0:T(8,128)(2,1)S(1)}, u32[]{:S(2)}, u32[]{:S(2)}) collective-permute-start(bf16[128,1344]{1,0:T(8,128)(2,1)} %get-tuple-element.20), channel_id=1, source_target_pairs={{0,112},{1,17},{2,114},{3,19},{4,116},{5,21},{6,118},{7,23},{8,120... | collective-permute-start | bytes 1032200 | tf_op jit(solution)/shard_map/ppermute | solution.py:174
  36.3 20.5 %collective-permute-start.2 = (bf16[128,1344]{1,0:T(8,128)(2,1)}, bf16[128,1344]{1,0:T(8,128)(2,1)S(1)}, u32[]{:S(2)}, u32[]{:S(2)}) collective-permute-start(bf16[128,1344]{1,0:T(8,128)(2,1)} %get-tuple-element.21), channel_id=1, source_target_pairs={{0,8},{1,121},{2,10},{3,123},{4,12},{5,125},{6,14},{7,127},{8,16},... | collective-permute-start | bytes 1032200 | tf_op jit(solution)/shard_map/ppermute | solution.py:174
  44.4 14.7 %collective-permute-start.3 = (bf16[128,1344]{1,0:T(8,128)(2,1)}, bf16[128,1344]{1,0:T(8,128)(2,1)S(1)}, u32[]{:S(2)}, u32[]{:S(2)}) collective-permute-start(bf16[128,1344]{1,0:T(8,128)(2,1)} %get-tuple-element.22), channel_id=1, source_target_pairs={{0,120},{1,9},{2,122},{3,11},{4,124},{5,13},{6,126},{7,15},{8,0},{... | collective-permute-start | bytes 1032200 | tf_op jit(solution)/shard_map/ppermute | solution.py:174
  60.6 18.6 %collective-permute-start.4 = (bf16[32,1344]{1,0:T(8,128)(2,1)S(1)}, bf16[32,1344]{1,0:T(8,128)(2,1)S(1)}, u32[]{:S(2)}, u32[]{:S(2)}) collective-permute-start(bf16[32,1344]{1,0:T(8,128)(2,1)S(1)} %get-tuple-element.24), channel_id=1, source_target_pairs={{0,64},{1,65},{2,66},{3,67},{4,68},{5,69},{6,70},{7,71},{8,72},{9,... | collective-permute-start | bytes 258056 | tf_op jit(solution)/shard_map/ppermute | solution.py:174
  70.0 13.9 %collective-permute-start.5 = (bf16[32,1344]{1,0:T(8,128)(2,1)S(1)}, bf16[32,1344]{1,0:T(8,128)(2,1)S(1)}, u32[]{:S(2)}, u32[]{:S(2)}) collective-permute-start(bf16[32,1344]{1,0:T(8,128)(2,1)S(1)} %get-tuple-element.25), channel_id=1, source_target_pairs={{0,32},{1,97},{2,34},{3,99},{4,36},{5,101},{6,38},{7,103},{8,40},{... | collective-permute-start | bytes 258056 | tf_op jit(solution)/shard_map/ppermute | solution.py:174
  71.9 12.0 %collective-permute-start.6 = (bf16[32,1344]{1,0:T(8,128)(2,1)S(1)}, bf16[32,1344]{1,0:T(8,128)(2,1)S(1)}, u32[]{:S(2)}, u32[]{:S(2)}) collective-permute-start(bf16[32,1344]{1,0:T(8,128)(2,1)S(1)} %get-tuple-element.26), channel_id=1, source_target_pairs={{0,96},{1,33},{2,98},{3,35},{4,100},{5,37},{6,102},{7,39},{8,104},... | collective-permute-start | bytes 258056 | tf_op jit(solution)/shard_map/ppermute | solution.py:174
  107.3 10.8 %collective-permute-start.7 = (bf16[128,1344]{1,0:T(8,128)(2,1)S(1)}, bf16[128,1344]{1,0:T(8,128)(2,1)S(1)}, u32[]{:S(2)}, u32[]{:S(2)}) collective-permute-start(bf16[128,1344]{1,0:T(8,128)(2,1)S(1)} %all_gather.3.c0), channel_id=1, source_target_pairs={{0,16},{1,113},{2,18},{3,115},{4,20},{5,117},{6,22},{7,119},{8,24}... | collective-permute-start | bytes 1032200 | tf_op jit(solution)/shard_map/ppermute | solution.py:174
  110.2 17.7 %collective-permute-start.8 = (bf16[128,1344]{1,0:T(8,128)(2,1)S(1)}, bf16[128,1344]{1,0:T(8,128)(2,1)S(1)}, u32[]{:S(2)}, u32[]{:S(2)}) collective-permute-start(bf16[128,1344]{1,0:T(8,128)(2,1)S(1)} %all_gather.3.c0), channel_id=1, source_target_pairs={{0,120},{1,9},{2,122},{3,11},{4,124},{5,13},{6,126},{7,15},{8,0},{... | collective-permute-start | bytes 1032200 | tf_op jit(solution)/shard_map/ppermute | solution.py:174
  116.1 12.1 %collective-permute-start.9 = (bf16[128,1344]{1,0:T(8,128)(2,1)S(1)}, bf16[128,1344]{1,0:T(8,128)(2,1)S(1)}, u32[]{:S(2)}, u32[]{:S(2)}) collective-permute-start(bf16[128,1344]{1,0:T(8,128)(2,1)S(1)} %all_gather.3.c0), channel_id=1, source_target_pairs={{0,8},{1,121},{2,10},{3,123},{4,12},{5,125},{6,14},{7,127},{8,16},... | collective-permute-start | bytes 1032200 | tf_op jit(solution)/shard_map/ppermute | solution.py:174
  129.4 6.4 %collective-permute-start.10 = (bf16[16,16,1024]{2,1,0:T(8,128)(2,1)S(1)}, bf16[16,16,1024]{2,1,0:T(8,128)(2,1)S(1)}, u32[]{:S(2)}, u32[]{:S(2)}) collective-permute-start(bf16[16,16,1024]{2,1,0:T(8,128)(2,1)S(1)} %shard_map.106), channel_id=1, source_target_pairs={{0,1},{1,0},{2,3},{3,2},{4,5},{5,4},{6,7},{7,6},{8,9},{9,8},{10,11... | collective-permute-start | bytes 1572872 | tf_op jit(solution)/shard_map/ppermute | solution.py:188
  136.7 13.8 %all-to-all-start.1 = ((bf16[16,16,1024]{2,1,0:T(8,128)(2,1)}), bf16[16,16,1024]{2,1,0:T(8,128)(2,1)S(1)}, u32[]{:S(2)}, u32[]{:S(2)}) async-start(bf16[16,16,1024]{2,1,0:T(8,128)(2,1)} %shard_map.107), calls=%async_computation.1 | async-start | bytes 1048576 | tf_op jit(solution)/shard_map/all_to_all | solution.py:191
  140.3 1.2 copy-start.2

commit v4 on v3

--- a/solution.py
+++ b/solution.py
@@ -12,6 +12,7 @@
 F32 = jnp.float32
 GROUP = ("row", "depth")
 NEAR = (0, -1, 1, 2)
+ORDER = [(peer, step) for peer in range(4) for step in range(4)]
 
 
 def nt(left, right):
@@ -28,7 +29,7 @@
 
 def call(body, out_shapes, n_scalar, n_array, scratch=(), mib=8, outside=(), outside_out=()):
     def place(at, away):
-        return pl.BlockSpec(memory_space=pl.ANY if at in away else pltpu.VMEM)
+        return pl.BlockSpec(memory_space=pltpu.HBM if at in away else pltpu.VMEM)
 
     return pl.pallas_call(
         body,
@@ -47,51 +48,44 @@
 
 def decoded(x):
     wide = x.astype(F32)
-    root = jnp.sqrt(jnp.abs(wide))
-    return jnp.where(wide < 0, -root, root)
-
-
-def spread(tokens, cotangent, out, both, sems):
-    width = tokens.shape[1]
-    left = pltpu.make_async_copy(tokens, both.at[:, :width], sems.at[0])
-    right = pltpu.make_async_copy(cotangent, both.at[:, width:], sems.at[1])
-    left.start()
-    right.start()
-    left.wait()
-    right.wait()
+    return wide * lax.rsqrt(jnp.abs(wide) + 1e-36)
+
+
+def spread(both, out):
     for at in range(out.shape[0]):
         out[at] = both[...]
+
+
+def gather_rows(index, mine, other, ordered, slots):
+    rows = mine.shape[1]
+    for at, slot in enumerate(slots):
+        ordered[2 * at * rows : (2 * at + 1) * rows, :] = mine[index[slot]]
+        ordered[(2 * at + 1) * rows : (2 * at + 2) * rows, :] = other[index[slot]]
 
 
 def partial_sums(index, mine, other, pair, down, third, first, second, own, kept, ordered, sems):
     width = pair.shape[1]
     both = pair.shape[0]
-    rows = mine.shape[1]
-    chunk = 2 * rows
-    block = 4 * chunk
-    copies = []
-    for at, out in ((3, third), (1, first), (2, second), (0, own)):
-        for j in range(4):
-            slot = at * 4 + j
-            ordered[slot * chunk : slot * chunk + rows, :] = mine[index[slot]]
-            ordered[slot * chunk + rows : (slot + 1) * chunk, :] = other[index[slot]]
-        here = pl.ds(at * block, block)
-        copies.append(pltpu.make_async_copy(ordered.at[here], kept.at[here], sems.at[at]))
-        copies[-1].start()
-        block_rows = ordered[at * block : (at + 1) * block, :]
-        gate_up = nt(block_rows[:, :width], pair[...])
-        cot = nt(block_rows[:, width:], down[...])
-        out[:, 0:both] = gate_up if at == 0 else coded(gate_up)
-        out[:, both:] = cot if at == 0 else coded(cot)
-    for copy in copies:
-        copy.wait()
-
-
-def near_sum(place, own, third, first, second, far, near, back, keep):
+    block = own.shape[0]
+    gather_rows(index, mine, other, ordered, range(16))
+    copy = pltpu.make_async_copy(ordered, kept, sems.at[0])
+    copy.start()
+    gate_up = nt(ordered[:, :width], pair[...])
+    cot = nt(ordered[:, width:], down[...])
+    own[:, :both] = gate_up[:block, :]
+    own[:, both:] = cot[:block, :]
+    for at, out in ((3, third), (1, first), (2, second)):
+        rows = slice(at * block, (at + 1) * block)
+        out[:, :both] = coded(gate_up[rows, :])
+        out[:, both:] = coded(cot[rows, :])
+    copy.wait()
+
+
+def near_sum(own, third, first, second, far, near, back, keep):
     chunk = keep.shape[0]
 
     def total(at):
-        rows = pl.ds(pl.multiple_of(place[at] * chunk, chunk), chunk)
+        rows = slice(at * chunk, (at + 1) * chunk)
         return own[rows, :] + (decoded(first[rows, :]) + decoded(second[rows, :]) + decoded(third[rows, :]))
 
     far[...] = coded(total(2))
@@ -134,12 +128,14 @@
     out[...] = (keep[...] + arrived[...].astype(F32)).astype(BF)
 
 
-def weight_grads(c0, c1, c2, c3, ordered, gate_g, up_g, down_g, allc):
+def weight_grads(place, c0, c1, c2, c3, ordered, gate_g, up_g, down_g, allc):
     ff, width = gate_g.shape
-    block = c0.shape[0]
+    chunk = c0.shape[0] // 4
     scale = 1.0 / math.sqrt(ordered.shape[0])
     for at, c in enumerate((c0, c1, c2, c3)):
-        allc[at * block : (at + 1) * block, :] = c[...]
+        for slot in [i for i, (peer, _) in enumerate(ORDER) if peer == at]:
+            rows = pl.ds(pl.multiple_of(place[slot] * chunk, chunk), chunk)
+            allc[slot * chunk : (slot + 1) * chunk, :] = c[rows, :]
     both = tn(allc[:, : 2 * ff], ordered[:, :width]) * scale
     gate_g[...] = both[:ff, :].astype(BF)
     up_g[...] = both[ff:, :].astype(BF)
@@ -175,10 +171,14 @@
 
     z = lax.axis_index("col")
     sign = 1 - 2 * (lax.axis_index("depth") % 2)
-    four = jnp.arange(4, dtype=jnp.int32)
-    classes = (z - sign * jnp.array(NEAR, jnp.int32) + 16) % 4
-    index = (classes[:, None] + 4 * four[None, :]).reshape(16).astype(jnp.int32)
-    place = ((z // 4 + sign * four + 4) % 4).astype(jnp.int32)
+    peer_of = jnp.array([NEAR[peer] for peer, _ in ORDER], jnp.int32)
+    step_of = jnp.array([step for _, step in ORDER], jnp.int32)
+    peers = (z - sign * peer_of + 16) % 16
+    place = (peers // 4 + sign * step_of + 4) % 4
+    index = 4 * place + peers % 4
+    row_of = jnp.array([at % 4 for at in range(16)], jnp.int32)
+    near_of = jnp.array([NEAR[at // 4] for at in range(16)], jnp.int32)
+    by_row = 4 * row_of + (z - sign * near_of + 16) % 4
 
     cores = 2
     chips = ranks // cores
@@ -190,14 +190,8 @@
     def exchange(x):
         return lax.all_to_all(x, GROUP, 0, 0, tiled=True, axis_index_groups=same_core)
 
-    (sent,) = call(
-        spread,
-        [((chips, rows, 2 * width), BF)],
-        0,
-        2,
-        [pltpu.VMEM((rows, 2 * width), BF), pltpu.SemaphoreType.DMA((2,))],
-        outside=(0, 1),
-    )(tokens, cotangent)
+    both = jnp.concatenate([tokens, cotangent], axis=1)
+    (sent,) = call(spread, [((chips, rows, 2 * width), BF)], 0, 1)(both)
     mine = exchange(sent)
     other = swap(mine)
     pair = jnp.concatenate([gate_weight.T, up_weight.T], axis=0)
@@ -206,16 +200,16 @@
         [((block, wide), BF)] * 3 + [((block, wide), F32), ((total, 2 * width), BF)],
         1,
         4,
-        [pltpu.VMEM((total, 2 * width), BF), pltpu.SemaphoreType.DMA((4,))],
-        mib=12,
+        [pltpu.VMEM((total, 2 * width), BF), pltpu.SemaphoreType.DMA((1,))],
+        mib=16,
         outside_out=(4,),
     )(index, mine, other, pair, down_weight)
     third = shift(third, -NEAR[3])
     first = shift(first, -NEAR[1])
     second = shift(second, -NEAR[2])
     far, near, back, keep = call(
-        near_sum, [((chunk, wide), BF)] * 3 + [((chunk, wide), F32)], 1, 4
-    )(place, own, third, first, second)
+        near_sum, [((chunk, wide), BF)] * 3 + [((chunk, wide), F32)], 0, 4
+    )(own, third, first, second)
     far = shift(far, 8)
     near = shift(near, 4)
     back = shift(back, -4)
@@ -232,15 +226,15 @@
             1,
             6,
             [pltpu.VMEM((total // cores, wide), BF)],
-        )(index, c3, c1, c2, c0, pair, down_weight)[0]
+        )(by_row, c3, c1, c2, c0, pair, down_weight)[0]
 
     arrived = swap(half_out(1, BF))
     (summed,) = call(core_sum, [((chips, rows, 2 * width), BF)], 0, 2)(half_out(0, F32), arrived)
     parts = exchange(summed)
     layer_out, tokens_grad = call(last_sum, [((rows, width), BF)] * 2, 0, 1)(parts)
     gate_g, up_g, down_g = call(
-        weight_grads, [((ff, width), BF)] * 3, 0, 5, [pltpu.VMEM((total, wide), BF)], mib=12
-    )(c0, c1, c2, c3, ordered)
+        weight_grads, [((ff, width), BF)] * 3, 1, 5, [pltpu.VMEM((total, wide), BF)], mib=12
+    )(place, c0, c1, c2, c3, ordered)
     return (layer_out, tokens_grad, gate_g.T, up_g.T, down_g)
 
 

time: 152 us -> 146 us (0.961)
  local copies, waits for them, and re-layouts: 3.76 us -> 0.04 us
  waiting for transfers between devices: 44.5 us -> 47.6 us
  Pallas kernels: 12.1 us -> 9.37 us
    unnamed x14 -> x12, local copies, waits for them, and re-layouts: 3.68 us -> 0.04 us
    pallas_call x1, Pallas kernels: 3.95 us -> 1.73 us  [shards(): call(partial_sums, [((block, wide), BF)] * 3 + [((block, wide), F32), ((t...]
  transfers between devices with their start and end apart: 13 -> 13, of which waited for: 10 -> 11; matrix products, arithmetic and copies ran while one was open for 1% -> 0% of each run, Pallas kernels for 2% -> 2%
where the time goes in v4:
time: 146 us; the launch traced here: 145 us
  starting transfers between devices  64.1 us (44%)
  waiting for transfers between devices  47.6 us (33%)
  blocking collectives  22.1 us (15%)
  Pallas kernels  9.37 us (6%)
    ppermute x9, starting transfers between devices, shift(): return lax.ppermute(x, ('col', 'depth'), pairs)  42.3 us
    ppermute x9, waiting for transfers between devices, shift(): return lax.ppermute(x, ('col', 'depth'), pairs)  28.8 us
    all_gather x1, blocking collectives, shards(): lax.all_gather(act, 'col', axis=0, tiled=True, axis_index_groups=strided)  22.1 us
    all_to_all x2, waiting for transfers between devices, exchange(): lax.all_to_all(x, GROUP, 0, 0, tiled=True, axis_index_groups=same_core)  17.1 us
    all_to_all x2, starting transfers between devices, exchange(): lax.all_to_all(x, GROUP, 0, 0, tiled=True, axis_index_groups=same_core)  11.5 us
    ppermute x2, starting transfers between devices, swap(): return lax.ppermute(x, 'depth', [(d, d ^ 1) for d in range(depth)])  10.4 us
  transfers between devices with their start and end apart: 13, of which 11 were waited for; matrix products, arithmetic and copies ran while one was open for 0% of the time, Pallas kernels for 2%

profile of v4, /device:TPU:1, one launch (start us, length us, event | category | flops | bytes accessed | tf_op | source)
XLA Modules:
  0.0 145.0 jit_solution(4933309737716534655)
XLA Ops:
  0.6 0.0 copy-start.1
  0.6 0.0 copy-start.2
  0.7 0.8 pad_maximum_fusion.1.both
  1.5 0.8 shard_map.128
  2.3 7.6 %all-to-all-start = ((bf16[16,16,1024]{2,1,0:T(8,128)(2,1)}), bf16[16,16,1024]{2,1,0:T(8,128)(2,1)S(1)}, u32[]{:S(2)}, u32[]{:S(2)}) async-start(bf16[16,16,1024]{2,1,0:T(8,128)(2,1)} %shard_map.128), calls=%async_computation | async-start | bytes 1048576 | tf_op jit(solution)/shard_map/all_to_all | solution.py:191
  9.9 0.0 copy-start.4
  9.9 0.0 copy-start.5
  9.9 0.0 copy-start.3
  9.9 0.0 copy-start
  10.0 9.0 %all-to-all-done.mine = bf16[16,16,1024]{2,1,0:T(8,128)(2,1)S(1)} async-done(((bf16[16,16,1024]{2,1,0:T(8,128)(2,1)}), bf16[16,16,1024]{2,1,0:T(8,128)(2,1)S(1)}, u32[]{:S(2)}, u32[]{:S(2)}) %all-to-all-start) | async-done | bytes 524320 | tf_op jit(solution)/shard_map/all_to_all | solution.py:191
  19.0 5.8 %collective-permute-start = (bf16[16,16,1024]{2,1,0:T(8,128)(2,1)S(1)}, bf16[16,16,1024]{2,1,0:T(8,128)(2,1)S(1)}, u32[]{:S(2)}, u32[]{:S(2)}) collective-permute-start(bf16[16,16,1024]{2,1,0:T(8,128)(2,1)S(1)} %all-to-all-done.mine), channel_id=1, source_target_pairs={{0,1},{1,0},{2,3},{3,2},{4,5},{5,4},{6,7},{7,6},{8,9},{9,8},{10,11... | collective-permute-start | bytes 1572872 | tf_op jit(solution)/shard_map/ppermute | solution.py:188
  24.7 0.0 copy-done.1
  24.7 0.0 copy-done.2
  24.7 0.1 pad_maximum_fusion.pair
  24.8 0.0 copy-done.4
  24.8 0.0 copy-done.5
  24.9 0.0 copy-done.3
  24.9 1.3 collective-permute-done.other
  26.2 0.0 copy-done
  26.2 1.7 %shard_map.129 = (bf16[128,1344]{1,0:T(8,128)(2,1)S(1)}, bf16[128,1344]{1,0:T(8,128)(2,1)S(1)}, bf16[128,1344]{1,0:T(8,128)(2,1)S(1)}, f32[128,1344]{1,0:T(8,128)S(1)}, bf16[512,1024]{1,0:T(8,128)(2,1)S(1)}) custom-call(s32[16]{0:T(128)S(1)} %get-tuple-element.33.index, bf16[16,16,1024]{2,1,0:T(8,128)(2,1)S(1)} %all-to-all-done.mine, ...), custom_call_target="tpu_custom_call" | custom-call | tf_op jit(solution)/shard_map/pallas_call | solution.py:198
  28.0 4.4 %collective-permute-start.1 = (bf16[128,1344]{1,0:T(8,128)(2,1)S(1)}, bf16[128,1344]{1,0:T(8,128)(2,1)S(1)}, u32[]{:S(2)}, u32[]{:S(2)}) collective-permute-start(bf16[128,1344]{1,0:T(8,128)(2,1)S(1)} %get-tuple-element.20), channel_id=1, source_target_pairs={{0,112},{1,17},{2,114},{3,19},{4,116},{5,21},{6,118},{7,23},{8,120... | collective-permute-start | bytes 1032200 | tf_op jit(solution)/shard_map/ppermute | solution.py:170
  32.4 8.1 %collective-permute-start.2 = (bf16[128,1344]{1,0:T(8,128)(2,1)S(1)}, bf16[128,1344]{1,0:T(8,128)(2,1)S(1)}, u32[]{:S(2)}, u32[]{:S(2)}) collective-permute-start(bf16[128,1344]{1,0:T(8,128)(2,1)S(1)} %get-tuple-element.21), channel_id=1, source_target_pairs={{0,8},{1,121},{2,10},{3,123},{4,12},{5,125},{6,14},{7,127},{8,16},... | collective-permute-start | bytes 1032200 | tf_op jit(solution)/shard_map/ppermute | solution.py:170
  40.6 1.9 %collective-permute-start.3 = (bf16[128,1344]{1,0:T(8,128)(2,1)S(1)}, bf16[128,1344]{1,0:T(8,128)(2,1)S(1)}, u32[]{:S(2)}, u32[]{:S(2)}) collective-permute-start(bf16[128,1344]{1,0:T(8,128)(2,1)S(1)} %get-tuple-element.22), channel_id=1, source_target_pairs={{0,120},{1,9},{2,122},{3,11},{4,124},{5,13},{6,126},{7,15},{8,0},{... | collective-permute-start | bytes 1032200 | tf_op jit(solution)/shard_map/ppermute | solution.py:170
  42.5 3.0 %collective-permute-done.1.third = bf16[128,1344]{1,0:T(8,128)(2,1)S(1)} collective-permute-done((bf16[128,1344]{1,0:T(8,128)(2,1)S(1)}, bf16[128,1344]{1,0:T(8,128)(2,1)S(1)}, u32[]{:S(2)}, u32[]{:S(2)}) %collective-permute-start.1) | collective-permute-done | bytes 344096 | tf_op jit(solution)/shard_map/ppermute | solution.py:170
  45.5 7.1 %collective-permute-done.2.first = bf16[128,1344]{1,0:T(8,128)(2,1)S(1)} collective-permute-done((bf16[128,1344]{1,0:T(8,128)(2,1)S(1)}, bf16[128,1344]{1,0:T(8,128)(2,1)S(1)}, u32[]{:S(2)}, u32[]{:S(2)}) %collective-permute-start.2) | collective-permute-done | bytes 344096 | tf_op jit(solution)/shard_map/ppermute | solution.py:170
  52.6 2.5 %collective-permute-done.3.second = bf16[128,1344]{1,0:T(8,128)(2,1)S(1)} collective-permute-done((bf16[128,1344]{1,0:T(8,128)(2,1)S(1)}, bf16[128,1344]{1,0:T(8,128)(2,1)S(1)}, u32[]{:S(2)}, u32[]{:S(2)}) %collective-permute-start.3) | collective-permute-done | bytes 344096 | tf_op jit(solution)/shard_map/ppermute | solution.py:170
  55.0 0.5 shard_map.130
  55.5 9.4 %collective-permute-start.4 = (bf16[32,1344]{1,0:T(8,128)(2,1)S(1)}, bf16[32,1344]{1,0:T(8,128)(2,1)S(1)}, u32[]{:S(2)}, u32[]{:S(2)}) collective-permute-start(bf16[32,1344]{1,0:T(8,128)(2,1)S(1)} %get-tuple-element.24), channel_id=1, source_target_pairs={{0,64},{1,65},{2,66},{3,67},{4,68},{5,69},{6,70},{7,71},{8,72},{9,... | collective-permute-start | bytes 258056 | tf_op jit(solution)/shard_map/ppermute | solution.py:170
  64.8 1.9 %collective-permute-start.5 = (bf16[32,1344]{1,0:T(8,128)(2,1)S(1)}, bf16[32,1344]{1,0:T(8,128)(2,1)S(1)}, u32[]{:S(2)}, u32[]{:S(2)}) collective-permute-start(bf16[32,1344]{1,0:T(8,128)(2,1)S(1)} %get-tuple-element.25), channel_id=1, source_target_pairs={{0,32},{1,97},{2,34},{3,99},{4,36},{5,101},{6,38},{7,103},{8,40},{... | collective-permute-start | bytes 258056 | tf_op jit(solution)/shard_map/ppermute | solution.py:170
  66.8 7.3 %collective-permute-start.6 = (bf16[32,1344]{1,0:T(8,128)(2,1)S(1)}, bf16[32,1344]{1,0:T(8,128)(2,1)S(1)}, u32[]{:S(2)}, u32[]{:S(2)}) collective-permute-start(bf16[32,1344]{1,0:T(8,128)(2,1)S(1)} %get-tuple-element.26), channel_id=1, source_target_pairs={{0,96},{1,33},{2,98},{3,35},{4,100},{5,37},{6,102},{7,39},{8,104},... | collective-permute-start | bytes 258056 | tf_op jit(solution)/shard_map/ppermute | solution.py:170
  74.1 0.0 collective-permute-done.4.far
  74.1 4.6 %collective-permute-done.5.near = bf16[32,1344]{1,0:T(8,128)(2,1)S(1)} collective-permute-done((bf16[32,1344]{1,0:T(8,128)(2,1)S(1)}, bf16[32,1344]{1,0:T(8,128)(2,1)S(1)}, u32[]{:S(2)}, u32[]{:S(2)}) %collective-permute-start.5) | collective-permute-done | bytes 86048 | tf_op jit(solution)/shard_map/ppermute | solution.py:170
  78.7 0.0 collective-permute-done.6.back
  78.7 0.2 shard_map.131
  78.9 22.1 %all_gather.3.c0 = bf16[128,1344]{1,0:T(8,128)(2,1)S(1)} all-gather(bf16[32,1344]{1,0:T(8,128)(2,1)S(1)} %shard_map.131), channel_id=1, replica_groups={{0,32,64,96},{8,40,72,104},{16,48,80,112},{24,56,88,120},{1,33,65,97},{..., dimensions={0}, use_global_device_ids=true | all-gather | bytes 430080 | tf_op jit(solution)/shard_map/all_gather | solution.py:218
  101.0 2.0 %collective-permute-start.7 = (bf16[128,1344]{1,0:T(8,128)(2,1)S(1)}, bf16[128,1344]{1,0:T(8,128)(2,1)S(1)}, u32[]{:S(2)}, u32[]{:S(2)}) collective-permute-start(bf16[128,1344]{1,0:T(8,128)(2,1)S(1)} %all_gather.3.c0), channel_id=1, source_target_pairs={{0,16},{1,113},{2,18},{3,115},{4,20},{5,117},{6,22},{7,119},{8,24}... | collective-permute-start | bytes 1032200 | tf_op jit(solution)/shard_map/ppermute | solution.py:170
  103.0 5.4 %collective-permute-start.8 = (bf16[128,1344]{1,0:T(8,128)(2,1)S(1)}, bf16[128,1344]{1,0:T(8,128)(2,1)S(1)}, u32[]{:S(2)}, u32[]{:S(2)}) collective-permute-start(bf16[128,1344]{1,0:T(8,128)(2,1)S(1)} %all_gather.3.c0), channel_id=1, source_target_pairs={{0,120},{1,9},{2,122},{3,11},{4,124},{5,13},{6,126},{7,15},{8,0},{... | collective-permute-start | bytes 1032200 | tf_op jit(solution)/shard_map/ppermute | solution.py:170
  108.4 1.9 %collective-permute-start.9 = (bf16[128,1344]{1,0:T(8,128)(2,1)S(1)}, bf16[128,1344]{1,0:T(8,128)(2,1)S(1)}, u32[]{:S(2)}, u32[]{:S(2)}) collective-permute-start(bf16[128,1344]{1,0:T(8,128)(2,1)S(1)} %all_gather.3.c0), channel_id=1, source_target_pairs={{0,8},{1,121},{2,10},{3,123},{4,12},{5,125},{6,14},{7,127},{8,16},... | collective-permute-start | bytes 1032200 | tf_op jit(solution)/shard_map/ppermute | solution.py:170
  110.3 1.0 collective-permute-done.7.c3
  111.4 9.2 %collective-permute-done.8.c1 = bf16[128,1344]{1,0:T(8,128)(2,1)S(1)} collective-permute-done((bf16[128,1344]{1,0:T(8,128)(2,1)S(1)}, bf16[128,1344]{1,0:T(8,128)(2,1)S(1)}, u32[]{:S(2)}, u32[]{:S(2)}) %collective-permute-start.8) | collective-permute-done | bytes 344096 | tf_op jit(solution)/shard_map/ppermute | solution.py:170
  120.5 1.4 collective-permute-done.9.c2
  121.9 1.1 shard_map.133
  123.1 4.6 %collective-permute-start.10 = (bf16[16,16,1024]{2,1,0:T(8,128)(2,1)S(1)}, bf16[16,16,1024]{2,1,0:T(8,128)(2,1)S(1)}, u32[]{:S(2)}, u32[]{:S(2)}) collective-permute-start(bf16[16,16,1024]{2,1,0:T(8,128)(2,1)S(1)} %shard_map.133), channel_id=1, source_target_pairs={{0,1},{1,0},{2,3},{3,2},{4,5},{5,4},{6,7},{7,6},{8,9},{9,8},{10,11... | collective-permute-start | bytes 1572872 | tf_op jit(solution)/shard_map/ppermute | solution.py:188
  127.7 1.1 shard_map.132.keep
  128.8 0.4 collective-permute-done.10.arrived
  129.2 0.9 shard_map.134
  130.1 3.9 %all-to-all-start.1 = ((bf16[16,16,1024]{2,1,0:T(8,128)(2,1)}), bf16[16,16,1024]{2,1,0:T(8,128)(2,1)S(1)}, u32[]{:S(2)}, u32[]{:S(2)}) async-start(bf16[16,16,1024]{2,1,0:T(8,128)(2,1)} %shard_map.134), calls=%async_computation.1 | async-start | bytes 1048576 | tf_op jit(solution)/shard_map/all_to_all | solution.py:191
  134.0 2.3 %shard_map.136 = (bf16[448,512]{1,0:T(8,128)(2,1)}, bf16[448,512]{1,0:T(8,128)(2,1)}, bf16[448,512]{1,0:T(8,128)(2,1)}) custom-call(s32[16]{0:T(128)S(1)} %get-tuple-element.34.place, bf16[128,1344]{1,0:T(8,128)(2,1)S(1)} %all_gather.3.c0, bf16[128,1344]{1,0:T(8,128)(2,1)S(1)} %collective-permute-done.8.c1, bf16[128,1344]{1,0:T(8,128)(2,1)S(1)} %collective-permute-done.9.c2, ...), custom_call_target="tpu_custom_call" | custom-call | tf_op jit(solution)/shard_map/pallas_call | solution.py:235
  136.3 8.1 %all-to-all-done.1.parts = bf16[16,16,1024]{2,1,0:T(8,128)(2,1)S(1)} async-done(((bf16[16,16,1024]{2,1,0:T(8,128)(2,1)}), bf16[16,16,1024]{2,1,0:T(8,128)(2,1)S(1)}, u32[]{:S(2)}, u32[]{:S(2)}) %all-to-all-start.1) | async-done | bytes 524320 | tf_op jit(solution)/shard_map/all_to_all | solution.py:191
  144.4 0.7 shard_map.135
  (2 shorter events, 0.0 us)
Async XLA Ops:
  0.6 24.1 %copy-start.1 = (bf16[512,448]{0,1:T(8,128)(2,1)S(1)}, bf16[512,448]{0,1:T(8,128)(2,1)}, u32[]{:S(2)}) copy-start(bf16[512,448]{0,1:T(8,128)(2,1)} %param.12) | copy-start | bytes 1376260
  0.6 24.1 %copy-start.2 = (bf16[512,448]{0,1:T(8,128)(2,1)S(1)}, bf16[512,448]{0,1:T(8,128)(2,1)}, u32[]{:S(2)}) copy-start(bf16[512,448]{0,1:T(8,128)(2,1)} %param.11) | copy-start | bytes 1376260
  2.3 16.7 %all-to-all-start = ((bf16[16,16,1024]{2,1,0:T(8,128)(2,1)}), bf16[16,16,1024]{2,1,0:T(8,128)(2,1)S(1)}, u32[]{:S(2)}, u32[]{:S(2)}) async-start(bf16[16,16,1024]{2,1,0:T(8,128)(2,1)} %shard_map.128), calls=%async_computation | async-start | bytes 1048576 | tf_op jit(solution)/shard_map/all_to_all | solution.py:191
  9.9 14.9 %copy-start.4 = (s32[16]{0:T(128)S(1)}, s32[16]{0:T(128)}, u32[]{:S(2)}) copy-start(s32[16]{0:T(128)} %constant.75.clone) | copy-start | bytes 196
  9.9 14.9 %copy-start.5 = (s32[16]{0:T(128)S(1)}, s32[16]{0:T(128)}, u32[]{:S(2)}) copy-start(s32[16]{0:T(128)} %constant.79) | copy-start | bytes 196
  9.9 14.9 %copy-start.3 = (s32[16]{0:T(128)S(1)}, s32[16]{0:T(128)}, u32[]{:S(2)}) copy-start(s32[16]{0:T(128)} %constant.76.clone) | copy-start | bytes 196
  9.9 16.3 %copy-start = (bf16[448,512]{1,0:T(8,128)(2,1)S(1)}, bf16[448,512]{1,0:T(8,128)(2,1)}, u32[]{:S(2)}) copy-start(bf16[448,512]{1,0:T(8,128)(2,1)} %down.5) | copy-start | bytes 1376260
  19.0 7.3 %collective-permute-start = (bf16[16,16,1024]{2,1,0:T(8,128)(2,1)S(1)}, bf16[16,16,1024]{2,1,0:T(8,128)(2,1)S(1)}, u32[]{:S(2)}, u32[]{:S(2)}) collective-permute-start(bf16[16,16,1024]{2,1,0:T(8,128)(2,1)S(1)} %all-to-all-done.mine), channel_id=1, source_target_pairs={{0,1},{1,0},{2,3},{3,2},{4,5},{5,4},{6,7},{7,6},{8,9},{9,8},{10,11... | collective-permute-start | bytes 1572872 | tf_op jit(solution)/shard_map/ppermute | solution.py:188
  28.0 17.5 %collective-permute-start.1 = (bf16[128,1344]{1,0:T(8,128)(2,1)S(1)}, bf16[128,1344]{1,0:T(8,128)(2,1)S(1)}, u32[]{:S(2)}, u32[]{:S(2)}) collective-permute-start(bf16[128,1344]{1,0:T(8,128)(2,1)S(1)} %get-tuple-element.20), channel_id=1, source_target_pairs={{0,112},{1,17},{2,114},{3,19},{4,116},{5,21},{6,118},{7,23},{8,120... | collective-permute-start | bytes 1032200 | tf_op jit(solution)/shard_map/ppermute | solution.py:170
  32.4 20.1 %collective-permute-start.2 = (bf16[128,1344]{1,0:T(8,128)(2,1)S(1)}, bf16[128,1344]{1,0:T(8,128)(2,1)S(1)}, u32[]{:S(2)}, u32[]{:S(2)}) collective-permute-start(bf16[128,1344]{1,0:T(8,128)(2,1)S(1)} %get-tuple-element.21), channel_id=1, source_target_pairs={{0,8},{1,121},{2,10},{3,123},{4,12},{5,125},{6,14},{7,127},{8,16},... | collective-permute-start | bytes 1032200 | tf_op jit(solution)/shard_map/ppermute | solution.py:170
  40.6 14.5 %collective-permute-start.3 = (bf16[128,1344]{1,0:T(8,128)(2,1)S(1)}, bf16[128,1344]{1,0:T(8,128)(2,1)S(1)}, u32[]{:S(2)}, u32[]{:S(2)}) collective-permute-start(bf16[128,1344]{1,0:T(8,128)(2,1)S(1)} %get-tuple-element.22), channel_id=1, source_target_pairs={{0,120},{1,9},{2,122},{3,11},{4,124},{5,13},{6,126},{7,15},{8,0},{... | collective-permute-start | bytes 1032200 | tf_op jit(solution)/shard_map/ppermute | solution.py:170
  55.5 18.6 %collective-permute-start.4 = (bf16[32,1344]{1,0:T(8,128)(2,1)S(1)}, bf16[32,1344]{1,0:T(8,128)(2,1)S(1)}, u32[]{:S(2)}, u32[]{:S(2)}) collective-permute-start(bf16[32,1344]{1,0:T(8,128)(2,1)S(1)} %get-tuple-element.24), channel_id=1, source_target_pairs={{0,64},{1,65},{2,66},{3,67},{4,68},{5,69},{6,70},{7,71},{8,72},{9,... | collective-permute-start | bytes 258056 | tf_op jit(solution)/shard_map/ppermute | solution.py:170
  64.8 13.9 %collective-permute-start.5 = (bf16[32,1344]{1,0:T(8,128)(2,1)S(1)}, bf16[32,1344]{1,0:T(8,128)(2,1)S(1)}, u32[]{:S(2)}, u32[]{:S(2)}) collective-permute-start(bf16[32,1344]{1,0:T(8,128)(2,1)S(1)} %get-tuple-element.25), channel_id=1, source_target_pairs={{0,32},{1,97},{2,34},{3,99},{4,36},{5,101},{6,38},{7,103},{8,40},{... | collective-permute-start | bytes 258056 | tf_op jit(solution)/shard_map/ppermute | solution.py:170
  66.8 11.9 %collective-permute-start.6 = (bf16[32,1344]{1,0:T(8,128)(2,1)S(1)}, bf16[32,1344]{1,0:T(8,128)(2,1)S(1)}, u32[]{:S(2)}, u32[]{:S(2)}) collective-permute-start(bf16[32,1344]{1,0:T(8,128)(2,1)S(1)} %get-tuple-element.26), channel_id=1, source_target_pairs={{0,96},{1,33},{2,98},{3,35},{4,100},{5,37},{6,102},{7,39},{8,104},... | collective-permute-start | bytes 258056 | tf_op jit(solution)/shard_map/ppermute | solution.py:170
  101.0 10.3 %collective-permute-start.7 = (bf16[128,1344]{1,0:T(8,128)(2,1)S(1)}, bf16[128,1344]{1,0:T(8,128)(2,1)S(1)}, u32[]{:S(2)}, u32[]{:S(2)}) collective-permute-start(bf16[128,1344]{1,0:T(8,128)(2,1)S(1)} %all_gather.3.c0), channel_id=1, source_target_pairs={{0,16},{1,113},{2,18},{3,115},{4,20},{5,117},{6,22},{7,119},{8,24}... | collective-permute-start | bytes 1032200 | tf_op jit(solution)/shard_map/ppermute | solution.py:170
  103.0 17.5 %collective-permute-start.8 = (bf16[128,1344]{1,0:T(8,128)(2,1)S(1)}, bf16[128,1344]{1,0:T(8,128)(2,1)S(1)}, u32[]{:S(2)}, u32[]{:S(2)}) collective-permute-start(bf16[128,1344]{1,0:T(8,128)(2,1)S(1)} %all_gather.3.c0), channel_id=1, source_target_pairs={{0,120},{1,9},{2,122},{3,11},{4,124},{5,13},{6,126},{7,15},{8,0},{... | collective-permute-start | bytes 1032200 | tf_op jit(solution)/shard_map/ppermute | solution.py:170
  108.4 13.6 %collective-permute-start.9 = (bf16[128,1344]{1,0:T(8,128)(2,1)S(1)}, bf16[128,1344]{1,0:T(8,128)(2,1)S(1)}, u32[]{:S(2)}, u32[]{:S(2)}) collective-permute-start(bf16[128,1344]{1,0:T(8,128)(2,1)S(1)} %all_gather.3.c0), channel_id=1, source_target_pairs={{0,8},{1,121},{2,10},{3,123},{4,12},{5,125},{6,14},{7,127},{8,16},... | collective-permute-start | bytes 1032200 | tf_op jit(solution)/shard_map/ppermute | solution.py:170
  123.1 6.1 %collective-permute-start.10 = (bf16[16,16,1024]{2,1,0:T(8,128)(2,1)S(1)}, bf16[16,16,1024]{2,1,0:T(8,128)(2,1)S(1)}, u32[]{:S(2)}, u32[]{:S(2)}) collective-permute-start(bf16[16,16,1024]{2,1,0:T(8,128)(2,1)S(1)} %shard_map.133), channel_id=1, source_target_pairs={{0,1},{1,0},{2,3},{3,2},{4,5},{5,4},{6,7},{7,6},{8,9},{9,8},{10,11... | collective-permute-start | bytes 1572872 | tf_op jit(solution)/shard_map/ppermute | solution.py:188
  130.1 14.2 %all-to-all-start.1 = ((bf16[16,16,1024]{2,1,0:T(8,128)(2,1)}), bf16[16,16,1024]{2,1,0:T(8,128)(2,1)S(1)}, u32[]{:S(2)}, u32[]{:S(2)}) async-start(bf16[16,16,1024]{2,1,0:T(8,128)(2,1)} %shard_map.134), calls=%async_computation.1 | async-start | bytes 1048576 | tf_op jit(solution)/shard_map/all_to_all | solution.py:191

commit v5 on v4

v5 whole, which is shorter than its diff:
```python
import functools
import math

import jax
import jax.numpy as jnp
from jax import lax
from jax.experimental import pallas as pl
from jax.experimental.pallas import tpu as pltpu
from jax.sharding import PartitionSpec as P

BF = jnp.bfloat16
F32 = jnp.float32
GROUP = ("row", "depth")
NEAR = (0, -1, 1, 2)


def peer(at):
    z = lax.axis_index("col")
    sign = 1 - 2 * lax.rem(lax.axis_index("depth"), 2)
    return lax.rem(z - sign * NEAR[at] + 16, 16), sign


def place(at, step):
    z, sign = peer(at)
    return lax.rem(z // 4 + sign * step + 4, 4)


def chunk_of(at, place_of):
    return 4 * place_of + lax.rem(peer(at)[0], 4)


def nt(left, right):
    return lax.dot_general(left, right, (((1,), (1,)), ((), ())), preferred_element_type=F32)


def nn(left, right):
    return lax.dot_general(left, right, (((1,), (0,)), ((), ())), preferred_element_type=F32)


def tn(left, right):
    return lax.dot_general(left, right, (((0,), (0,)), ((), ())), preferred_element_type=F32)


def call(body, out_shapes, n_scalar, n_array, scratch=(), mib=4, outside=(), outside_out=()):
    def place(at, away):
        return pl.BlockSpec(memory_space=pltpu.HBM if at in away else pltpu.VMEM)

    return pl.pallas_call(
        body,
        out_shape=[jax.ShapeDtypeStruct(s, d) for s, d in out_shapes],
        in_specs=[pl.BlockSpec(memory_space=pltpu.SMEM)] * n_scalar
        + [place(at, outside) for at in range(n_array)],
        out_specs=[place(at, outside_out) for at in range(len(out_shapes))],
        scratch_shapes=list(scratch),
        compiler_params=pltpu.CompilerParams(vmem_limit_bytes=mib * 1024 * 1024),
    )


def coded(x):
    return (x * jnp.abs(x)).astype(BF)


def decoded(x):
    wide = x.astype(F32)
    return wide * lax.rsqrt(jnp.abs(wide) + 1e-36)


def spread(both, out):
    for at in range(out.shape[0]):
        out[at] = both[...]


def stack(gate, gate_away, up, up_away, down, down_away, pair, both_down):
    ff = gate.shape[0]
    for at, rows in enumerate((gate, gate_away, up, up_away)):
        pair[at * ff : (at + 1) * ff, :] = rows[...]
    both_down[:ff, :] = down[...]
    both_down[ff:, :] = down_away[...]


def partial_sums(
    mine, w0, w1, w2, w3, w4, w5, third, first, second, own, kept, kept_pair, kept_down, ordered, pair, down, sems
):
    both, width = pair.shape
    block = own.shape[0]
    rows = mine.shape[1]
    for at in range(4):
        for step in range(4):
            to = at * block + step * rows
            ordered[to : to + rows, :] = mine[chunk_of(at, place(at, step))]
    stack(w0, w1, w2, w3, w4, w5, pair, down)
    copies = [
        pltpu.make_async_copy(held, to, sems.at[at])
        for at, (held, to) in enumerate(((ordered, kept), (pair, kept_pair), (down, kept_down)))
    ]
    for copy in copies:
        copy.start()
    gate_up = nt(ordered[:, :width], pair[...])
    cot = nt(ordered[:, width:], down[...])
    own[:, :both] = gate_up[:block, :]
    own[:, both:] = cot[:block, :]
    for at, out in ((3, third), (1, first), (2, second)):
        here = slice(at * block, (at + 1) * block)
        out[:, :both] = coded(gate_up[here, :])
        out[:, both:] = coded(cot[here, :])
    for copy in copies:
        copy.wait()


def near_sum(own, third, first, second, far, near, back, keep):
    chunk = keep.shape[0]

    def total(at):
        rows = slice(at * chunk, (at + 1) * chunk)
        return own[rows, :] + (decoded(first[rows, :]) + decoded(second[rows, :]) + decoded(third[rows, :]))

    far[...] = coded(total(2))
    near[...] = coded(total(1))
    back[...] = coded(total(3))
    keep[...] = total(0)


def swish(keep, far, near, back, out):
    ff = out.shape[1] // 3
    total = keep[...] + (decoded(near[...]) + decoded(far[...]) + decoded(back[...]))
    gate_sum = total[:, :ff]
    up_sum = total[:, ff : 2 * ff]
    hidden_cot = total[:, 2 * ff :]
    sig = jax.nn.sigmoid(gate_sum)
    gate_cot = hidden_cot * up_sum * sig * (1.0 + gate_sum * (1.0 - sig))
    up_cot = hidden_cot * gate_sum * sig
    out[:, :ff] = gate_cot.astype(BF)
    out[:, ff : 2 * ff] = up_cot.astype(BF)
    out[:, 2 * ff :] = (gate_sum * sig * up_sum).astype(BF)


def outward(c3, c1, c2, c0, pair, down, out, rows_of):
    both, width = pair.shape
    rows = out.shape[1]
    block = c0.shape[0]
    for at, c in ((3, c3), (1, c1), (2, c2), (0, c0)):
        rows_of[at * block : (at + 1) * block, :] = c[...]
    layer = nn(rows_of[:, both:], down[...]).astype(BF)
    back = nn(rows_of[:, :both], pair[...]).astype(BF)
    for at in range(4):
        for j in range(4):
            here = slice(at * block + j * rows, at * block + (j + 1) * rows)
            chunk = chunk_of(at, j)
            out[chunk, :, :width] = layer[here, :]
            out[chunk, :, width:] = back[here, :]


def weight_part(start, kind, c0, c1, c2, c3, ordered, part):
    width = ordered.shape[1] // 2
    size = part.shape[1]
    rows = c0.shape[0] // 4
    for at, c in enumerate((c0, c1, c2, c3)):
        for step in range(4):
            here = pl.ds(pl.multiple_of(place(at, step) * rows, rows), rows)
            to = at * c.shape[0] + step * rows
            part[to : to + rows, :] = c[here, start : start + size]
    tokens = ordered[:, width:] if kind == 2 else ordered[:, :width]
    return tn(part[...], tokens)


def weight_away(c0, c1, c2, c3, ordered, gate, up, down, part):
    ff = gate.shape[0]
    extra = part.shape[1] - ff
    for kind, out in enumerate((gate, up, down)):
        start = (2 * kind + 1) * ff - extra
        out[...] = coded(weight_part(start, kind, c0, c1, c2, c3, ordered, part)[extra:, :])


def weight_own(scale, c0, c1, c2, c3, ordered, a0, a1, a2, gate, up, down, part):
    ff = gate.shape[0]
    for kind, (arrived, out) in enumerate(((a0, gate), (a1, up), (a2, down))):
        sums = weight_part(2 * kind * ff, kind, c0, c1, c2, c3, ordered, part)[:ff, :]
        out[...] = ((sums + decoded(arrived[...])) * scale).astype(BF)


def last_sum(parts, layer_out, tokens_grad):
    width = layer_out.shape[1]
    total = parts[0].astype(F32)
    for at in range(1, parts.shape[0]):
        total = total + parts[at].astype(F32)
    layer_out[...] = total[:, :width].astype(BF)
    tokens_grad[...] = total[:, width:].astype(BF)


def shards(mesh, tokens, cotangent, gate_weight, up_weight, down_weight):
    cols, depth = mesh.shape["col"], mesh.shape["depth"]
    ranks = mesh.shape["row"] * depth
    ff, width = down_weight.shape
    rows = tokens.shape[0]
    total = rows * ranks
    cores = 2
    chips = ranks // cores
    chunk = rows
    block = 4 * chunk
    wide = 3 * cores * ff

    def shift(x, step):
        pairs = []
        for z in range(cols):
            for d in range(depth):
                to = (z + (step if d % 2 == 0 else -step)) % cols
                pairs.append((z * depth + d, to * depth + d))
        return lax.ppermute(x, ("col", "depth"), pairs)

    same_core = [[c + cores * a for a in range(chips)] for c in range(cores)]

    def swap(x):
        return lax.ppermute(x, "depth", [(d, d ^ 1) for d in range(depth)])

    def exchange(x):
        return lax.all_to_all(x, GROUP, 0, 0, tiled=True, axis_index_groups=same_core)

    both = jnp.concatenate([tokens, cotangent], axis=1)
    (sent,) = call(spread, [((chips, rows, 2 * width), BF)], 0, 1)(both)
    mine = exchange(sent)
    weights = []
    for held in (gate_weight.T, up_weight.T, down_weight):
        weights += [held, swap(held)]
    kept = [(4 * block, 2 * width), (4 * ff, width), (2 * ff, width)]
    third, first, second, own, ordered, pair, down = call(
        partial_sums,
        [((block, wide), BF)] * 3 + [((block, wide), F32)] + [(shape, BF) for shape in kept],
        0,
        7,
        [pltpu.VMEM(shape, BF) for shape in kept] + [pltpu.SemaphoreType.DMA((3,))],
        mib=10,
        outside_out=(4, 5, 6),
    )(mine, *weights)
    third = shift(third, -NEAR[3])
    first = shift(first, -NEAR[1])
    second = shift(second, -NEAR[2])
    far, near, back, keep = call(
        near_sum, [((chunk, wide), BF)] * 3 + [((chunk, wide), F32)], 0, 4
    )(own, third, first, second)
    far = shift(far, 8)
    near = shift(near, 4)
    back = shift(back, -4)
    (act,) = call(swish, [((chunk, wide), BF)], 0, 4)(keep, far, near, back)
    strided = [[i + 4 * j for j in range(4)] for i in range(4)]
    c0 = lax.all_gather(act, "col", axis=0, tiled=True, axis_index_groups=strided)
    c3 = shift(c0, NEAR[3])
    c1 = shift(c0, NEAR[1])
    c2 = shift(c0, NEAR[2])
    (out,) = call(
        outward,
        [((chips, rows, 2 * width), BF)],
        0,
        6,
        [pltpu.VMEM((4 * block, wide), BF)],
        mib=8,
    )(c3, c1, c2, c0, pair, down)
    out, c0, c1, c2, c3 = lax.optimization_barrier((out, c0, c1, c2, c3))
    parts = exchange(out)
    window = [pltpu.VMEM((4 * block, -(-ff // 128) * 128), BF)]
    grads = [((ff, width), BF)] * 3
    away = call(weight_away, grads, 0, 5, window, mib=8)(c0, c1, c2, c3, ordered)
    gate_g, up_g, down_g = call(
        functools.partial(weight_own, 1.0 / math.sqrt(total)), grads, 0, 8, window, mib=8
    )(c0, c1, c2, c3, ordered, *[swap(x) for x in away])
    parts, gate_g = lax.optimization_barrier((parts, gate_g))
    layer_out, tokens_grad = call(last_sum, [((rows, width), BF)] * 2, 0, 1)(parts)
    return (layer_out, tokens_grad, gate_g.T, up_g.T, down_g)


def solution(mesh):
    tok = P(GROUP, "col")
    wide = P("col", GROUP)

    def run(*args):
        return shards(mesh, *args)

    return jax.shard_map(
        run,
        mesh=mesh,
        in_specs=(tok, tok, wide, wide, tok),
        out_specs=(tok, tok, wide, wide, tok),
        check_vma=False,
    )
```

time: 146 us -> 141 us (0.966)
  waiting for transfers between devices: 47.6 us -> 32.4 us
  starting transfers between devices: 64.1 us -> 75 us
  local copies, waits for them, and re-layouts: 0.04 us -> 3.58 us
  blocking collectives: 22.1 us -> 19.4 us
    all_to_all x2, waiting for transfers between devices: 17.1 us -> 0.01 us  [exchange(): lax.all_to_all(x, GROUP, 0, 0, tiled=True, axis_index_groups=same_core)]
    ppermute x2 -> x6, starting transfers between devices: 10.4 us -> 16.9 us  [swap(): return lax.ppermute(x, 'depth', [(d, d ^ 1) for d in range(depth)])]
    unnamed x12 -> x14, local copies, waits for them, and re-layouts: 0.04 us -> 3.58 us
    all_to_all x2, starting transfers between devices: 11.5 us -> 14.3 us  [exchange(): lax.all_to_all(x, GROUP, 0, 0, tiled=True, axis_index_groups=same_core)]
    all_gather x1, blocking collectives: 22.1 us -> 19.4 us  [shards(): lax.all_gather(act, 'col', axis=0, tiled=True, axis_index_groups=strided)]
    pallas_call x5 -> x4, Pallas kernels: 7.17 us -> 5.82 us  [the longest x1 1.79 us: shards(): call(functools.partial(weight_own, 1.0 / math.sqrt(total)), grads, 0, 8,...]
  transfers between devices with their start and end apart: 13 -> 17, of which waited for: 11 -> 9; matrix products, arithmetic and copies ran while one was open for 0% -> 0% of each run, Pallas kernels for 2% -> 2%
where the time goes in v5:
time: 141 us; the launch traced here: 140 us
  starting transfers between devices  75 us (53%)
  waiting for transfers between devices  32.4 us (23%)
  blocking collectives  19.4 us (14%)
  Pallas kernels  7.95 us (6%)
  local copies, waits for them, and re-layouts  3.58 us (3%)
    ppermute x9, starting transfers between devices, shift(): return lax.ppermute(x, ('col', 'depth'), pairs)  43.8 us
    ppermute x9, waiting for transfers between devices, shift(): return lax.ppermute(x, ('col', 'depth'), pairs)  30.1 us
    all_gather x1, blocking collectives, shards(): lax.all_gather(act, 'col', axis=0, tiled=True, axis_index_groups=strided)  19.4 us
    ppermute x6, starting transfers between devices, swap(): return lax.ppermute(x, 'depth', [(d, d ^ 1) for d in range(depth)])  16.9 us
    all_to_all x2, starting transfers between devices, exchange(): lax.all_to_all(x, GROUP, 0, 0, tiled=True, axis_index_groups=same_core)  14.3 us
    unnamed x14, local copies, waits for them, and re-layouts  3.58 us
  transfers between devices with their start and end apart: 17, of which 9 were waited for; matrix products, arithmetic and copies ran while one was open for 0% of the time, Pallas kernels for 2%

profile of v5, /device:TPU:1, one launch (start us, length us, event | category | flops | bytes accessed | tf_op | source)
XLA Modules:
  0.0 140.0 jit_solution(8958397370512313742)
XLA Ops:
  0.6 0.0 copy-start
  0.6 0.0 copy-start.1
  0.7 0.0 copy-start.2
  0.7 0.8 pad_maximum_fusion.both
  1.5 0.9 shard_map.92
  2.4 7.6 %all-to-all-start = ((bf16[16,16,1024]{2,1,0:T(8,128)(2,1)}), bf16[16,16,1024]{2,1,0:T(8,128)(2,1)S(1)}, u32[]{:S(2)}, u32[]{:S(2)}) async-start(bf16[16,16,1024]{2,1,0:T(8,128)(2,1)} %shard_map.92), calls=%async_computation | async-start | bytes 1048576 | tf_op jit(solution)/shard_map/all_to_all | solution.py:216
  10.0 4.8 %collective-permute-start = (bf16[448,512]{1,0:T(8,128)(2,1)}, bf16[448,512]{1,0:T(8,128)(2,1)S(1)}, u32[]{:S(2)}, u32[]{:S(2)}) collective-permute-start(bf16[448,512]{1,0:T(8,128)(2,1)} %bitcast.4), channel_id=1, source_target_pairs={{0,1},{1,0},{2,3},{3,2},{4,5},{5,4},{6,7},{7,6},{8,9},{9,8},{10,11... | collective-permute-start | bytes 1376264 | tf_op jit(solution)/shard_map/ppermute | solution.py:213
  14.7 1.9 %collective-permute-start.1 = (bf16[448,512]{1,0:T(8,128)(2,1)}, bf16[448,512]{1,0:T(8,128)(2,1)S(1)}, u32[]{:S(2)}, u32[]{:S(2)}) collective-permute-start(bf16[448,512]{1,0:T(8,128)(2,1)} %bitcast.6), channel_id=1, source_target_pairs={{0,1},{1,0},{2,3},{3,2},{4,5},{5,4},{6,7},{7,6},{8,9},{9,8},{10,11... | collective-permute-start | bytes 1376264 | tf_op jit(solution)/shard_map/ppermute | solution.py:213
  16.7 2.4 %collective-permute-start.2 = (bf16[448,512]{1,0:T(8,128)(2,1)}, bf16[448,512]{1,0:T(8,128)(2,1)S(1)}, u32[]{:S(2)}, u32[]{:S(2)}) collective-permute-start(bf16[448,512]{1,0:T(8,128)(2,1)} %w4.1), channel_id=1, source_target_pairs={{0,1},{1,0},{2,3},{3,2},{4,5},{5,4},{6,7},{7,6},{8,9},{9,8},{10,11... | collective-permute-start | bytes 1376264 | tf_op jit(solution)/shard_map/ppermute | solution.py:213
  19.1 0.0 collective-permute-done.w1
  19.1 0.0 collective-permute-done.1.w3
  19.1 0.0 copy-start.3
  19.1 0.8 copy-done.3
  19.9 0.8 collective-permute-done.2.w5
  20.7 0.0 copy-start.5
  20.7 0.8 copy-done.5
  21.5 0.0 all-to-all-done.mine
  21.5 0.0 copy-done
  21.5 0.0 copy-done.1
  21.5 0.0 copy-done.2
  21.5 0.0 copy-start.4
  21.5 1.0 copy-done.4
  22.5 0.0 copy-start.6
  22.5 1.0 copy-done.6
  23.6 1.6 %shard_map.93 = (bf16[64,2688]{1,0:T(8,128)(2,1)S(1)}, bf16[64,2688]{1,0:T(8,128)(2,1)S(1)}, bf16[64,2688]{1,0:T(8,128)(2,1)S(1)}, f32[64,2688]{1,0:T(8,128)S(1)...) custom-call(bf16[16,16,1024]{2,1,0:T(8,128)(2,1)S(1)} %all-to-all-done.mine, ...), custom_call_target="tpu_custom_call" | custom-call | tf_op jit(solution)/shard_map/pallas_call | solution.py:225
  25.2 3.7 %collective-permute-start.3 = (bf16[64,2688]{1,0:T(8,128)(2,1)S(1)}, bf16[64,2688]{1,0:T(8,128)(2,1)S(1)}, u32[]{:S(2)}, u32[]{:S(2)}) collective-permute-start(bf16[64,2688]{1,0:T(8,128)(2,1)S(1)} %get-tuple-element.32), channel_id=1, source_target_pairs={{0,112},{1,17},{2,114},{3,19},{4,116},{5,21},{6,118},{7,23},{8,120... | collective-permute-start | bytes 1032200 | tf_op jit(solution)/shard_map/ppermute | solution.py:208
  28.8 8.1 %collective-permute-start.4 = (bf16[64,2688]{1,0:T(8,128)(2,1)S(1)}, bf16[64,2688]{1,0:T(8,128)(2,1)S(1)}, u32[]{:S(2)}, u32[]{:S(2)}) collective-permute-start(bf16[64,2688]{1,0:T(8,128)(2,1)S(1)} %get-tuple-element.33), channel_id=1, source_target_pairs={{0,8},{1,121},{2,10},{3,123},{4,12},{5,125},{6,14},{7,127},{8,16},... | collective-permute-start | bytes 1032200 | tf_op jit(solution)/shard_map/ppermute | solution.py:208
  37.0 1.9 %collective-permute-start.5 = (bf16[64,2688]{1,0:T(8,128)(2,1)S(1)}, bf16[64,2688]{1,0:T(8,128)(2,1)S(1)}, u32[]{:S(2)}, u32[]{:S(2)}) collective-permute-start(bf16[64,2688]{1,0:T(8,128)(2,1)S(1)} %get-tuple-element.34), channel_id=1, source_target_pairs={{0,120},{1,9},{2,122},{3,11},{4,124},{5,13},{6,126},{7,15},{8,0},{... | collective-permute-start | bytes 1032200 | tf_op jit(solution)/shard_map/ppermute | solution.py:208
  38.9 2.4 %collective-permute-done.3.third = bf16[64,2688]{1,0:T(8,128)(2,1)S(1)} collective-permute-done((bf16[64,2688]{1,0:T(8,128)(2,1)S(1)}, bf16[64,2688]{1,0:T(8,128)(2,1)S(1)}, u32[]{:S(2)}, u32[]{:S(2)}) %collective-permute-start.3) | collective-permute-done | bytes 344096 | tf_op jit(solution)/shard_map/ppermute | solution.py:208
  41.3 6.1 %collective-permute-done.4.first = bf16[64,2688]{1,0:T(8,128)(2,1)S(1)} collective-permute-done((bf16[64,2688]{1,0:T(8,128)(2,1)S(1)}, bf16[64,2688]{1,0:T(8,128)(2,1)S(1)}, u32[]{:S(2)}, u32[]{:S(2)}) %collective-permute-start.4) | collective-permute-done | bytes 344096 | tf_op jit(solution)/shard_map/ppermute | solution.py:208
  47.4 3.0 %collective-permute-done.5.second = bf16[64,2688]{1,0:T(8,128)(2,1)S(1)} collective-permute-done((bf16[64,2688]{1,0:T(8,128)(2,1)S(1)}, bf16[64,2688]{1,0:T(8,128)(2,1)S(1)}, u32[]{:S(2)}, u32[]{:S(2)}) %collective-permute-start.5) | collective-permute-done | bytes 344096 | tf_op jit(solution)/shard_map/ppermute | solution.py:208
  50.4 0.4 shard_map.94
  50.9 9.7 %collective-permute-start.6 = (bf16[16,2688]{1,0:T(8,128)(2,1)S(1)}, bf16[16,2688]{1,0:T(8,128)(2,1)S(1)}, u32[]{:S(2)}, u32[]{:S(2)}) collective-permute-start(bf16[16,2688]{1,0:T(8,128)(2,1)S(1)} %get-tuple-element.36), channel_id=1, source_target_pairs={{0,64},{1,65},{2,66},{3,67},{4,68},{5,69},{6,70},{7,71},{8,72},{9,... | collective-permute-start | bytes 258056 | tf_op jit(solution)/shard_map/ppermute | solution.py:208
  60.5 1.9 %collective-permute-start.7 = (bf16[16,2688]{1,0:T(8,128)(2,1)S(1)}, bf16[16,2688]{1,0:T(8,128)(2,1)S(1)}, u32[]{:S(2)}, u32[]{:S(2)}) collective-permute-start(bf16[16,2688]{1,0:T(8,128)(2,1)S(1)} %get-tuple-element.37), channel_id=1, source_target_pairs={{0,32},{1,97},{2,34},{3,99},{4,36},{5,101},{6,38},{7,103},{8,40},{... | collective-permute-start | bytes 258056 | tf_op jit(solution)/shard_map/ppermute | solution.py:208
  62.5 7.3 %collective-permute-start.8 = (bf16[16,2688]{1,0:T(8,128)(2,1)S(1)}, bf16[16,2688]{1,0:T(8,128)(2,1)S(1)}, u32[]{:S(2)}, u32[]{:S(2)}) collective-permute-start(bf16[16,2688]{1,0:T(8,128)(2,1)S(1)} %get-tuple-element.38), channel_id=1, source_target_pairs={{0,96},{1,33},{2,98},{3,35},{4,100},{5,37},{6,102},{7,39},{8,104},... | collective-permute-start | bytes 258056 | tf_op jit(solution)/shard_map/ppermute | solution.py:208
  69.8 0.0 collective-permute-done.6.far
  69.8 4.1 %collective-permute-done.7.near = bf16[16,2688]{1,0:T(8,128)(2,1)S(1)} collective-permute-done((bf16[16,2688]{1,0:T(8,128)(2,1)S(1)}, bf16[16,2688]{1,0:T(8,128)(2,1)S(1)}, u32[]{:S(2)}, u32[]{:S(2)}) %collective-permute-start.7) | collective-permute-done | bytes 86048 | tf_op jit(solution)/shard_map/ppermute | solution.py:208
  73.8 1.3 collective-permute-done.8.back
  75.1 0.1 shard_map.95
  75.3 19.4 %all_gather.3.c0 = bf16[64,2688]{1,0:T(8,128)(2,1)S(1)} all-gather(bf16[16,2688]{1,0:T(8,128)(2,1)S(1)} %shard_map.95), channel_id=1, replica_groups={{0,32,64,96},{8,40,72,104},{16,48,80,112},{24,56,88,120},{1,33,65,97},{..., dimensions={0}, use_global_device_ids=true | all-gather | bytes 430080 | tf_op jit(solution)/shard_map/all_gather | solution.py:245
  94.6 6.2 %collective-permute-start.11 = (bf16[64,2688]{1,0:T(8,128)(2,1)S(1)}, bf16[64,2688]{1,0:T(8,128)(2,1)S(1)}, u32[]{:S(2)}, u32[]{:S(2)}) collective-permute-start(bf16[64,2688]{1,0:T(8,128)(2,1)S(1)} %all_gather.3.c0), channel_id=1, source_target_pairs={{0,8},{1,121},{2,10},{3,123},{4,12},{5,125},{6,14},{7,127},{8,16},... | collective-permute-start | bytes 1032200 | tf_op jit(solution)/shard_map/ppermute | solution.py:208
  100.8 1.9 %collective-permute-start.10 = (bf16[64,2688]{1,0:T(8,128)(2,1)S(1)}, bf16[64,2688]{1,0:T(8,128)(2,1)S(1)}, u32[]{:S(2)}, u32[]{:S(2)}) collective-permute-start(bf16[64,2688]{1,0:T(8,128)(2,1)S(1)} %all_gather.3.c0), channel_id=1, source_target_pairs={{0,120},{1,9},{2,122},{3,11},{4,124},{5,13},{6,126},{7,15},{8,0},{... | collective-permute-start | bytes 1032200 | tf_op jit(solution)/shard_map/ppermute | solution.py:208
  102.7 3.1 %collective-permute-start.9 = (bf16[64,2688]{1,0:T(8,128)(2,1)S(1)}, bf16[64,2688]{1,0:T(8,128)(2,1)S(1)}, u32[]{:S(2)}, u32[]{:S(2)}) collective-permute-start(bf16[64,2688]{1,0:T(8,128)(2,1)S(1)} %all_gather.3.c0), channel_id=1, source_target_pairs={{0,16},{1,113},{2,18},{3,115},{4,20},{5,117},{6,22},{7,119},{8,24}... | collective-permute-start | bytes 1032200 | tf_op jit(solution)/shard_map/ppermute | solution.py:208
  105.8 0.0 collective-permute-done.11.c2
  105.8 7.8 %collective-permute-done.10.c1 = bf16[64,2688]{1,0:T(8,128)(2,1)S(1)} collective-permute-done((bf16[64,2688]{1,0:T(8,128)(2,1)S(1)}, bf16[64,2688]{1,0:T(8,128)(2,1)S(1)}, u32[]{:S(2)}, u32[]{:S(2)}) %collective-permute-start.10) | collective-permute-done | bytes 344096 | tf_op jit(solution)/shard_map/ppermute | solution.py:208
  113.7 5.4 %collective-permute-done.9.c3 = bf16[64,2688]{1,0:T(8,128)(2,1)S(1)} collective-permute-done((bf16[64,2688]{1,0:T(8,128)(2,1)S(1)}, bf16[64,2688]{1,0:T(8,128)(2,1)S(1)}, u32[]{:S(2)}, u32[]{:S(2)}) %collective-permute-start.9) | collective-permute-done | bytes 344096 | tf_op jit(solution)/shard_map/ppermute | solution.py:208
  119.1 1.7 %shard_map.96 = bf16[16,16,1024]{2,1,0:T(8,128)(2,1)} custom-call(bf16[64,2688]{1,0:T(8,128)(2,1)S(1)} %collective-permute-done.9.c3, bf16[64,2688]{1,0:T(8,128)(2,1)S(1)} %collective-permute-done.10.c1, bf16[64,2688]{1,0:T(8,128)(2,1)S(1)} %collective-permute-done.11.c2, bf16[64,2688]{1,0:T(8,128)(2,1)S(1)} %all_gather.3.c0, ...), custom_call_target="tpu_custom_call" | custom-call | tf_op jit(solution)/shard_map/pallas_call | solution.py:249
  120.8 6.8 %all-to-all-start.1 = ((bf16[16,16,1024]{2,1,0:T(8,128)(2,1)}), bf16[16,16,1024]{2,1,0:T(8,128)(2,1)S(1)}, u32[]{:S(2)}, u32[]{:S(2)}) async-start(bf16[16,16,1024]{2,1,0:T(8,128)(2,1)} %shard_map.96), calls=%async_computation.1 | async-start | bytes 1048576 | tf_op jit(solution)/shard_map/all_to_all | solution.py:216
  127.6 0.7 shard_map.97
  128.3 3.5 %collective-permute-start.12 = (bf16[448,512]{1,0:T(8,128)(2,1)S(1)}, bf16[448,512]{1,0:T(8,128)(2,1)S(1)}, u32[]{:S(2)}, u32[]{:S(2)}) collective-permute-start(bf16[448,512]{1,0:T(8,128)(2,1)S(1)} %get-tuple-element.47), channel_id=1, source_target_pairs={{0,1},{1,0},{2,3},{3,2},{4,5},{5,4},{6,7},{7,6},{8,9},{9,8},{10,11... | collective-permute-start | bytes 1376264 | tf_op jit(solution)/shard_map/ppermute | solution.py:213
  131.8 1.9 %collective-permute-start.13 = (bf16[448,512]{1,0:T(8,128)(2,1)S(1)}, bf16[448,512]{1,0:T(8,128)(2,1)S(1)}, u32[]{:S(2)}, u32[]{:S(2)}) collective-permute-start(bf16[448,512]{1,0:T(8,128)(2,1)S(1)} %get-tuple-element.48), channel_id=1, source_target_pairs={{0,1},{1,0},{2,3},{3,2},{4,5},{5,4},{6,7},{7,6},{8,9},{9,8},{10,11... | collective-permute-start | bytes 1376264 | tf_op jit(solution)/shard_map/ppermute | solution.py:213
  133.7 2.4 %collective-permute-start.14 = (bf16[448,512]{1,0:T(8,128)(2,1)S(1)}, bf16[448,512]{1,0:T(8,128)(2,1)S(1)}, u32[]{:S(2)}, u32[]{:S(2)}) collective-permute-start(bf16[448,512]{1,0:T(8,128)(2,1)S(1)} %get-tuple-element.49), channel_id=1, source_target_pairs={{0,1},{1,0},{2,3},{3,2},{4,5},{5,4},{6,7},{7,6},{8,9},{9,8},{10,11... | collective-permute-start | bytes 1376264 | tf_op jit(solution)/shard_map/ppermute | solution.py:213
  136.1 0.0 collective-permute-done.12.a0
  136.1 0.0 collective-permute-done.13.a1
  136.1 1.4 collective-permute-done.14.a2
  137.5 1.8 %shard_map.98 = (bf16[448,512]{1,0:T(8,128)(2,1)}, bf16[448,512]{1,0:T(8,128)(2,1)}, bf16[448,512]{1,0:T(8,128)(2,1)}) custom-call(bf16[64,2688]{1,0:T(8,128)(2,1)S(1)} %all_gather.3.c0, bf16[64,2688]{1,0:T(8,128)(2,1)S(1)} %collective-permute-done.10.c1, bf16[64,2688]{1,0:T(8,128)(2,1)S(1)} %collective-permute-done.11.c2, ...), custom_call_target="tpu_custom_call" | custom-call | tf_op jit(solution)/shard_map/pallas_call | solution.py:262
  139.3 0.0 all-to-all-done.1.parts
  139.3 0.7 shard_map.99
Async XLA Ops:
  0.6 20.9 %copy-start = (bf16[512,448]{0,1:T(8,128)(2,1)S(1)}, bf16[512,448]{0,1:T(8,128)(2,1)}, u32[]{:S(2)}) copy-start(bf16[512,448]{0,1:T(8,128)(2,1)} %param.7) | copy-start | bytes 1376260
  0.6 20.9 %copy-start.1 = (bf16[512,448]{0,1:T(8,128)(2,1)S(1)}, bf16[512,448]{0,1:T(8,128)(2,1)}, u32[]{:S(2)}) copy-start(bf16[512,448]{0,1:T(8,128)(2,1)} %param.8) | copy-start | bytes 1376260
  0.7 20.8 %copy-start.2 = (bf16[448,512]{1,0:T(8,128)(2,1)S(1)}, bf16[448,512]{1,0:T(8,128)(2,1)}, u32[]{:S(2)}) copy-start(bf16[448,512]{1,0:T(8,128)(2,1)} %w4.1) | copy-start | bytes 1376260
  2.4 19.1 %all-to-all-start = ((bf16[16,16,1024]{2,1,0:T(8,128)(2,1)}), bf16[16,16,1024]{2,1,0:T(8,128)(2,1)S(1)}, u32[]{:S(2)}, u32[]{:S(2)}) async-start(bf16[16,16,1024]{2,1,0:T(8,128)(2,1)} %shard_map.92), calls=%async_computation | async-start | bytes 1048576 | tf_op jit(solution)/shard_map/all_to_all | solution.py:216
  10.0 9.1 %collective-permute-start = (bf16[448,512]{1,0:T(8,128)(2,1)}, bf16[448,512]{1,0:T(8,128)(2,1)S(1)}, u32[]{:S(2)}, u32[]{:S(2)}) collective-permute-start(bf16[448,512]{1,0:T(8,128)(2,1)} %bitcast.4), channel_id=1, source_target_pairs={{0,1},{1,0},{2,3},{3,2},{4,5},{5,4},{6,7},{7,6},{8,9},{9,8},{10,11... | collective-permute-start | bytes 1376264 | tf_op jit(solution)/shard_map/ppermute | solution.py:213
  14.7 4.4 %collective-permute-start.1 = (bf16[448,512]{1,0:T(8,128)(2,1)}, bf16[448,512]{1,0:T(8,128)(2,1)S(1)}, u32[]{:S(2)}, u32[]{:S(2)}) collective-permute-start(bf16[448,512]{1,0:T(8,128)(2,1)} %bitcast.6), channel_id=1, source_target_pairs={{0,1},{1,0},{2,3},{3,2},{4,5},{5,4},{6,7},{7,6},{8,9},{9,8},{10,11... | collective-permute-start | bytes 1376264 | tf_op jit(solution)/shard_map/ppermute | solution.py:213
  16.7 4.0 %collective-permute-start.2 = (bf16[448,512]{1,0:T(8,128)(2,1)}, bf16[448,512]{1,0:T(8,128)(2,1)S(1)}, u32[]{:S(2)}, u32[]{:S(2)}) collective-permute-start(bf16[448,512]{1,0:T(8,128)(2,1)} %w4.1), channel_id=1, source_target_pairs={{0,1},{1,0},{2,3},{3,2},{4,5},{5,4},{6,7},{7,6},{8,9},{9,8},{10,11... | collective-permute-start | bytes 1376264 | tf_op jit(solution)/shard_map/ppermute | solution.py:213
  19.1 0.8 copy-start.3
  20.7 0.8 copy-start.5
  21.5 1.0 copy-start.4
  22.5 1.0 copy-start.6
  25.2 16.1 %collective-permute-start.3 = (bf16[64,2688]{1,0:T(8,128)(2,1)S(1)}, bf16[64,2688]{1,0:T(8,128)(2,1)S(1)}, u32[]{:S(2)}, u32[]{:S(2)}) collective-permute-start(bf16[64,2688]{1,0:T(8,128)(2,1)S(1)} %get-tuple-element.32), channel_id=1, source_target_pairs={{0,112},{1,17},{2,114},{3,19},{4,116},{5,21},{6,118},{7,23},{8,120... | collective-permute-start | bytes 1032200 | tf_op jit(solution)/shard_map/ppermute | solution.py:208
  28.8 18.6 %collective-permute-start.4 = (bf16[64,2688]{1,0:T(8,128)(2,1)S(1)}, bf16[64,2688]{1,0:T(8,128)(2,1)S(1)}, u32[]{:S(2)}, u32[]{:S(2)}) collective-permute-start(bf16[64,2688]{1,0:T(8,128)(2,1)S(1)} %get-tuple-element.33), channel_id=1, source_target_pairs={{0,8},{1,121},{2,10},{3,123},{4,12},{5,125},{6,14},{7,127},{8,16},... | collective-permute-start | bytes 1032200 | tf_op jit(solution)/shard_map/ppermute | solution.py:208
  37.0 13.4 %collective-permute-start.5 = (bf16[64,2688]{1,0:T(8,128)(2,1)S(1)}, bf16[64,2688]{1,0:T(8,128)(2,1)S(1)}, u32[]{:S(2)}, u32[]{:S(2)}) collective-permute-start(bf16[64,2688]{1,0:T(8,128)(2,1)S(1)} %get-tuple-element.34), channel_id=1, source_target_pairs={{0,120},{1,9},{2,122},{3,11},{4,124},{5,13},{6,126},{7,15},{8,0},{... | collective-permute-start | bytes 1032200 | tf_op jit(solution)/shard_map/ppermute | solution.py:208
  50.9 18.9 %collective-permute-start.6 = (bf16[16,2688]{1,0:T(8,128)(2,1)S(1)}, bf16[16,2688]{1,0:T(8,128)(2,1)S(1)}, u32[]{:S(2)}, u32[]{:S(2)}) collective-permute-start(bf16[16,2688]{1,0:T(8,128)(2,1)S(1)} %get-tuple-element.36), channel_id=1, source_target_pairs={{0,64},{1,65},{2,66},{3,67},{4,68},{5,69},{6,70},{7,71},{8,72},{9,... | collective-permute-start | bytes 258056 | tf_op jit(solution)/shard_map/ppermute | solution.py:208
  60.5 13.3 %collective-permute-start.7 = (bf16[16,2688]{1,0:T(8,128)(2,1)S(1)}, bf16[16,2688]{1,0:T(8,128)(2,1)S(1)}, u32[]{:S(2)}, u32[]{:S(2)}) collective-permute-start(bf16[16,2688]{1,0:T(8,128)(2,1)S(1)} %get-tuple-element.37), channel_id=1, source_target_pairs={{0,32},{1,97},{2,34},{3,99},{4,36},{5,101},{6,38},{7,103},{8,40},{... | collective-permute-start | bytes 258056 | tf_op jit(solution)/shard_map/ppermute | solution.py:208
  62.5 12.6 %collective-permute-start.8 = (bf16[16,2688]{1,0:T(8,128)(2,1)S(1)}, bf16[16,2688]{1,0:T(8,128)(2,1)S(1)}, u32[]{:S(2)}, u32[]{:S(2)}) collective-permute-start(bf16[16,2688]{1,0:T(8,128)(2,1)S(1)} %get-tuple-element.38), channel_id=1, source_target_pairs={{0,96},{1,33},{2,98},{3,35},{4,100},{5,37},{6,102},{7,39},{8,104},... | collective-permute-start | bytes 258056 | tf_op jit(solution)/shard_map/ppermute | solution.py:208
  94.6 11.2 %collective-permute-start.11 = (bf16[64,2688]{1,0:T(8,128)(2,1)S(1)}, bf16[64,2688]{1,0:T(8,128)(2,1)S(1)}, u32[]{:S(2)}, u32[]{:S(2)}) collective-permute-start(bf16[64,2688]{1,0:T(8,128)(2,1)S(1)} %all_gather.3.c0), channel_id=1, source_target_pairs={{0,8},{1,121},{2,10},{3,123},{4,12},{5,125},{6,14},{7,127},{8,16},... | collective-permute-start | bytes 1032200 | tf_op jit(solution)/shard_map/ppermute | solution.py:208
  100.8 12.9 %collective-permute-start.10 = (bf16[64,2688]{1,0:T(8,128)(2,1)S(1)}, bf16[64,2688]{1,0:T(8,128)(2,1)S(1)}, u32[]{:S(2)}, u32[]{:S(2)}) collective-permute-start(bf16[64,2688]{1,0:T(8,128)(2,1)S(1)} %all_gather.3.c0), channel_id=1, source_target_pairs={{0,120},{1,9},{2,122},{3,11},{4,124},{5,13},{6,126},{7,15},{8,0},{... | collective-permute-start | bytes 1032200 | tf_op jit(solution)/shard_map/ppermute | solution.py:208
  102.7 16.4 %collective-permute-start.9 = (bf16[64,2688]{1,0:T(8,128)(2,1)S(1)}, bf16[64,2688]{1,0:T(8,128)(2,1)S(1)}, u32[]{:S(2)}, u32[]{:S(2)}) collective-permute-start(bf16[64,2688]{1,0:T(8,128)(2,1)S(1)} %all_gather.3.c0), channel_id=1, source_target_pairs={{0,16},{1,113},{2,18},{3,115},{4,20},{5,117},{6,22},{7,119},{8,24}... | collective-permute-start | bytes 1032200 | tf_op jit(solution)/shard_map/ppermute | solution.py:208
  120.8 18.5 %all-to-all-start.1 = ((bf16[16,16,1024]{2,1,0:T(8,128)(2,1)}), bf16[16,16,1024]{2,1,0:T(8,128)(2,1)S(1)}, u32[]{:S(2)}, u32[]{:S(2)}) async-start(bf16[16,16,1024]{2,1,0:T(8,128)(2,1)} %shard_map.96), calls=%async_computation.1 | async-start | bytes 1048576 | tf_op jit(solution)/shard_map/all_to_all | solution.py:216
  128.3 7.8 %collective-permute-start.12 = (bf16[448,512]{1,0:T(8,128)(2,1)S(1)}, bf16[448,512]{1,0:T(8,128)(2,1)S(1)}, u32[]{:S(2)}, u32[]{:S(2)}) collective-permute-start(bf16[448,512]{1,0:T(8,128)(2,1)S(1)} %get-tuple-element.47), channel_id=1, source_target_pairs={{0,1},{1,0},{2,3},{3,2},{4,5},{5,4},{6,7},{7,6},{8,9},{9,8},{10,11... | collective-permute-start | bytes 1376264 | tf_op jit(solution)/shard_map/ppermute | solution.py:213
  131.8 4.4 %collective-permute-start.13 = (bf16[448,512]{1,0:T(8,128)(2,1)S(1)}, bf16[448,512]{1,0:T(8,128)(2,1)S(1)}, u32[]{:S(2)}, u32[]{:S(2)}) collective-permute-start(bf16[448,512]{1,0:T(8,128)(2,1)S(1)} %get-tuple-element.48), channel_id=1, source_target_pairs={{0,1},{1,0},{2,3},{3,2},{4,5},{5,4},{6,7},{7,6},{8,9},{9,8},{10,11... | collective-permute-start | bytes 1376264 | tf_op jit(solution)/shard_map/ppermute | solution.py:213
  133.7 3.8 %collective-permute-start.14 = (bf16[448,512]{1,0:T(8,128)(2,1)S(1)}, bf16[448,512]{1,0:T(8,128)(2,1)S(1)}, u32[]{:S(2)}, u32[]{:S(2)}) collective-permute-start(bf16[448,512]{1,0:T(8,128)(2,1)S(1)} %get-tuple-element.49), channel_id=1, source_target_pairs={{0,1},{1,0},{2,3},{3,2},{4,5},{5,4},{6,7},{7,6},{8,9},{9,8},{10,11... | collective-permute-start | bytes 1376264 | tf_op jit(solution)/shard_map/ppermute | solution.py:213

commit v6 on v5

--- a/solution.py
+++ b/solution.py
@@ -78,9 +78,7 @@
     both_down[ff:, :] = down_away[...]
 
 
-def partial_sums(
-    mine, w0, w1, w2, w3, w4, w5, third, first, second, own, kept, kept_pair, kept_down, ordered, pair, down, sems
-):
+def partial_sums(mine, pair, down, third, first, second, own, kept, kept_pair, kept_down, ordered, sems):
     both, width = pair.shape
     block = own.shape[0]
     rows = mine.shape[1]
@@ -88,7 +86,6 @@
         for step in range(4):
             to = at * block + step * rows
             ordered[to : to + rows, :] = mine[chunk_of(at, place(at, step))]
-    stack(w0, w1, w2, w3, w4, w5, pair, down)
     copies = [
         pltpu.make_async_copy(held, to, sems.at[at])
         for at, (held, to) in enumerate(((ordered, kept), (pair, kept_pair), (down, kept_down)))
@@ -107,7 +104,7 @@
         copy.wait()
 
 
-def near_sum(own, third, first, second, far, near, back, keep):
+def near_sum(own, first, second, third, far, near, back, keep):
     chunk = keep.shape[0]
 
     def total(at):
@@ -134,11 +131,11 @@
     out[:, 2 * ff :] = (gate_sum * sig * up_sum).astype(BF)
 
 
-def outward(c3, c1, c2, c0, pair, down, out, rows_of):
+def outward(c2, c1, c3, c0, pair, down, out, rows_of):
     both, width = pair.shape
     rows = out.shape[1]
     block = c0.shape[0]
-    for at, c in ((3, c3), (1, c1), (2, c2), (0, c0)):
+    for at, c in ((2, c2), (1, c1), (3, c3), (0, c0)):
         rows_of[at * block : (at + 1) * block, :] = c[...]
     layer = nn(rows_of[:, both:], down[...]).astype(BF)
     back = nn(rows_of[:, :both], pair[...]).astype(BF)
@@ -226,17 +223,17 @@
         partial_sums,
         [((block, wide), BF)] * 3 + [((block, wide), F32)] + [(shape, BF) for shape in kept],
         0,
-        7,
-        [pltpu.VMEM(shape, BF) for shape in kept] + [pltpu.SemaphoreType.DMA((3,))],
+        3,
+        [pltpu.VMEM(kept[0], BF), pltpu.SemaphoreType.DMA((3,))],
         mib=10,
         outside_out=(4, 5, 6),
-    )(mine, *weights)
+    )(mine, *call(stack, [(shape, BF) for shape in kept[1:]], 0, 6, mib=4)(*weights))
     third = shift(third, -NEAR[3])
     first = shift(first, -NEAR[1])
     second = shift(second, -NEAR[2])
     far, near, back, keep = call(
         near_sum, [((chunk, wide), BF)] * 3 + [((chunk, wide), F32)], 0, 4
-    )(own, third, first, second)
+    )(own, first, second, third)
     far = shift(far, 8)
     near = shift(near, 4)
     back = shift(back, -4)
@@ -253,7 +250,7 @@
         6,
         [pltpu.VMEM((4 * block, wide), BF)],
         mib=8,
-    )(c3, c1, c2, c0, pair, down)
+    )(c2, c1, c3, c0, pair, down)
     out, c0, c1, c2, c3 = lax.optimization_barrier((out, c0, c1, c2, c3))
     parts = exchange(out)
     window = [pltpu.VMEM((4 * block, -(-ff // 128) * 128), BF)]

time: 141 us -> 138 us (0.979)
    ppermute x9, waiting for transfers between devices: 30.1 us -> 28.2 us  [shift(): return lax.ppermute(x, ('col', 'depth'), pairs)]
    ppermute x6, starting transfers between devices: 16.9 us -> 18.8 us  [swap(): return lax.ppermute(x, 'depth', [(d, d ^ 1) for d in range(depth)])]
    unnamed x14 -> x10, local copies, waits for them, and re-layouts: 3.58 us -> 2.76 us
where the time goes in v6:
time: 138 us
  starting transfers between devices  75.2 us (54%)
  waiting for transfers between devices  31.2 us (23%)
  blocking collectives  18.7 us (14%)
  Pallas kernels  7.94 us (6%)
  local copies, waits for them, and re-layouts  2.76 us (2%)
    ppermute x9, starting transfers between devices, shift(): return lax.ppermute(x, ('col', 'depth'), pairs)  43.3 us
    ppermute x9, waiting for transfers between devices, shift(): return lax.ppermute(x, ('col', 'depth'), pairs)  28.2 us
    ppermute x6, starting transfers between devices, swap(): return lax.ppermute(x, 'depth', [(d, d ^ 1) for d in range(depth)])  18.8 us
    all_gather x1, blocking collectives, shards(): lax.all_gather(act, 'col', axis=0, tiled=True, axis_index_groups=strided)  18.7 us
    all_to_all x2, starting transfers between devices, exchange(): lax.all_to_all(x, GROUP, 0, 0, tiled=True, axis_index_groups=same_core)  13.1 us
    ppermute x6, waiting for transfers between devices, swap(): return lax.ppermute(x, 'depth', [(d, d ^ 1) for d in range(depth)])  3.02 us
  transfers between devices with their start and end apart: 17, of which 9 were waited for; matrix products, arithmetic and copies ran while one was open for 0% of the time, Pallas kernels for 2%

profile of v6, /device:TPU:1, one launch (start us, length us, event | category | flops | bytes accessed | tf_op | source)
XLA Modules:
  0.0 137.5 jit_solution(2966280476533068837)
XLA Ops:
  0.6 0.0 copy-start.2
  0.6 0.0 copy-start.3
  0.7 0.0 copy-start.4
  0.7 0.8 pad_maximum_fusion.both
  1.5 0.8 shard_map.92
  2.3 7.6 %all-to-all-start = ((bf16[16,16,1024]{2,1,0:T(8,128)(2,1)}), bf16[16,16,1024]{2,1,0:T(8,128)(2,1)S(1)}, u32[]{:S(2)}, u32[]{:S(2)}) async-start(bf16[16,16,1024]{2,1,0:T(8,128)(2,1)} %shard_map.92), calls=%async_computation | async-start | bytes 1048576 | tf_op jit(solution)/shard_map/all_to_all | solution.py:213
  9.9 4.8 %collective-permute-start = (bf16[448,512]{1,0:T(8,128)(2,1)}, bf16[448,512]{1,0:T(8,128)(2,1)S(1)}, u32[]{:S(2)}, u32[]{:S(2)}) collective-permute-start(bf16[448,512]{1,0:T(8,128)(2,1)} %bitcast.4), channel_id=1, source_target_pairs={{0,1},{1,0},{2,3},{3,2},{4,5},{5,4},{6,7},{7,6},{8,9},{9,8},{10,11... | collective-permute-start | bytes 1376264 | tf_op jit(solution)/shard_map/ppermute | solution.py:210
  14.7 1.9 %collective-permute-start.1 = (bf16[448,512]{1,0:T(8,128)(2,1)}, bf16[448,512]{1,0:T(8,128)(2,1)S(1)}, u32[]{:S(2)}, u32[]{:S(2)}) collective-permute-start(bf16[448,512]{1,0:T(8,128)(2,1)} %bitcast.6), channel_id=1, source_target_pairs={{0,1},{1,0},{2,3},{3,2},{4,5},{5,4},{6,7},{7,6},{8,9},{9,8},{10,11... | collective-permute-start | bytes 1376264 | tf_op jit(solution)/shard_map/ppermute | solution.py:210
  16.7 2.4 %collective-permute-start.2 = (bf16[448,512]{1,0:T(8,128)(2,1)}, bf16[448,512]{1,0:T(8,128)(2,1)S(1)}, u32[]{:S(2)}, u32[]{:S(2)}) collective-permute-start(bf16[448,512]{1,0:T(8,128)(2,1)} %down.1), channel_id=1, source_target_pairs={{0,1},{1,0},{2,3},{3,2},{4,5},{5,4},{6,7},{7,6},{8,9},{9,8},{10,11... | collective-permute-start | bytes 1376264 | tf_op jit(solution)/shard_map/ppermute | solution.py:210
  19.1 0.0 collective-permute-done.gate_away
  19.1 0.0 collective-permute-done.1.up_away
  19.1 1.6 %collective-permute-done.2.down_away = bf16[448,512]{1,0:T(8,128)(2,1)S(1)} collective-permute-done((bf16[448,512]{1,0:T(8,128)(2,1)}, bf16[448,512]{1,0:T(8,128)(2,1)S(1)}, u32[]{:S(2)}, u32[]{:S(2)}) %collective-permute-start.2) | collective-permute-done | bytes 458784 | tf_op jit(solution)/shard_map/ppermute | solution.py:210
  20.7 0.0 copy-done.2
  20.7 0.0 copy-done.3
  20.7 0.0 copy-done.4
  20.7 0.2 shard_map.93
  20.9 0.0 copy-start
  20.9 1.2 copy-done
  22.1 0.0 all-to-all-done.mine
  22.1 0.0 copy-start.1
  22.1 1.5 %copy-done.1 = bf16[1792,512]{1,0:T(8,128)(2,1)S(1)} copy-done((bf16[1792,512]{1,0:T(8,128)(2,1)S(1)}, bf16[1792,512]{1,0:T(8,128)(2,1)}, u32[]{:S(2)}) %copy-start.1) | copy-done | bytes 1835032
  23.6 1.5 %shard_map.94 = (bf16[64,2688]{1,0:T(8,128)(2,1)S(1)}, bf16[64,2688]{1,0:T(8,128)(2,1)S(1)}, bf16[64,2688]{1,0:T(8,128)(2,1)S(1)}, f32[64,2688]{1,0:T(8,128)S(1)...) custom-call(bf16[16,16,1024]{2,1,0:T(8,128)(2,1)S(1)} %all-to-all-done.mine, ...), custom_call_target="tpu_custom_call" | custom-call | tf_op jit(solution)/shard_map/pallas_call | solution.py:222
  25.1 9.2 %collective-permute-start.3 = (bf16[64,2688]{1,0:T(8,128)(2,1)S(1)}, bf16[64,2688]{1,0:T(8,128)(2,1)S(1)}, u32[]{:S(2)}, u32[]{:S(2)}) collective-permute-start(bf16[64,2688]{1,0:T(8,128)(2,1)S(1)} %get-tuple-element.36), channel_id=1, source_target_pairs={{0,8},{1,121},{2,10},{3,123},{4,12},{5,125},{6,14},{7,127},{8,16},... | collective-permute-start | bytes 1032200 | tf_op jit(solution)/shard_map/ppermute | solution.py:205
  34.3 1.9 %collective-permute-start.4 = (bf16[64,2688]{1,0:T(8,128)(2,1)S(1)}, bf16[64,2688]{1,0:T(8,128)(2,1)S(1)}, u32[]{:S(2)}, u32[]{:S(2)}) collective-permute-start(bf16[64,2688]{1,0:T(8,128)(2,1)S(1)} %get-tuple-element.37), channel_id=1, source_target_pairs={{0,120},{1,9},{2,122},{3,11},{4,124},{5,13},{6,126},{7,15},{8,0},{... | collective-permute-start | bytes 1032200 | tf_op jit(solution)/shard_map/ppermute | solution.py:205
  36.3 1.9 %collective-permute-start.5 = (bf16[64,2688]{1,0:T(8,128)(2,1)S(1)}, bf16[64,2688]{1,0:T(8,128)(2,1)S(1)}, u32[]{:S(2)}, u32[]{:S(2)}) collective-permute-start(bf16[64,2688]{1,0:T(8,128)(2,1)S(1)} %get-tuple-element.38), channel_id=1, source_target_pairs={{0,112},{1,17},{2,114},{3,19},{4,116},{5,21},{6,118},{7,23},{8,120... | collective-permute-start | bytes 1032200 | tf_op jit(solution)/shard_map/ppermute | solution.py:205
  38.2 0.3 collective-permute-done.3.first
  38.5 6.6 %collective-permute-done.4.second = bf16[64,2688]{1,0:T(8,128)(2,1)S(1)} collective-permute-done((bf16[64,2688]{1,0:T(8,128)(2,1)S(1)}, bf16[64,2688]{1,0:T(8,128)(2,1)S(1)}, u32[]{:S(2)}, u32[]{:S(2)}) %collective-permute-start.4) | collective-permute-done | bytes 344096 | tf_op jit(solution)/shard_map/ppermute | solution.py:205
  45.1 6.5 %collective-permute-done.5.third = bf16[64,2688]{1,0:T(8,128)(2,1)S(1)} collective-permute-done((bf16[64,2688]{1,0:T(8,128)(2,1)S(1)}, bf16[64,2688]{1,0:T(8,128)(2,1)S(1)}, u32[]{:S(2)}, u32[]{:S(2)}) %collective-permute-start.5) | collective-permute-done | bytes 344096 | tf_op jit(solution)/shard_map/ppermute | solution.py:205
  51.6 0.4 shard_map.95
  52.0 7.7 %collective-permute-start.6 = (bf16[16,2688]{1,0:T(8,128)(2,1)S(1)}, bf16[16,2688]{1,0:T(8,128)(2,1)S(1)}, u32[]{:S(2)}, u32[]{:S(2)}) collective-permute-start(bf16[16,2688]{1,0:T(8,128)(2,1)S(1)} %get-tuple-element.40), channel_id=1, source_target_pairs={{0,64},{1,65},{2,66},{3,67},{4,68},{5,69},{6,70},{7,71},{8,72},{9,... | collective-permute-start | bytes 258056 | tf_op jit(solution)/shard_map/ppermute | solution.py:205
  59.7 1.9 %collective-permute-start.7 = (bf16[16,2688]{1,0:T(8,128)(2,1)S(1)}, bf16[16,2688]{1,0:T(8,128)(2,1)S(1)}, u32[]{:S(2)}, u32[]{:S(2)}) collective-permute-start(bf16[16,2688]{1,0:T(8,128)(2,1)S(1)} %get-tuple-element.41), channel_id=1, source_target_pairs={{0,32},{1,97},{2,34},{3,99},{4,36},{5,101},{6,38},{7,103},{8,40},{... | collective-permute-start | bytes 258056 | tf_op jit(solution)/shard_map/ppermute | solution.py:205
  61.7 7.3 %collective-permute-start.8 = (bf16[16,2688]{1,0:T(8,128)(2,1)S(1)}, bf16[16,2688]{1,0:T(8,128)(2,1)S(1)}, u32[]{:S(2)}, u32[]{:S(2)}) collective-permute-start(bf16[16,2688]{1,0:T(8,128)(2,1)S(1)} %get-tuple-element.42), channel_id=1, source_target_pairs={{0,96},{1,33},{2,98},{3,35},{4,100},{5,37},{6,102},{7,39},{8,104},... | collective-permute-start | bytes 258056 | tf_op jit(solution)/shard_map/ppermute | solution.py:205
  69.0 2.1 %collective-permute-done.6.far = bf16[16,2688]{1,0:T(8,128)(2,1)S(1)} collective-permute-done((bf16[16,2688]{1,0:T(8,128)(2,1)S(1)}, bf16[16,2688]{1,0:T(8,128)(2,1)S(1)}, u32[]{:S(2)}, u32[]{:S(2)}) %collective-permute-start.6) | collective-permute-done | bytes 86048 | tf_op jit(solution)/shard_map/ppermute | solution.py:205
  71.1 2.7 %collective-permute-done.7.near = bf16[16,2688]{1,0:T(8,128)(2,1)S(1)} collective-permute-done((bf16[16,2688]{1,0:T(8,128)(2,1)S(1)}, bf16[16,2688]{1,0:T(8,128)(2,1)S(1)}, u32[]{:S(2)}, u32[]{:S(2)}) %collective-permute-start.7) | collective-permute-done | bytes 86048 | tf_op jit(solution)/shard_map/ppermute | solution.py:205
  73.7 0.0 collective-permute-done.8.back
  73.7 0.1 shard_map.96
  73.9 18.7 %all_gather.3.c0 = bf16[64,2688]{1,0:T(8,128)(2,1)S(1)} all-gather(bf16[16,2688]{1,0:T(8,128)(2,1)S(1)} %shard_map.96), channel_id=1, replica_groups={{0,32,64,96},{8,40,72,104},{16,48,80,112},{24,56,88,120},{1,33,65,97},{..., dimensions={0}, use_global_device_ids=true | all-gather | bytes 430080 | tf_op jit(solution)/shard_map/all_gather | solution.py:242
  92.6 6.5 %collective-permute-start.11 = (bf16[64,2688]{1,0:T(8,128)(2,1)S(1)}, bf16[64,2688]{1,0:T(8,128)(2,1)S(1)}, u32[]{:S(2)}, u32[]{:S(2)}) collective-permute-start(bf16[64,2688]{1,0:T(8,128)(2,1)S(1)} %all_gather.3.c0), channel_id=1, source_target_pairs={{0,16},{1,113},{2,18},{3,115},{4,20},{5,117},{6,22},{7,119},{8,24}... | collective-permute-start | bytes 1032200 | tf_op jit(solution)/shard_map/ppermute | solution.py:205
  99.1 4.9 %collective-permute-start.10 = (bf16[64,2688]{1,0:T(8,128)(2,1)S(1)}, bf16[64,2688]{1,0:T(8,128)(2,1)S(1)}, u32[]{:S(2)}, u32[]{:S(2)}) collective-permute-start(bf16[64,2688]{1,0:T(8,128)(2,1)S(1)} %all_gather.3.c0), channel_id=1, source_target_pairs={{0,120},{1,9},{2,122},{3,11},{4,124},{5,13},{6,126},{7,15},{8,0},{... | collective-permute-start | bytes 1032200 | tf_op jit(solution)/shard_map/ppermute | solution.py:205
  104.0 2.0 %collective-permute-start.9 = (bf16[64,2688]{1,0:T(8,128)(2,1)S(1)}, bf16[64,2688]{1,0:T(8,128)(2,1)S(1)}, u32[]{:S(2)}, u32[]{:S(2)}) collective-permute-start(bf16[64,2688]{1,0:T(8,128)(2,1)S(1)} %all_gather.3.c0), channel_id=1, source_target_pairs={{0,8},{1,121},{2,10},{3,123},{4,12},{5,125},{6,14},{7,127},{8,16},... | collective-permute-start | bytes 1032200 | tf_op jit(solution)/shard_map/ppermute | solution.py:205
  106.0 0.9 collective-permute-done.11.c3
  106.9 9.1 %collective-permute-done.10.c1 = bf16[64,2688]{1,0:T(8,128)(2,1)S(1)} collective-permute-done((bf16[64,2688]{1,0:T(8,128)(2,1)S(1)}, bf16[64,2688]{1,0:T(8,128)(2,1)S(1)}, u32[]{:S(2)}, u32[]{:S(2)}) %collective-permute-start.10) | collective-permute-done | bytes 344096 | tf_op jit(solution)/shard_map/ppermute | solution.py:205
  116.0 0.0 collective-permute-done.9.c2
  116.0 1.7 %shard_map.97 = bf16[16,16,1024]{2,1,0:T(8,128)(2,1)} custom-call(bf16[64,2688]{1,0:T(8,128)(2,1)S(1)} %collective-permute-done.9.c2, bf16[64,2688]{1,0:T(8,128)(2,1)S(1)} %collective-permute-done.10.c1, bf16[64,2688]{1,0:T(8,128)(2,1)S(1)} %collective-permute-done.11.c3, bf16[64,2688]{1,0:T(8,128)(2,1)S(1)} %all_gather.3.c0, ...), custom_call_target="tpu_custom_call" | custom-call | tf_op jit(solution)/shard_map/pallas_call | solution.py:246
  117.7 5.5 %all-to-all-start.1 = ((bf16[16,16,1024]{2,1,0:T(8,128)(2,1)}), bf16[16,16,1024]{2,1,0:T(8,128)(2,1)S(1)}, u32[]{:S(2)}, u32[]{:S(2)}) async-start(bf16[16,16,1024]{2,1,0:T(8,128)(2,1)} %shard_map.97), calls=%async_computation.1 | async-start | bytes 1048576 | tf_op jit(solution)/shard_map/all_to_all | solution.py:213
  123.2 0.7 shard_map.98
  123.9 5.3 %collective-permute-start.12 = (bf16[448,512]{1,0:T(8,128)(2,1)S(1)}, bf16[448,512]{1,0:T(8,128)(2,1)S(1)}, u32[]{:S(2)}, u32[]{:S(2)}) collective-permute-start(bf16[448,512]{1,0:T(8,128)(2,1)S(1)} %get-tuple-element.51), channel_id=1, source_target_pairs={{0,1},{1,0},{2,3},{3,2},{4,5},{5,4},{6,7},{7,6},{8,9},{9,8},{10,11... | collective-permute-start | bytes 1376264 | tf_op jit(solution)/shard_map/ppermute | solution.py:210
  129.3 1.9 %collective-permute-start.13 = (bf16[448,512]{1,0:T(8,128)(2,1)S(1)}, bf16[448,512]{1,0:T(8,128)(2,1)S(1)}, u32[]{:S(2)}, u32[]{:S(2)}) collective-permute-start(bf16[448,512]{1,0:T(8,128)(2,1)S(1)} %get-tuple-element.52), channel_id=1, source_target_pairs={{0,1},{1,0},{2,3},{3,2},{4,5},{5,4},{6,7},{7,6},{8,9},{9,8},{10,11... | collective-permute-start | bytes 1376264 | tf_op jit(solution)/shard_map/ppermute | solution.py:210
  131.2 2.4 %collective-permute-start.14 = (bf16[448,512]{1,0:T(8,128)(2,1)S(1)}, bf16[448,512]{1,0:T(8,128)(2,1)S(1)}, u32[]{:S(2)}, u32[]{:S(2)}) collective-permute-start(bf16[448,512]{1,0:T(8,128)(2,1)S(1)} %get-tuple-element.53), channel_id=1, source_target_pairs={{0,1},{1,0},{2,3},{3,2},{4,5},{5,4},{6,7},{7,6},{8,9},{9,8},{10,11... | collective-permute-start | bytes 1376264 | tf_op jit(solution)/shard_map/ppermute | solution.py:210
  133.6 0.0 collective-permute-done.12.a0
  133.6 0.0 collective-permute-done.13.a1
  133.6 1.4 %collective-permute-done.14.a2 = bf16[448,512]{1,0:T(8,128)(2,1)S(1)} collective-permute-done((bf16[448,512]{1,0:T(8,128)(2,1)S(1)}, bf16[448,512]{1,0:T(8,128)(2,1)S(1)}, u32[]{:S(2)}, u32[]{:S(2)}) %collective-permute-start.14) | collective-permute-done | bytes 458784 | tf_op jit(solution)/shard_map/ppermute | solution.py:210
  135.0 1.8 %shard_map.99 = (bf16[448,512]{1,0:T(8,128)(2,1)}, bf16[448,512]{1,0:T(8,128)(2,1)}, bf16[448,512]{1,0:T(8,128)(2,1)}) custom-call(bf16[64,2688]{1,0:T(8,128)(2,1)S(1)} %all_gather.3.c0, bf16[64,2688]{1,0:T(8,128)(2,1)S(1)} %collective-permute-done.10.c1, bf16[64,2688]{1,0:T(8,128)(2,1)S(1)} %collective-permute-done.9.c2, ...), custom_call_target="tpu_custom_call" | custom-call | tf_op jit(solution)/shard_map/pallas_call | solution.py:259
  136.8 0.0 all-to-all-done.1.parts
  136.8 0.7 shard_map.100
Async XLA Ops:
  0.6 20.1 %copy-start.2 = (bf16[512,448]{0,1:T(8,128)(2,1)S(1)}, bf16[512,448]{0,1:T(8,128)(2,1)}, u32[]{:S(2)}) copy-start(bf16[512,448]{0,1:T(8,128)(2,1)} %param.7) | copy-start | bytes 1376260
  0.6 20.1 %copy-start.3 = (bf16[512,448]{0,1:T(8,128)(2,1)S(1)}, bf16[512,448]{0,1:T(8,128)(2,1)}, u32[]{:S(2)}) copy-start(bf16[512,448]{0,1:T(8,128)(2,1)} %param.8) | copy-start | bytes 1376260
  0.7 20.1 %copy-start.4 = (bf16[448,512]{1,0:T(8,128)(2,1)S(1)}, bf16[448,512]{1,0:T(8,128)(2,1)}, u32[]{:S(2)}) copy-start(bf16[448,512]{1,0:T(8,128)(2,1)} %down.1) | copy-start | bytes 1376260
  2.3 19.8 %all-to-all-start = ((bf16[16,16,1024]{2,1,0:T(8,128)(2,1)}), bf16[16,16,1024]{2,1,0:T(8,128)(2,1)S(1)}, u32[]{:S(2)}, u32[]{:S(2)}) async-start(bf16[16,16,1024]{2,1,0:T(8,128)(2,1)} %shard_map.92), calls=%async_computation | async-start | bytes 1048576 | tf_op jit(solution)/shard_map/all_to_all | solution.py:213
  9.9 9.1 %collective-permute-start = (bf16[448,512]{1,0:T(8,128)(2,1)}, bf16[448,512]{1,0:T(8,128)(2,1)S(1)}, u32[]{:S(2)}, u32[]{:S(2)}) collective-permute-start(bf16[448,512]{1,0:T(8,128)(2,1)} %bitcast.4), channel_id=1, source_target_pairs={{0,1},{1,0},{2,3},{3,2},{4,5},{5,4},{6,7},{7,6},{8,9},{9,8},{10,11... | collective-permute-start | bytes 1376264 | tf_op jit(solution)/shard_map/ppermute | solution.py:210
  14.7 4.4 %collective-permute-start.1 = (bf16[448,512]{1,0:T(8,128)(2,1)}, bf16[448,512]{1,0:T(8,128)(2,1)S(1)}, u32[]{:S(2)}, u32[]{:S(2)}) collective-permute-start(bf16[448,512]{1,0:T(8,128)(2,1)} %bitcast.6), channel_id=1, source_target_pairs={{0,1},{1,0},{2,3},{3,2},{4,5},{5,4},{6,7},{7,6},{8,9},{9,8},{10,11... | collective-permute-start | bytes 1376264 | tf_op jit(solution)/shard_map/ppermute | solution.py:210
  16.7 4.0 %collective-permute-start.2 = (bf16[448,512]{1,0:T(8,128)(2,1)}, bf16[448,512]{1,0:T(8,128)(2,1)S(1)}, u32[]{:S(2)}, u32[]{:S(2)}) collective-permute-start(bf16[448,512]{1,0:T(8,128)(2,1)} %down.1), channel_id=1, source_target_pairs={{0,1},{1,0},{2,3},{3,2},{4,5},{5,4},{6,7},{7,6},{8,9},{9,8},{10,11... | collective-permute-start | bytes 1376264 | tf_op jit(solution)/shard_map/ppermute | solution.py:210
  20.9 1.2 copy-start
  22.1 1.5 %copy-start.1 = (bf16[1792,512]{1,0:T(8,128)(2,1)S(1)}, bf16[1792,512]{1,0:T(8,128)(2,1)}, u32[]{:S(2)}) copy-start(bf16[1792,512]{1,0:T(8,128)(2,1)} %copy-done) | copy-start | bytes 5505028
  25.1 13.4 %collective-permute-start.3 = (bf16[64,2688]{1,0:T(8,128)(2,1)S(1)}, bf16[64,2688]{1,0:T(8,128)(2,1)S(1)}, u32[]{:S(2)}, u32[]{:S(2)}) collective-permute-start(bf16[64,2688]{1,0:T(8,128)(2,1)S(1)} %get-tuple-element.36), channel_id=1, source_target_pairs={{0,8},{1,121},{2,10},{3,123},{4,12},{5,125},{6,14},{7,127},{8,16},... | collective-permute-start | bytes 1032200 | tf_op jit(solution)/shard_map/ppermute | solution.py:205
  34.3 10.8 %collective-permute-start.4 = (bf16[64,2688]{1,0:T(8,128)(2,1)S(1)}, bf16[64,2688]{1,0:T(8,128)(2,1)S(1)}, u32[]{:S(2)}, u32[]{:S(2)}) collective-permute-start(bf16[64,2688]{1,0:T(8,128)(2,1)S(1)} %get-tuple-element.37), channel_id=1, source_target_pairs={{0,120},{1,9},{2,122},{3,11},{4,124},{5,13},{6,126},{7,15},{8,0},{... | collective-permute-start | bytes 1032200 | tf_op jit(solution)/shard_map/ppermute | solution.py:205
  36.3 15.3 %collective-permute-start.5 = (bf16[64,2688]{1,0:T(8,128)(2,1)S(1)}, bf16[64,2688]{1,0:T(8,128)(2,1)S(1)}, u32[]{:S(2)}, u32[]{:S(2)}) collective-permute-start(bf16[64,2688]{1,0:T(8,128)(2,1)S(1)} %get-tuple-element.38), channel_id=1, source_target_pairs={{0,112},{1,17},{2,114},{3,19},{4,116},{5,21},{6,118},{7,23},{8,120... | collective-permute-start | bytes 1032200 | tf_op jit(solution)/shard_map/ppermute | solution.py:205
  52.0 19.0 %collective-permute-start.6 = (bf16[16,2688]{1,0:T(8,128)(2,1)S(1)}, bf16[16,2688]{1,0:T(8,128)(2,1)S(1)}, u32[]{:S(2)}, u32[]{:S(2)}) collective-permute-start(bf16[16,2688]{1,0:T(8,128)(2,1)S(1)} %get-tuple-element.40), channel_id=1, source_target_pairs={{0,64},{1,65},{2,66},{3,67},{4,68},{5,69},{6,70},{7,71},{8,72},{9,... | collective-permute-start | bytes 258056 | tf_op jit(solution)/shard_map/ppermute | solution.py:205
  59.7 14.0 %collective-permute-start.7 = (bf16[16,2688]{1,0:T(8,128)(2,1)S(1)}, bf16[16,2688]{1,0:T(8,128)(2,1)S(1)}, u32[]{:S(2)}, u32[]{:S(2)}) collective-permute-start(bf16[16,2688]{1,0:T(8,128)(2,1)S(1)} %get-tuple-element.41), channel_id=1, source_target_pairs={{0,32},{1,97},{2,34},{3,99},{4,36},{5,101},{6,38},{7,103},{8,40},{... | collective-permute-start | bytes 258056 | tf_op jit(solution)/shard_map/ppermute | solution.py:205
  61.7 12.1 %collective-permute-start.8 = (bf16[16,2688]{1,0:T(8,128)(2,1)S(1)}, bf16[16,2688]{1,0:T(8,128)(2,1)S(1)}, u32[]{:S(2)}, u32[]{:S(2)}) collective-permute-start(bf16[16,2688]{1,0:T(8,128)(2,1)S(1)} %get-tuple-element.42), channel_id=1, source_target_pairs={{0,96},{1,33},{2,98},{3,35},{4,100},{5,37},{6,102},{7,39},{8,104},... | collective-permute-start | bytes 258056 | tf_op jit(solution)/shard_map/ppermute | solution.py:205
  92.6 14.3 %collective-permute-start.11 = (bf16[64,2688]{1,0:T(8,128)(2,1)S(1)}, bf16[64,2688]{1,0:T(8,128)(2,1)S(1)}, u32[]{:S(2)}, u32[]{:S(2)}) collective-permute-start(bf16[64,2688]{1,0:T(8,128)(2,1)S(1)} %all_gather.3.c0), channel_id=1, source_target_pairs={{0,16},{1,113},{2,18},{3,115},{4,20},{5,117},{6,22},{7,119},{8,24}... | collective-permute-start | bytes 1032200 | tf_op jit(solution)/shard_map/ppermute | solution.py:205
  99.1 16.9 %collective-permute-start.10 = (bf16[64,2688]{1,0:T(8,128)(2,1)S(1)}, bf16[64,2688]{1,0:T(8,128)(2,1)S(1)}, u32[]{:S(2)}, u32[]{:S(2)}) collective-permute-start(bf16[64,2688]{1,0:T(8,128)(2,1)S(1)} %all_gather.3.c0), channel_id=1, source_target_pairs={{0,120},{1,9},{2,122},{3,11},{4,124},{5,13},{6,126},{7,15},{8,0},{... | collective-permute-start | bytes 1032200 | tf_op jit(solution)/shard_map/ppermute | solution.py:205
  104.0 12.0 %collective-permute-start.9 = (bf16[64,2688]{1,0:T(8,128)(2,1)S(1)}, bf16[64,2688]{1,0:T(8,128)(2,1)S(1)}, u32[]{:S(2)}, u32[]{:S(2)}) collective-permute-start(bf16[64,2688]{1,0:T(8,128)(2,1)S(1)} %all_gather.3.c0), channel_id=1, source_target_pairs={{0,8},{1,121},{2,10},{3,123},{4,12},{5,125},{6,14},{7,127},{8,16},... | collective-permute-start | bytes 1032200 | tf_op jit(solution)/shard_map/ppermute | solution.py:205
  117.7 19.1 %all-to-all-start.1 = ((bf16[16,16,1024]{2,1,0:T(8,128)(2,1)}), bf16[16,16,1024]{2,1,0:T(8,128)(2,1)S(1)}, u32[]{:S(2)}, u32[]{:S(2)}) async-start(bf16[16,16,1024]{2,1,0:T(8,128)(2,1)} %shard_map.97), calls=%async_computation.1 | async-start | bytes 1048576 | tf_op jit(solution)/shard_map/all_to_all | solution.py:213
  123.9 9.7 %collective-permute-start.12 = (bf16[448,512]{1,0:T(8,128)(2,1)S(1)}, bf16[448,512]{1,0:T(8,128)(2,1)S(1)}, u32[]{:S(2)}, u32[]{:S(2)}) collective-permute-start(bf16[448,512]{1,0:T(8,128)(2,1)S(1)} %get-tuple-element.51), channel_id=1, source_target_pairs={{0,1},{1,0},{2,3},{3,2},{4,5},{5,4},{6,7},{7,6},{8,9},{9,8},{10,11... | collective-permute-start | bytes 1376264 | tf_op jit(solution)/shard_map/ppermute | solution.py:210
  129.3 4.4 %collective-permute-start.13 = (bf16[448,512]{1,0:T(8,128)(2,1)S(1)}, bf16[448,512]{1,0:T(8,128)(2,1)S(1)}, u32[]{:S(2)}, u32[]{:S(2)}) collective-permute-start(bf16[448,512]{1,0:T(8,128)(2,1)S(1)} %get-tuple-element.52), channel_id=1, source_target_pairs={{0,1},{1,0},{2,3},{3,2},{4,5},{5,4},{6,7},{7,6},{8,9},{9,8},{10,11... | collective-permute-start | bytes 1376264 | tf_op jit(solution)/shard_map/ppermute | solution.py:210
  131.2 3.8 %collective-permute-start.14 = (bf16[448,512]{1,0:T(8,128)(2,1)S(1)}, bf16[448,512]{1,0:T(8,128)(2,1)S(1)}, u32[]{:S(2)}, u32[]{:S(2)}) collective-permute-start(bf16[448,512]{1,0:T(8,128)(2,1)S(1)} %get-tuple-element.53), channel_id=1, source_target_pairs={{0,1},{1,0},{2,3},{3,2},{4,5},{5,4},{6,7},{7,6},{8,9},{9,8},{10,11... | collective-permute-start | bytes 1376264 | tf_op jit(solution)/shard_map/ppermute | solution.py:210

commit v7 on v6

--- a/solution.py
+++ b/solution.py
@@ -131,20 +131,29 @@
     out[:, 2 * ff :] = (gate_sum * sig * up_sum).astype(BF)
 
 
-def outward(c2, c1, c3, c0, pair, down, out, rows_of):
+def products(rows_of, pair, down, out):
     both, width = pair.shape
+    out[:, :width] = nn(rows_of[:, both:], down[...]).astype(BF)
+    out[:, width:] = nn(rows_of[:, :both], pair[...]).astype(BF)
+
+
+def outward_early(c1, c3, c0, pair, down, out, rows_of):
+    block = c0.shape[0]
+    for slot, c in enumerate((c3, c1, c0)):
+        rows_of[slot * block : (slot + 1) * block, :] = c[...]
+    products(rows_of, pair, down, out)
+
+
+def outward(c2, early, pair, down, out, last):
     rows = out.shape[1]
-    block = c0.shape[0]
-    for at, c in ((2, c2), (1, c1), (3, c3), (0, c0)):
-        rows_of[at * block : (at + 1) * block, :] = c[...]
-    layer = nn(rows_of[:, both:], down[...]).astype(BF)
-    back = nn(rows_of[:, :both], pair[...]).astype(BF)
-    for at in range(4):
+    block = c2.shape[0]
+    for slot, at in enumerate((3, 1, 0)):
         for j in range(4):
-            here = slice(at * block + j * rows, at * block + (j + 1) * rows)
-            chunk = chunk_of(at, j)
-            out[chunk, :, :width] = layer[here, :]
-            out[chunk, :, width:] = back[here, :]
+            here = slot * block + j * rows
+            out[chunk_of(at, j)] = early[here : here + rows, :]
+    products(c2, pair, down, last)
+    for j in range(4):
+        out[chunk_of(2, j)] = last[j * rows : (j + 1) * rows, :]
 
 
 def weight_part(start, kind, c0, c1, c2, c3, ordered, part):
@@ -243,14 +252,22 @@
     c3 = shift(c0, NEAR[3])
     c1 = shift(c0, NEAR[1])
     c2 = shift(c0, NEAR[2])
+    (early,) = call(
+        outward_early,
+        [((3 * block, 2 * width), BF)],
+        0,
+        5,
+        [pltpu.VMEM((3 * block, wide), BF)],
+        mib=8,
+    )(c1, c3, c0, pair, down)
     (out,) = call(
         outward,
         [((chips, rows, 2 * width), BF)],
         0,
-        6,
-        [pltpu.VMEM((4 * block, wide), BF)],
+        4,
+        [pltpu.VMEM((block, 2 * width), BF)],
         mib=8,
-    )(c2, c1, c3, c0, pair, down)
+    )(c2, early, pair, down)
     out, c0, c1, c2, c3 = lax.optimization_barrier((out, c0, c1, c2, c3))
     parts = exchange(out)
     window = [pltpu.VMEM((4 * block, -(-ff // 128) * 128), BF)]

time: 138 us -> 138 us (level)
  no operation moved by 1% of the time
where the time goes in v7:
time: 138 us; the launch traced here: 137 us
  starting transfers between devices  74.4 us (54%)
  waiting for transfers between devices  31.2 us (23%)
  blocking collectives  18.7 us (14%)
  Pallas kernels  8.35 us (6%)
  local copies, waits for them, and re-layouts  2.76 us (2%)
    ppermute x9, starting transfers between devices, shift(): return lax.ppermute(x, ('col', 'depth'), pairs)  43.3 us
    ppermute x9, waiting for transfers between devices, shift(): return lax.ppermute(x, ('col', 'depth'), pairs)  28.2 us
    all_gather x1, blocking collectives, shards(): lax.all_gather(act, 'col', axis=0, tiled=True, axis_index_groups=strided)  18.7 us
    ppermute x6, starting transfers between devices, swap(): return lax.ppermute(x, 'depth', [(d, d ^ 1) for d in range(depth)])  18 us
    all_to_all x2, starting transfers between devices, exchange(): lax.all_to_all(x, GROUP, 0, 0, tiled=True, axis_index_groups=same_core)  13.1 us
    ppermute x6, waiting for transfers between devices, swap(): return lax.ppermute(x, 'depth', [(d, d ^ 1) for d in range(depth)])  3.02 us
  transfers between devices with their start and end apart: 17, of which 9 were waited for; matrix products, arithmetic and copies ran while one was open for 0% of the time, Pallas kernels for 2%

profile of v7, /device:TPU:1, one launch (start us, length us, event | category | flops | bytes accessed | tf_op | source)
XLA Modules:
  0.0 137.2 jit_solution(11879768773258252912)
XLA Ops:
  0.6 0.0 copy-start.2
  0.6 0.0 copy-start.3
  0.7 0.0 copy-start.4
  0.7 0.8 pad_maximum_fusion.both
  1.5 0.8 shard_map.92
  2.3 7.6 %all-to-all-start = ((bf16[16,16,1024]{2,1,0:T(8,128)(2,1)}), bf16[16,16,1024]{2,1,0:T(8,128)(2,1)S(1)}, u32[]{:S(2)}, u32[]{:S(2)}) async-start(bf16[16,16,1024]{2,1,0:T(8,128)(2,1)} %shard_map.92), calls=%async_computation | async-start | bytes 1048576 | tf_op jit(solution)/shard_map/all_to_all | solution.py:222
  9.9 4.8 %collective-permute-start = (bf16[448,512]{1,0:T(8,128)(2,1)}, bf16[448,512]{1,0:T(8,128)(2,1)S(1)}, u32[]{:S(2)}, u32[]{:S(2)}) collective-permute-start(bf16[448,512]{1,0:T(8,128)(2,1)} %bitcast.4), channel_id=1, source_target_pairs={{0,1},{1,0},{2,3},{3,2},{4,5},{5,4},{6,7},{7,6},{8,9},{9,8},{10,11... | collective-permute-start | bytes 1376264 | tf_op jit(solution)/shard_map/ppermute | solution.py:219
  14.7 1.9 %collective-permute-start.1 = (bf16[448,512]{1,0:T(8,128)(2,1)}, bf16[448,512]{1,0:T(8,128)(2,1)S(1)}, u32[]{:S(2)}, u32[]{:S(2)}) collective-permute-start(bf16[448,512]{1,0:T(8,128)(2,1)} %bitcast.6), channel_id=1, source_target_pairs={{0,1},{1,0},{2,3},{3,2},{4,5},{5,4},{6,7},{7,6},{8,9},{9,8},{10,11... | collective-permute-start | bytes 1376264 | tf_op jit(solution)/shard_map/ppermute | solution.py:219
  16.7 2.4 %collective-permute-start.2 = (bf16[448,512]{1,0:T(8,128)(2,1)}, bf16[448,512]{1,0:T(8,128)(2,1)S(1)}, u32[]{:S(2)}, u32[]{:S(2)}) collective-permute-start(bf16[448,512]{1,0:T(8,128)(2,1)} %down.1), channel_id=1, source_target_pairs={{0,1},{1,0},{2,3},{3,2},{4,5},{5,4},{6,7},{7,6},{8,9},{9,8},{10,11... | collective-permute-start | bytes 1376264 | tf_op jit(solution)/shard_map/ppermute | solution.py:219
  19.1 0.0 collective-permute-done.gate_away
  19.1 0.0 collective-permute-done.1.up_away
  19.1 1.6 %collective-permute-done.2.down_away = bf16[448,512]{1,0:T(8,128)(2,1)S(1)} collective-permute-done((bf16[448,512]{1,0:T(8,128)(2,1)}, bf16[448,512]{1,0:T(8,128)(2,1)S(1)}, u32[]{:S(2)}, u32[]{:S(2)}) %collective-permute-start.2) | collective-permute-done | bytes 458784 | tf_op jit(solution)/shard_map/ppermute | solution.py:219
  20.7 0.0 copy-done.2
  20.7 0.0 copy-done.3
  20.7 0.0 copy-done.4
  20.7 0.2 shard_map.93
  20.9 0.0 copy-start
  20.9 1.2 copy-done
  22.1 0.0 all-to-all-done.mine
  22.1 0.0 copy-start.1
  22.1 1.5 %copy-done.1 = bf16[1792,512]{1,0:T(8,128)(2,1)S(1)} copy-done((bf16[1792,512]{1,0:T(8,128)(2,1)S(1)}, bf16[1792,512]{1,0:T(8,128)(2,1)}, u32[]{:S(2)}) %copy-start.1) | copy-done | bytes 1835032
  23.6 1.5 %shard_map.94 = (bf16[64,2688]{1,0:T(8,128)(2,1)S(1)}, bf16[64,2688]{1,0:T(8,128)(2,1)S(1)}, bf16[64,2688]{1,0:T(8,128)(2,1)S(1)}, f32[64,2688]{1,0:T(8,128)S(1)...) custom-call(bf16[16,16,1024]{2,1,0:T(8,128)(2,1)S(1)} %all-to-all-done.mine, ...), custom_call_target="tpu_custom_call" | custom-call | tf_op jit(solution)/shard_map/pallas_call | solution.py:231
  25.1 9.2 %collective-permute-start.3 = (bf16[64,2688]{1,0:T(8,128)(2,1)S(1)}, bf16[64,2688]{1,0:T(8,128)(2,1)S(1)}, u32[]{:S(2)}, u32[]{:S(2)}) collective-permute-start(bf16[64,2688]{1,0:T(8,128)(2,1)S(1)} %get-tuple-element.36), channel_id=1, source_target_pairs={{0,8},{1,121},{2,10},{3,123},{4,12},{5,125},{6,14},{7,127},{8,16},... | collective-permute-start | bytes 1032200 | tf_op jit(solution)/shard_map/ppermute | solution.py:214
  34.3 1.9 %collective-permute-start.4 = (bf16[64,2688]{1,0:T(8,128)(2,1)S(1)}, bf16[64,2688]{1,0:T(8,128)(2,1)S(1)}, u32[]{:S(2)}, u32[]{:S(2)}) collective-permute-start(bf16[64,2688]{1,0:T(8,128)(2,1)S(1)} %get-tuple-element.37), channel_id=1, source_target_pairs={{0,120},{1,9},{2,122},{3,11},{4,124},{5,13},{6,126},{7,15},{8,0},{... | collective-permute-start | bytes 1032200 | tf_op jit(solution)/shard_map/ppermute | solution.py:214
  36.3 1.9 %collective-permute-start.5 = (bf16[64,2688]{1,0:T(8,128)(2,1)S(1)}, bf16[64,2688]{1,0:T(8,128)(2,1)S(1)}, u32[]{:S(2)}, u32[]{:S(2)}) collective-permute-start(bf16[64,2688]{1,0:T(8,128)(2,1)S(1)} %get-tuple-element.38), channel_id=1, source_target_pairs={{0,112},{1,17},{2,114},{3,19},{4,116},{5,21},{6,118},{7,23},{8,120... | collective-permute-start | bytes 1032200 | tf_op jit(solution)/shard_map/ppermute | solution.py:214
  38.2 0.3 collective-permute-done.3.first
  38.5 6.6 %collective-permute-done.4.second = bf16[64,2688]{1,0:T(8,128)(2,1)S(1)} collective-permute-done((bf16[64,2688]{1,0:T(8,128)(2,1)S(1)}, bf16[64,2688]{1,0:T(8,128)(2,1)S(1)}, u32[]{:S(2)}, u32[]{:S(2)}) %collective-permute-start.4) | collective-permute-done | bytes 344096 | tf_op jit(solution)/shard_map/ppermute | solution.py:214
  45.1 6.5 %collective-permute-done.5.third = bf16[64,2688]{1,0:T(8,128)(2,1)S(1)} collective-permute-done((bf16[64,2688]{1,0:T(8,128)(2,1)S(1)}, bf16[64,2688]{1,0:T(8,128)(2,1)S(1)}, u32[]{:S(2)}, u32[]{:S(2)}) %collective-permute-start.5) | collective-permute-done | bytes 344096 | tf_op jit(solution)/shard_map/ppermute | solution.py:214
  51.6 0.4 shard_map.95
  52.0 7.7 %collective-permute-start.6 = (bf16[16,2688]{1,0:T(8,128)(2,1)S(1)}, bf16[16,2688]{1,0:T(8,128)(2,1)S(1)}, u32[]{:S(2)}, u32[]{:S(2)}) collective-permute-start(bf16[16,2688]{1,0:T(8,128)(2,1)S(1)} %get-tuple-element.40), channel_id=1, source_target_pairs={{0,64},{1,65},{2,66},{3,67},{4,68},{5,69},{6,70},{7,71},{8,72},{9,... | collective-permute-start | bytes 258056 | tf_op jit(solution)/shard_map/ppermute | solution.py:214
  59.7 1.9 %collective-permute-start.7 = (bf16[16,2688]{1,0:T(8,128)(2,1)S(1)}, bf16[16,2688]{1,0:T(8,128)(2,1)S(1)}, u32[]{:S(2)}, u32[]{:S(2)}) collective-permute-start(bf16[16,2688]{1,0:T(8,128)(2,1)S(1)} %get-tuple-element.41), channel_id=1, source_target_pairs={{0,32},{1,97},{2,34},{3,99},{4,36},{5,101},{6,38},{7,103},{8,40},{... | collective-permute-start | bytes 258056 | tf_op jit(solution)/shard_map/ppermute | solution.py:214
  61.7 7.3 %collective-permute-start.8 = (bf16[16,2688]{1,0:T(8,128)(2,1)S(1)}, bf16[16,2688]{1,0:T(8,128)(2,1)S(1)}, u32[]{:S(2)}, u32[]{:S(2)}) collective-permute-start(bf16[16,2688]{1,0:T(8,128)(2,1)S(1)} %get-tuple-element.42), channel_id=1, source_target_pairs={{0,96},{1,33},{2,98},{3,35},{4,100},{5,37},{6,102},{7,39},{8,104},... | collective-permute-start | bytes 258056 | tf_op jit(solution)/shard_map/ppermute | solution.py:214
  69.0 2.1 %collective-permute-done.6.far = bf16[16,2688]{1,0:T(8,128)(2,1)S(1)} collective-permute-done((bf16[16,2688]{1,0:T(8,128)(2,1)S(1)}, bf16[16,2688]{1,0:T(8,128)(2,1)S(1)}, u32[]{:S(2)}, u32[]{:S(2)}) %collective-permute-start.6) | collective-permute-done | bytes 86048 | tf_op jit(solution)/shard_map/ppermute | solution.py:214
  71.1 2.7 %collective-permute-done.7.near = bf16[16,2688]{1,0:T(8,128)(2,1)S(1)} collective-permute-done((bf16[16,2688]{1,0:T(8,128)(2,1)S(1)}, bf16[16,2688]{1,0:T(8,128)(2,1)S(1)}, u32[]{:S(2)}, u32[]{:S(2)}) %collective-permute-start.7) | collective-permute-done | bytes 86048 | tf_op jit(solution)/shard_map/ppermute | solution.py:214
  73.7 0.0 collective-permute-done.8.back
  73.7 0.1 shard_map.96
  73.9 18.7 %all_gather.3.c0 = bf16[64,2688]{1,0:T(8,128)(2,1)S(1)} all-gather(bf16[16,2688]{1,0:T(8,128)(2,1)S(1)} %shard_map.96), channel_id=1, replica_groups={{0,32,64,96},{8,40,72,104},{16,48,80,112},{24,56,88,120},{1,33,65,97},{..., dimensions={0}, use_global_device_ids=true | all-gather | bytes 430080 | tf_op jit(solution)/shard_map/all_gather | solution.py:251
  92.6 6.5 %collective-permute-start.11 = (bf16[64,2688]{1,0:T(8,128)(2,1)S(1)}, bf16[64,2688]{1,0:T(8,128)(2,1)S(1)}, u32[]{:S(2)}, u32[]{:S(2)}) collective-permute-start(bf16[64,2688]{1,0:T(8,128)(2,1)S(1)} %all_gather.3.c0), channel_id=1, source_target_pairs={{0,16},{1,113},{2,18},{3,115},{4,20},{5,117},{6,22},{7,119},{8,24}... | collective-permute-start | bytes 1032200 | tf_op jit(solution)/shard_map/ppermute | solution.py:214
  99.1 4.9 %collective-permute-start.10 = (bf16[64,2688]{1,0:T(8,128)(2,1)S(1)}, bf16[64,2688]{1,0:T(8,128)(2,1)S(1)}, u32[]{:S(2)}, u32[]{:S(2)}) collective-permute-start(bf16[64,2688]{1,0:T(8,128)(2,1)S(1)} %all_gather.3.c0), channel_id=1, source_target_pairs={{0,120},{1,9},{2,122},{3,11},{4,124},{5,13},{6,126},{7,15},{8,0},{... | collective-permute-start | bytes 1032200 | tf_op jit(solution)/shard_map/ppermute | solution.py:214
  104.0 2.0 %collective-permute-start.9 = (bf16[64,2688]{1,0:T(8,128)(2,1)S(1)}, bf16[64,2688]{1,0:T(8,128)(2,1)S(1)}, u32[]{:S(2)}, u32[]{:S(2)}) collective-permute-start(bf16[64,2688]{1,0:T(8,128)(2,1)S(1)} %all_gather.3.c0), channel_id=1, source_target_pairs={{0,8},{1,121},{2,10},{3,123},{4,12},{5,125},{6,14},{7,127},{8,16},... | collective-permute-start | bytes 1032200 | tf_op jit(solution)/shard_map/ppermute | solution.py:214
  106.0 0.9 collective-permute-done.11.c3
  106.9 9.1 %collective-permute-done.10.c1 = bf16[64,2688]{1,0:T(8,128)(2,1)S(1)} collective-permute-done((bf16[64,2688]{1,0:T(8,128)(2,1)S(1)}, bf16[64,2688]{1,0:T(8,128)(2,1)S(1)}, u32[]{:S(2)}, u32[]{:S(2)}) %collective-permute-start.10) | collective-permute-done | bytes 344096 | tf_op jit(solution)/shard_map/ppermute | solution.py:214
  116.0 0.7 shard_map.97.early
  116.8 0.0 collective-permute-done.9.c2
  116.8 1.4 %shard_map.98 = bf16[16,16,1024]{2,1,0:T(8,128)(2,1)} custom-call(bf16[64,2688]{1,0:T(8,128)(2,1)S(1)} %collective-permute-done.9.c2, bf16[192,1024]{1,0:T(8,128)(2,1)S(1)} %shard_map.97.early, bf16[1792,512]{1,0:T(8,128)(2,1)S(1)} %get-tuple-element.43.pair, bf16[896,512]{1,0:T(8,128)(2,1)S(1)} %get-tuple-element.44.down), custom_call_target="tpu_custom_call" | custom-call | tf_op jit(solution)/shard_map/pallas_call | solution.py:263
  118.2 5.5 %all-to-all-start.1 = ((bf16[16,16,1024]{2,1,0:T(8,128)(2,1)}), bf16[16,16,1024]{2,1,0:T(8,128)(2,1)S(1)}, u32[]{:S(2)}, u32[]{:S(2)}) async-start(bf16[16,16,1024]{2,1,0:T(8,128)(2,1)} %shard_map.98), calls=%async_computation.1 | async-start | bytes 1048576 | tf_op jit(solution)/shard_map/all_to_all | solution.py:222
  123.7 0.7 shard_map.99
  124.4 4.6 %collective-permute-start.12 = (bf16[448,512]{1,0:T(8,128)(2,1)S(1)}, bf16[448,512]{1,0:T(8,128)(2,1)S(1)}, u32[]{:S(2)}, u32[]{:S(2)}) collective-permute-start(bf16[448,512]{1,0:T(8,128)(2,1)S(1)} %get-tuple-element.51), channel_id=1, source_target_pairs={{0,1},{1,0},{2,3},{3,2},{4,5},{5,4},{6,7},{7,6},{8,9},{9,8},{10,11... | collective-permute-start | bytes 1376264 | tf_op jit(solution)/shard_map/ppermute | solution.py:219
  129.0 1.9 %collective-permute-start.13 = (bf16[448,512]{1,0:T(8,128)(2,1)S(1)}, bf16[448,512]{1,0:T(8,128)(2,1)S(1)}, u32[]{:S(2)}, u32[]{:S(2)}) collective-permute-start(bf16[448,512]{1,0:T(8,128)(2,1)S(1)} %get-tuple-element.52), channel_id=1, source_target_pairs={{0,1},{1,0},{2,3},{3,2},{4,5},{5,4},{6,7},{7,6},{8,9},{9,8},{10,11... | collective-permute-start | bytes 1376264 | tf_op jit(solution)/shard_map/ppermute | solution.py:219
  130.9 2.4 %collective-permute-start.14 = (bf16[448,512]{1,0:T(8,128)(2,1)S(1)}, bf16[448,512]{1,0:T(8,128)(2,1)S(1)}, u32[]{:S(2)}, u32[]{:S(2)}) collective-permute-start(bf16[448,512]{1,0:T(8,128)(2,1)S(1)} %get-tuple-element.53), channel_id=1, source_target_pairs={{0,1},{1,0},{2,3},{3,2},{4,5},{5,4},{6,7},{7,6},{8,9},{9,8},{10,11... | collective-permute-start | bytes 1376264 | tf_op jit(solution)/shard_map/ppermute | solution.py:219
  133.3 0.0 collective-permute-done.12.a0
  133.3 0.0 collective-permute-done.13.a1
  133.3 1.4 %collective-permute-done.14.a2 = bf16[448,512]{1,0:T(8,128)(2,1)S(1)} collective-permute-done((bf16[448,512]{1,0:T(8,128)(2,1)S(1)}, bf16[448,512]{1,0:T(8,128)(2,1)S(1)}, u32[]{:S(2)}, u32[]{:S(2)}) %collective-permute-start.14) | collective-permute-done | bytes 458784 | tf_op jit(solution)/shard_map/ppermute | solution.py:219
  134.7 1.8 %shard_map.100 = (bf16[448,512]{1,0:T(8,128)(2,1)}, bf16[448,512]{1,0:T(8,128)(2,1)}, bf16[448,512]{1,0:T(8,128)(2,1)}) custom-call(bf16[64,2688]{1,0:T(8,128)(2,1)S(1)} %all_gather.3.c0, bf16[64,2688]{1,0:T(8,128)(2,1)S(1)} %collective-permute-done.10.c1, bf16[64,2688]{1,0:T(8,128)(2,1)S(1)} %collective-permute-done.9.c2, ...), custom_call_target="tpu_custom_call" | custom-call | tf_op jit(solution)/shard_map/pallas_call | solution.py:276
  136.5 0.0 all-to-all-done.1.parts
  136.5 0.7 shard_map.101
Async XLA Ops:
  0.6 20.1 %copy-start.2 = (bf16[512,448]{0,1:T(8,128)(2,1)S(1)}, bf16[512,448]{0,1:T(8,128)(2,1)}, u32[]{:S(2)}) copy-start(bf16[512,448]{0,1:T(8,128)(2,1)} %param.7) | copy-start | bytes 1376260
  0.6 20.1 %copy-start.3 = (bf16[512,448]{0,1:T(8,128)(2,1)S(1)}, bf16[512,448]{0,1:T(8,128)(2,1)}, u32[]{:S(2)}) copy-start(bf16[512,448]{0,1:T(8,128)(2,1)} %param.8) | copy-start | bytes 1376260
  0.7 20.1 %copy-start.4 = (bf16[448,512]{1,0:T(8,128)(2,1)S(1)}, bf16[448,512]{1,0:T(8,128)(2,1)}, u32[]{:S(2)}) copy-start(bf16[448,512]{1,0:T(8,128)(2,1)} %down.1) | copy-start | bytes 1376260
  2.3 19.8 %all-to-all-start = ((bf16[16,16,1024]{2,1,0:T(8,128)(2,1)}), bf16[16,16,1024]{2,1,0:T(8,128)(2,1)S(1)}, u32[]{:S(2)}, u32[]{:S(2)}) async-start(bf16[16,16,1024]{2,1,0:T(8,128)(2,1)} %shard_map.92), calls=%async_computation | async-start | bytes 1048576 | tf_op jit(solution)/shard_map/all_to_all | solution.py:222
  9.9 9.1 %collective-permute-start = (bf16[448,512]{1,0:T(8,128)(2,1)}, bf16[448,512]{1,0:T(8,128)(2,1)S(1)}, u32[]{:S(2)}, u32[]{:S(2)}) collective-permute-start(bf16[448,512]{1,0:T(8,128)(2,1)} %bitcast.4), channel_id=1, source_target_pairs={{0,1},{1,0},{2,3},{3,2},{4,5},{5,4},{6,7},{7,6},{8,9},{9,8},{10,11... | collective-permute-start | bytes 1376264 | tf_op jit(solution)/shard_map/ppermute | solution.py:219
  14.7 4.4 %collective-permute-start.1 = (bf16[448,512]{1,0:T(8,128)(2,1)}, bf16[448,512]{1,0:T(8,128)(2,1)S(1)}, u32[]{:S(2)}, u32[]{:S(2)}) collective-permute-start(bf16[448,512]{1,0:T(8,128)(2,1)} %bitcast.6), channel_id=1, source_target_pairs={{0,1},{1,0},{2,3},{3,2},{4,5},{5,4},{6,7},{7,6},{8,9},{9,8},{10,11... | collective-permute-start | bytes 1376264 | tf_op jit(solution)/shard_map/ppermute | solution.py:219
  16.7 4.0 %collective-permute-start.2 = (bf16[448,512]{1,0:T(8,128)(2,1)}, bf16[448,512]{1,0:T(8,128)(2,1)S(1)}, u32[]{:S(2)}, u32[]{:S(2)}) collective-permute-start(bf16[448,512]{1,0:T(8,128)(2,1)} %down.1), channel_id=1, source_target_pairs={{0,1},{1,0},{2,3},{3,2},{4,5},{5,4},{6,7},{7,6},{8,9},{9,8},{10,11... | collective-permute-start | bytes 1376264 | tf_op jit(solution)/shard_map/ppermute | solution.py:219
  20.9 1.2 copy-start
  22.1 1.5 %copy-start.1 = (bf16[1792,512]{1,0:T(8,128)(2,1)S(1)}, bf16[1792,512]{1,0:T(8,128)(2,1)}, u32[]{:S(2)}) copy-start(bf16[1792,512]{1,0:T(8,128)(2,1)} %copy-done) | copy-start | bytes 5505028
  25.1 13.4 %collective-permute-start.3 = (bf16[64,2688]{1,0:T(8,128)(2,1)S(1)}, bf16[64,2688]{1,0:T(8,128)(2,1)S(1)}, u32[]{:S(2)}, u32[]{:S(2)}) collective-permute-start(bf16[64,2688]{1,0:T(8,128)(2,1)S(1)} %get-tuple-element.36), channel_id=1, source_target_pairs={{0,8},{1,121},{2,10},{3,123},{4,12},{5,125},{6,14},{7,127},{8,16},... | collective-permute-start | bytes 1032200 | tf_op jit(solution)/shard_map/ppermute | solution.py:214
  34.3 10.8 %collective-permute-start.4 = (bf16[64,2688]{1,0:T(8,128)(2,1)S(1)}, bf16[64,2688]{1,0:T(8,128)(2,1)S(1)}, u32[]{:S(2)}, u32[]{:S(2)}) collective-permute-start(bf16[64,2688]{1,0:T(8,128)(2,1)S(1)} %get-tuple-element.37), channel_id=1, source_target_pairs={{0,120},{1,9},{2,122},{3,11},{4,124},{5,13},{6,126},{7,15},{8,0},{... | collective-permute-start | bytes 1032200 | tf_op jit(solution)/shard_map/ppermute | solution.py:214
  36.3 15.3 %collective-permute-start.5 = (bf16[64,2688]{1,0:T(8,128)(2,1)S(1)}, bf16[64,2688]{1,0:T(8,128)(2,1)S(1)}, u32[]{:S(2)}, u32[]{:S(2)}) collective-permute-start(bf16[64,2688]{1,0:T(8,128)(2,1)S(1)} %get-tuple-element.38), channel_id=1, source_target_pairs={{0,112},{1,17},{2,114},{3,19},{4,116},{5,21},{6,118},{7,23},{8,120... | collective-permute-start | bytes 1032200 | tf_op jit(solution)/shard_map/ppermute | solution.py:214
  52.0 19.0 %collective-permute-start.6 = (bf16[16,2688]{1,0:T(8,128)(2,1)S(1)}, bf16[16,2688]{1,0:T(8,128)(2,1)S(1)}, u32[]{:S(2)}, u32[]{:S(2)}) collective-permute-start(bf16[16,2688]{1,0:T(8,128)(2,1)S(1)} %get-tuple-element.40), channel_id=1, source_target_pairs={{0,64},{1,65},{2,66},{3,67},{4,68},{5,69},{6,70},{7,71},{8,72},{9,... | collective-permute-start | bytes 258056 | tf_op jit(solution)/shard_map/ppermute | solution.py:214
  59.7 14.0 %collective-permute-start.7 = (bf16[16,2688]{1,0:T(8,128)(2,1)S(1)}, bf16[16,2688]{1,0:T(8,128)(2,1)S(1)}, u32[]{:S(2)}, u32[]{:S(2)}) collective-permute-start(bf16[16,2688]{1,0:T(8,128)(2,1)S(1)} %get-tuple-element.41), channel_id=1, source_target_pairs={{0,32},{1,97},{2,34},{3,99},{4,36},{5,101},{6,38},{7,103},{8,40},{... | collective-permute-start | bytes 258056 | tf_op jit(solution)/shard_map/ppermute | solution.py:214
  61.7 12.1 %collective-permute-start.8 = (bf16[16,2688]{1,0:T(8,128)(2,1)S(1)}, bf16[16,2688]{1,0:T(8,128)(2,1)S(1)}, u32[]{:S(2)}, u32[]{:S(2)}) collective-permute-start(bf16[16,2688]{1,0:T(8,128)(2,1)S(1)} %get-tuple-element.42), channel_id=1, source_target_pairs={{0,96},{1,33},{2,98},{3,35},{4,100},{5,37},{6,102},{7,39},{8,104},... | collective-permute-start | bytes 258056 | tf_op jit(solution)/shard_map/ppermute | solution.py:214
  92.6 14.3 %collective-permute-start.11 = (bf16[64,2688]{1,0:T(8,128)(2,1)S(1)}, bf16[64,2688]{1,0:T(8,128)(2,1)S(1)}, u32[]{:S(2)}, u32[]{:S(2)}) collective-permute-start(bf16[64,2688]{1,0:T(8,128)(2,1)S(1)} %all_gather.3.c0), channel_id=1, source_target_pairs={{0,16},{1,113},{2,18},{3,115},{4,20},{5,117},{6,22},{7,119},{8,24}... | collective-permute-start | bytes 1032200 | tf_op jit(solution)/shard_map/ppermute | solution.py:214
  99.1 16.9 %collective-permute-start.10 = (bf16[64,2688]{1,0:T(8,128)(2,1)S(1)}, bf16[64,2688]{1,0:T(8,128)(2,1)S(1)}, u32[]{:S(2)}, u32[]{:S(2)}) collective-permute-start(bf16[64,2688]{1,0:T(8,128)(2,1)S(1)} %all_gather.3.c0), channel_id=1, source_target_pairs={{0,120},{1,9},{2,122},{3,11},{4,124},{5,13},{6,126},{7,15},{8,0},{... | collective-permute-start | bytes 1032200 | tf_op jit(solution)/shard_map/ppermute | solution.py:214
  104.0 12.8 %collective-permute-start.9 = (bf16[64,2688]{1,0:T(8,128)(2,1)S(1)}, bf16[64,2688]{1,0:T(8,128)(2,1)S(1)}, u32[]{:S(2)}, u32[]{:S(2)}) collective-permute-start(bf16[64,2688]{1,0:T(8,128)(2,1)S(1)} %all_gather.3.c0), channel_id=1, source_target_pairs={{0,8},{1,121},{2,10},{3,123},{4,12},{5,125},{6,14},{7,127},{8,16},... | collective-permute-start | bytes 1032200 | tf_op jit(solution)/shard_map/ppermute | solution.py:214
  118.2 18.3 %all-to-all-start.1 = ((bf16[16,16,1024]{2,1,0:T(8,128)(2,1)}), bf16[16,16,1024]{2,1,0:T(8,128)(2,1)S(1)}, u32[]{:S(2)}, u32[]{:S(2)}) async-start(bf16[16,16,1024]{2,1,0:T(8,128)(2,1)} %shard_map.98), calls=%async_computation.1 | async-start | bytes 1048576 | tf_op jit(solution)/shard_map/all_to_all | solution.py:222
  124.4 8.9 %collective-permute-start.12 = (bf16[448,512]{1,0:T(8,128)(2,1)S(1)}, bf16[448,512]{1,0:T(8,128)(2,1)S(1)}, u32[]{:S(2)}, u32[]{:S(2)}) collective-permute-start(bf16[448,512]{1,0:T(8,128)(2,1)S(1)} %get-tuple-element.51), channel_id=1, source_target_pairs={{0,1},{1,0},{2,3},{3,2},{4,5},{5,4},{6,7},{7,6},{8,9},{9,8},{10,11... | collective-permute-start | bytes 1376264 | tf_op jit(solution)/shard_map/ppermute | solution.py:219
  129.0 4.4 %collective-permute-start.13 = (bf16[448,512]{1,0:T(8,128)(2,1)S(1)}, bf16[448,512]{1,0:T(8,128)(2,1)S(1)}, u32[]{:S(2)}, u32[]{:S(2)}) collective-permute-start(bf16[448,512]{1,0:T(8,128)(2,1)S(1)} %get-tuple-element.52), channel_id=1, source_target_pairs={{0,1},{1,0},{2,3},{3,2},{4,5},{5,4},{6,7},{7,6},{8,9},{9,8},{10,11... | collective-permute-start | bytes 1376264 | tf_op jit(solution)/shard_map/ppermute | solution.py:219
  130.9 3.8 %collective-permute-start.14 = (bf16[448,512]{1,0:T(8,128)(2,1)S(1)}, bf16[448,512]{1,0:T(8,128)(2,1)S(1)}, u32[]{:S(2)}, u32[]{:S(2)}) collective-permute-start(bf16[448,512]{1,0:T(8,128)(2,1)S(1)} %get-tuple-element.53), channel_id=1, source_target_pairs={{0,1},{1,0},{2,3},{3,2},{4,5},{5,4},{6,7},{7,6},{8,9},{9,8},{10,11... | collective-permute-start | bytes 1376264 | tf_op jit(solution)/shard_map/ppermute | solution.py:219

commit v8 on v7

--- a/solution.py
+++ b/solution.py
@@ -276,7 +276,6 @@
     gate_g, up_g, down_g = call(
         functools.partial(weight_own, 1.0 / math.sqrt(total)), grads, 0, 8, window, mib=8
     )(c0, c1, c2, c3, ordered, *[swap(x) for x in away])
-    parts, gate_g = lax.optimization_barrier((parts, gate_g))
     layer_out, tokens_grad = call(last_sum, [((rows, width), BF)] * 2, 0, 1)(parts)
     return (layer_out, tokens_grad, gate_g.T, up_g.T, down_g)
 

time: 138 us -> 138 us (level)
  no operation moved by 1% of the time
where the time goes in v8:
time: 138 us; the launch traced here: 137 us
  starting transfers between devices  74.4 us (54%)
  waiting for transfers between devices  31.2 us (23%)
  blocking collectives  18.7 us (14%)
  Pallas kernels  8.35 us (6%)
  local copies, waits for them, and re-layouts  2.76 us (2%)
    ppermute x9, starting transfers between devices, shift(): return lax.ppermute(x, ('col', 'depth'), pairs)  43.3 us
    ppermute x9, waiting for transfers between devices, shift(): return lax.ppermute(x, ('col', 'depth'), pairs)  28.2 us
    all_gather x1, blocking collectives, shards(): lax.all_gather(act, 'col', axis=0, tiled=True, axis_index_groups=strided)  18.7 us
    ppermute x6, starting transfers between devices, swap(): return lax.ppermute(x, 'depth', [(d, d ^ 1) for d in range(depth)])  18 us
    all_to_all x2, starting transfers between devices, exchange(): lax.all_to_all(x, GROUP, 0, 0, tiled=True, axis_index_groups=same_core)  13.1 us
    ppermute x6, waiting for transfers between devices, swap(): return lax.ppermute(x, 'depth', [(d, d ^ 1) for d in range(depth)])  3.02 us
  transfers between devices with their start and end apart: 17, of which 9 were waited for; matrix products, arithmetic and copies ran while one was open for 0% of the time, Pallas kernels for 2%

profile of v8, /device:TPU:1, one launch (start us, length us, event | category | flops | bytes accessed | tf_op | source)
XLA Modules:
  0.0 137.2 jit_solution(5459717713084817554)
XLA Ops:
  0.6 0.0 copy-start.2
  0.6 0.0 copy-start.3
  0.7 0.0 copy-start.4
  0.7 0.8 pad_maximum_fusion.both
  1.5 0.8 shard_map.92
  2.3 7.6 %all-to-all-start = ((bf16[16,16,1024]{2,1,0:T(8,128)(2,1)}), bf16[16,16,1024]{2,1,0:T(8,128)(2,1)S(1)}, u32[]{:S(2)}, u32[]{:S(2)}) async-start(bf16[16,16,1024]{2,1,0:T(8,128)(2,1)} %shard_map.92), calls=%async_computation | async-start | bytes 1048576 | tf_op jit(solution)/shard_map/all_to_all | solution.py:222
  9.9 4.8 %collective-permute-start = (bf16[448,512]{1,0:T(8,128)(2,1)}, bf16[448,512]{1,0:T(8,128)(2,1)S(1)}, u32[]{:S(2)}, u32[]{:S(2)}) collective-permute-start(bf16[448,512]{1,0:T(8,128)(2,1)} %bitcast.4), channel_id=1, source_target_pairs={{0,1},{1,0},{2,3},{3,2},{4,5},{5,4},{6,7},{7,6},{8,9},{9,8},{10,11... | collective-permute-start | bytes 1376264 | tf_op jit(solution)/shard_map/ppermute | solution.py:219
  14.7 1.9 %collective-permute-start.1 = (bf16[448,512]{1,0:T(8,128)(2,1)}, bf16[448,512]{1,0:T(8,128)(2,1)S(1)}, u32[]{:S(2)}, u32[]{:S(2)}) collective-permute-start(bf16[448,512]{1,0:T(8,128)(2,1)} %bitcast.6), channel_id=1, source_target_pairs={{0,1},{1,0},{2,3},{3,2},{4,5},{5,4},{6,7},{7,6},{8,9},{9,8},{10,11... | collective-permute-start | bytes 1376264 | tf_op jit(solution)/shard_map/ppermute | solution.py:219
  16.7 2.4 %collective-permute-start.2 = (bf16[448,512]{1,0:T(8,128)(2,1)}, bf16[448,512]{1,0:T(8,128)(2,1)S(1)}, u32[]{:S(2)}, u32[]{:S(2)}) collective-permute-start(bf16[448,512]{1,0:T(8,128)(2,1)} %down.1), channel_id=1, source_target_pairs={{0,1},{1,0},{2,3},{3,2},{4,5},{5,4},{6,7},{7,6},{8,9},{9,8},{10,11... | collective-permute-start | bytes 1376264 | tf_op jit(solution)/shard_map/ppermute | solution.py:219
  19.1 0.0 collective-permute-done.gate_away
  19.1 0.0 collective-permute-done.1.up_away
  19.1 1.6 %collective-permute-done.2.down_away = bf16[448,512]{1,0:T(8,128)(2,1)S(1)} collective-permute-done((bf16[448,512]{1,0:T(8,128)(2,1)}, bf16[448,512]{1,0:T(8,128)(2,1)S(1)}, u32[]{:S(2)}, u32[]{:S(2)}) %collective-permute-start.2) | collective-permute-done | bytes 458784 | tf_op jit(solution)/shard_map/ppermute | solution.py:219
  20.7 0.0 copy-done.2
  20.7 0.0 copy-done.3
  20.7 0.0 copy-done.4
  20.7 0.2 shard_map.93
  20.9 0.0 copy-start
  20.9 1.2 copy-done
  22.1 0.0 all-to-all-done.mine
  22.1 0.0 copy-start.1
  22.1 1.5 %copy-done.1 = bf16[1792,512]{1,0:T(8,128)(2,1)S(1)} copy-done((bf16[1792,512]{1,0:T(8,128)(2,1)S(1)}, bf16[1792,512]{1,0:T(8,128)(2,1)}, u32[]{:S(2)}) %copy-start.1) | copy-done | bytes 1835032
  23.6 1.5 %shard_map.94 = (bf16[64,2688]{1,0:T(8,128)(2,1)S(1)}, bf16[64,2688]{1,0:T(8,128)(2,1)S(1)}, bf16[64,2688]{1,0:T(8,128)(2,1)S(1)}, f32[64,2688]{1,0:T(8,128)S(1)...) custom-call(bf16[16,16,1024]{2,1,0:T(8,128)(2,1)S(1)} %all-to-all-done.mine, ...), custom_call_target="tpu_custom_call" | custom-call | tf_op jit(solution)/shard_map/pallas_call | solution.py:231
  25.1 9.2 %collective-permute-start.3 = (bf16[64,2688]{1,0:T(8,128)(2,1)S(1)}, bf16[64,2688]{1,0:T(8,128)(2,1)S(1)}, u32[]{:S(2)}, u32[]{:S(2)}) collective-permute-start(bf16[64,2688]{1,0:T(8,128)(2,1)S(1)} %get-tuple-element.34), channel_id=1, source_target_pairs={{0,8},{1,121},{2,10},{3,123},{4,12},{5,125},{6,14},{7,127},{8,16},... | collective-permute-start | bytes 1032200 | tf_op jit(solution)/shard_map/ppermute | solution.py:214
  34.3 1.9 %collective-permute-start.4 = (bf16[64,2688]{1,0:T(8,128)(2,1)S(1)}, bf16[64,2688]{1,0:T(8,128)(2,1)S(1)}, u32[]{:S(2)}, u32[]{:S(2)}) collective-permute-start(bf16[64,2688]{1,0:T(8,128)(2,1)S(1)} %get-tuple-element.35), channel_id=1, source_target_pairs={{0,120},{1,9},{2,122},{3,11},{4,124},{5,13},{6,126},{7,15},{8,0},{... | collective-permute-start | bytes 1032200 | tf_op jit(solution)/shard_map/ppermute | solution.py:214
  36.3 1.9 %collective-permute-start.5 = (bf16[64,2688]{1,0:T(8,128)(2,1)S(1)}, bf16[64,2688]{1,0:T(8,128)(2,1)S(1)}, u32[]{:S(2)}, u32[]{:S(2)}) collective-permute-start(bf16[64,2688]{1,0:T(8,128)(2,1)S(1)} %get-tuple-element.36), channel_id=1, source_target_pairs={{0,112},{1,17},{2,114},{3,19},{4,116},{5,21},{6,118},{7,23},{8,120... | collective-permute-start | bytes 1032200 | tf_op jit(solution)/shard_map/ppermute | solution.py:214
  38.2 0.3 collective-permute-done.3.first
  38.5 6.6 %collective-permute-done.4.second = bf16[64,2688]{1,0:T(8,128)(2,1)S(1)} collective-permute-done((bf16[64,2688]{1,0:T(8,128)(2,1)S(1)}, bf16[64,2688]{1,0:T(8,128)(2,1)S(1)}, u32[]{:S(2)}, u32[]{:S(2)}) %collective-permute-start.4) | collective-permute-done | bytes 344096 | tf_op jit(solution)/shard_map/ppermute | solution.py:214
  45.1 6.5 %collective-permute-done.5.third = bf16[64,2688]{1,0:T(8,128)(2,1)S(1)} collective-permute-done((bf16[64,2688]{1,0:T(8,128)(2,1)S(1)}, bf16[64,2688]{1,0:T(8,128)(2,1)S(1)}, u32[]{:S(2)}, u32[]{:S(2)}) %collective-permute-start.5) | collective-permute-done | bytes 344096 | tf_op jit(solution)/shard_map/ppermute | solution.py:214
  51.6 0.4 shard_map.95
  52.0 7.7 %collective-permute-start.6 = (bf16[16,2688]{1,0:T(8,128)(2,1)S(1)}, bf16[16,2688]{1,0:T(8,128)(2,1)S(1)}, u32[]{:S(2)}, u32[]{:S(2)}) collective-permute-start(bf16[16,2688]{1,0:T(8,128)(2,1)S(1)} %get-tuple-element.38), channel_id=1, source_target_pairs={{0,64},{1,65},{2,66},{3,67},{4,68},{5,69},{6,70},{7,71},{8,72},{9,... | collective-permute-start | bytes 258056 | tf_op jit(solution)/shard_map/ppermute | solution.py:214
  59.7 1.9 %collective-permute-start.7 = (bf16[16,2688]{1,0:T(8,128)(2,1)S(1)}, bf16[16,2688]{1,0:T(8,128)(2,1)S(1)}, u32[]{:S(2)}, u32[]{:S(2)}) collective-permute-start(bf16[16,2688]{1,0:T(8,128)(2,1)S(1)} %get-tuple-element.39), channel_id=1, source_target_pairs={{0,32},{1,97},{2,34},{3,99},{4,36},{5,101},{6,38},{7,103},{8,40},{... | collective-permute-start | bytes 258056 | tf_op jit(solution)/shard_map/ppermute | solution.py:214
  61.7 7.3 %collective-permute-start.8 = (bf16[16,2688]{1,0:T(8,128)(2,1)S(1)}, bf16[16,2688]{1,0:T(8,128)(2,1)S(1)}, u32[]{:S(2)}, u32[]{:S(2)}) collective-permute-start(bf16[16,2688]{1,0:T(8,128)(2,1)S(1)} %get-tuple-element.40), channel_id=1, source_target_pairs={{0,96},{1,33},{2,98},{3,35},{4,100},{5,37},{6,102},{7,39},{8,104},... | collective-permute-start | bytes 258056 | tf_op jit(solution)/shard_map/ppermute | solution.py:214
  69.0 2.1 %collective-permute-done.6.far = bf16[16,2688]{1,0:T(8,128)(2,1)S(1)} collective-permute-done((bf16[16,2688]{1,0:T(8,128)(2,1)S(1)}, bf16[16,2688]{1,0:T(8,128)(2,1)S(1)}, u32[]{:S(2)}, u32[]{:S(2)}) %collective-permute-start.6) | collective-permute-done | bytes 86048 | tf_op jit(solution)/shard_map/ppermute | solution.py:214
  71.1 2.7 %collective-permute-done.7.near = bf16[16,2688]{1,0:T(8,128)(2,1)S(1)} collective-permute-done((bf16[16,2688]{1,0:T(8,128)(2,1)S(1)}, bf16[16,2688]{1,0:T(8,128)(2,1)S(1)}, u32[]{:S(2)}, u32[]{:S(2)}) %collective-permute-start.7) | collective-permute-done | bytes 86048 | tf_op jit(solution)/shard_map/ppermute | solution.py:214
  73.7 0.0 collective-permute-done.8.back
  73.7 0.1 shard_map.96
  73.9 18.7 %all_gather.3.c0 = bf16[64,2688]{1,0:T(8,128)(2,1)S(1)} all-gather(bf16[16,2688]{1,0:T(8,128)(2,1)S(1)} %shard_map.96), channel_id=1, replica_groups={{0,32,64,96},{8,40,72,104},{16,48,80,112},{24,56,88,120},{1,33,65,97},{..., dimensions={0}, use_global_device_ids=true | all-gather | bytes 430080 | tf_op jit(solution)/shard_map/all_gather | solution.py:251
  92.6 6.5 %collective-permute-start.11 = (bf16[64,2688]{1,0:T(8,128)(2,1)S(1)}, bf16[64,2688]{1,0:T(8,128)(2,1)S(1)}, u32[]{:S(2)}, u32[]{:S(2)}) collective-permute-start(bf16[64,2688]{1,0:T(8,128)(2,1)S(1)} %all_gather.3.c0), channel_id=1, source_target_pairs={{0,16},{1,113},{2,18},{3,115},{4,20},{5,117},{6,22},{7,119},{8,24}... | collective-permute-start | bytes 1032200 | tf_op jit(solution)/shard_map/ppermute | solution.py:214
  99.1 4.9 %collective-permute-start.10 = (bf16[64,2688]{1,0:T(8,128)(2,1)S(1)}, bf16[64,2688]{1,0:T(8,128)(2,1)S(1)}, u32[]{:S(2)}, u32[]{:S(2)}) collective-permute-start(bf16[64,2688]{1,0:T(8,128)(2,1)S(1)} %all_gather.3.c0), channel_id=1, source_target_pairs={{0,120},{1,9},{2,122},{3,11},{4,124},{5,13},{6,126},{7,15},{8,0},{... | collective-permute-start | bytes 1032200 | tf_op jit(solution)/shard_map/ppermute | solution.py:214
  104.0 2.0 %collective-permute-start.9 = (bf16[64,2688]{1,0:T(8,128)(2,1)S(1)}, bf16[64,2688]{1,0:T(8,128)(2,1)S(1)}, u32[]{:S(2)}, u32[]{:S(2)}) collective-permute-start(bf16[64,2688]{1,0:T(8,128)(2,1)S(1)} %all_gather.3.c0), channel_id=1, source_target_pairs={{0,8},{1,121},{2,10},{3,123},{4,12},{5,125},{6,14},{7,127},{8,16},... | collective-permute-start | bytes 1032200 | tf_op jit(solution)/shard_map/ppermute | solution.py:214
  106.0 0.9 collective-permute-done.11.c3
  106.9 9.1 %collective-permute-done.10.c1 = bf16[64,2688]{1,0:T(8,128)(2,1)S(1)} collective-permute-done((bf16[64,2688]{1,0:T(8,128)(2,1)S(1)}, bf16[64,2688]{1,0:T(8,128)(2,1)S(1)}, u32[]{:S(2)}, u32[]{:S(2)}) %collective-permute-start.10) | collective-permute-done | bytes 344096 | tf_op jit(solution)/shard_map/ppermute | solution.py:214
  116.0 0.7 shard_map.97.early
  116.8 0.0 collective-permute-done.9.c2
  116.8 1.4 %shard_map.98 = bf16[16,16,1024]{2,1,0:T(8,128)(2,1)} custom-call(bf16[64,2688]{1,0:T(8,128)(2,1)S(1)} %collective-permute-done.9.c2, bf16[192,1024]{1,0:T(8,128)(2,1)S(1)} %shard_map.97.early, bf16[1792,512]{1,0:T(8,128)(2,1)S(1)} %get-tuple-element.41.pair, bf16[896,512]{1,0:T(8,128)(2,1)S(1)} %get-tuple-element.42.down), custom_call_target="tpu_custom_call" | custom-call | tf_op jit(solution)/shard_map/pallas_call | solution.py:263
  118.2 5.5 %all-to-all-start.1 = ((bf16[16,16,1024]{2,1,0:T(8,128)(2,1)}), bf16[16,16,1024]{2,1,0:T(8,128)(2,1)S(1)}, u32[]{:S(2)}, u32[]{:S(2)}) async-start(bf16[16,16,1024]{2,1,0:T(8,128)(2,1)} %shard_map.98), calls=%async_computation.1 | async-start | bytes 1048576 | tf_op jit(solution)/shard_map/all_to_all | solution.py:222
  123.7 0.7 shard_map.100
  124.4 4.6 %collective-permute-start.12 = (bf16[448,512]{1,0:T(8,128)(2,1)S(1)}, bf16[448,512]{1,0:T(8,128)(2,1)S(1)}, u32[]{:S(2)}, u32[]{:S(2)}) collective-permute-start(bf16[448,512]{1,0:T(8,128)(2,1)S(1)} %get-tuple-element.51), channel_id=1, source_target_pairs={{0,1},{1,0},{2,3},{3,2},{4,5},{5,4},{6,7},{7,6},{8,9},{9,8},{10,11... | collective-permute-start | bytes 1376264 | tf_op jit(solution)/shard_map/ppermute | solution.py:219
  129.0 1.9 %collective-permute-start.13 = (bf16[448,512]{1,0:T(8,128)(2,1)S(1)}, bf16[448,512]{1,0:T(8,128)(2,1)S(1)}, u32[]{:S(2)}, u32[]{:S(2)}) collective-permute-start(bf16[448,512]{1,0:T(8,128)(2,1)S(1)} %get-tuple-element.52), channel_id=1, source_target_pairs={{0,1},{1,0},{2,3},{3,2},{4,5},{5,4},{6,7},{7,6},{8,9},{9,8},{10,11... | collective-permute-start | bytes 1376264 | tf_op jit(solution)/shard_map/ppermute | solution.py:219
  130.9 2.4 %collective-permute-start.14 = (bf16[448,512]{1,0:T(8,128)(2,1)S(1)}, bf16[448,512]{1,0:T(8,128)(2,1)S(1)}, u32[]{:S(2)}, u32[]{:S(2)}) collective-permute-start(bf16[448,512]{1,0:T(8,128)(2,1)S(1)} %get-tuple-element.53), channel_id=1, source_target_pairs={{0,1},{1,0},{2,3},{3,2},{4,5},{5,4},{6,7},{7,6},{8,9},{9,8},{10,11... | collective-permute-start | bytes 1376264 | tf_op jit(solution)/shard_map/ppermute | solution.py:219
  133.3 0.0 collective-permute-done.12.a0
  133.3 0.0 collective-permute-done.13.a1
  133.3 1.4 %collective-permute-done.14.a2 = bf16[448,512]{1,0:T(8,128)(2,1)S(1)} collective-permute-done((bf16[448,512]{1,0:T(8,128)(2,1)S(1)}, bf16[448,512]{1,0:T(8,128)(2,1)S(1)}, u32[]{:S(2)}, u32[]{:S(2)}) %collective-permute-start.14) | collective-permute-done | bytes 458784 | tf_op jit(solution)/shard_map/ppermute | solution.py:219
  134.7 1.8 %shard_map.101 = (bf16[448,512]{1,0:T(8,128)(2,1)}, bf16[448,512]{1,0:T(8,128)(2,1)}, bf16[448,512]{1,0:T(8,128)(2,1)}) custom-call(bf16[64,2688]{1,0:T(8,128)(2,1)S(1)} %all_gather.3.c0, bf16[64,2688]{1,0:T(8,128)(2,1)S(1)} %collective-permute-done.10.c1, bf16[64,2688]{1,0:T(8,128)(2,1)S(1)} %collective-permute-done.9.c2, ...), custom_call_target="tpu_custom_call" | custom-call | tf_op jit(solution)/shard_map/pallas_call | solution.py:276
  136.5 0.0 all-to-all-done.1.parts
  136.5 0.7 shard_map.99
Async XLA Ops:
  0.6 20.1 %copy-start.2 = (bf16[512,448]{0,1:T(8,128)(2,1)S(1)}, bf16[512,448]{0,1:T(8,128)(2,1)}, u32[]{:S(2)}) copy-start(bf16[512,448]{0,1:T(8,128)(2,1)} %param.7) | copy-start | bytes 1376260
  0.6 20.1 %copy-start.3 = (bf16[512,448]{0,1:T(8,128)(2,1)S(1)}, bf16[512,448]{0,1:T(8,128)(2,1)}, u32[]{:S(2)}) copy-start(bf16[512,448]{0,1:T(8,128)(2,1)} %param.8) | copy-start | bytes 1376260
  0.7 20.1 %copy-start.4 = (bf16[448,512]{1,0:T(8,128)(2,1)S(1)}, bf16[448,512]{1,0:T(8,128)(2,1)}, u32[]{:S(2)}) copy-start(bf16[448,512]{1,0:T(8,128)(2,1)} %down.1) | copy-start | bytes 1376260
  2.3 19.8 %all-to-all-start = ((bf16[16,16,1024]{2,1,0:T(8,128)(2,1)}), bf16[16,16,1024]{2,1,0:T(8,128)(2,1)S(1)}, u32[]{:S(2)}, u32[]{:S(2)}) async-start(bf16[16,16,1024]{2,1,0:T(8,128)(2,1)} %shard_map.92), calls=%async_computation | async-start | bytes 1048576 | tf_op jit(solution)/shard_map/all_to_all | solution.py:222
  9.9 9.1 %collective-permute-start = (bf16[448,512]{1,0:T(8,128)(2,1)}, bf16[448,512]{1,0:T(8,128)(2,1)S(1)}, u32[]{:S(2)}, u32[]{:S(2)}) collective-permute-start(bf16[448,512]{1,0:T(8,128)(2,1)} %bitcast.4), channel_id=1, source_target_pairs={{0,1},{1,0},{2,3},{3,2},{4,5},{5,4},{6,7},{7,6},{8,9},{9,8},{10,11... | collective-permute-start | bytes 1376264 | tf_op jit(solution)/shard_map/ppermute | solution.py:219
  14.7 4.4 %collective-permute-start.1 = (bf16[448,512]{1,0:T(8,128)(2,1)}, bf16[448,512]{1,0:T(8,128)(2,1)S(1)}, u32[]{:S(2)}, u32[]{:S(2)}) collective-permute-start(bf16[448,512]{1,0:T(8,128)(2,1)} %bitcast.6), channel_id=1, source_target_pairs={{0,1},{1,0},{2,3},{3,2},{4,5},{5,4},{6,7},{7,6},{8,9},{9,8},{10,11... | collective-permute-start | bytes 1376264 | tf_op jit(solution)/shard_map/ppermute | solution.py:219
  16.7 4.0 %collective-permute-start.2 = (bf16[448,512]{1,0:T(8,128)(2,1)}, bf16[448,512]{1,0:T(8,128)(2,1)S(1)}, u32[]{:S(2)}, u32[]{:S(2)}) collective-permute-start(bf16[448,512]{1,0:T(8,128)(2,1)} %down.1), channel_id=1, source_target_pairs={{0,1},{1,0},{2,3},{3,2},{4,5},{5,4},{6,7},{7,6},{8,9},{9,8},{10,11... | collective-permute-start | bytes 1376264 | tf_op jit(solution)/shard_map/ppermute | solution.py:219
  20.9 1.2 copy-start
  22.1 1.5 %copy-start.1 = (bf16[1792,512]{1,0:T(8,128)(2,1)S(1)}, bf16[1792,512]{1,0:T(8,128)(2,1)}, u32[]{:S(2)}) copy-start(bf16[1792,512]{1,0:T(8,128)(2,1)} %copy-done) | copy-start | bytes 5505028
  25.1 13.4 %collective-permute-start.3 = (bf16[64,2688]{1,0:T(8,128)(2,1)S(1)}, bf16[64,2688]{1,0:T(8,128)(2,1)S(1)}, u32[]{:S(2)}, u32[]{:S(2)}) collective-permute-start(bf16[64,2688]{1,0:T(8,128)(2,1)S(1)} %get-tuple-element.34), channel_id=1, source_target_pairs={{0,8},{1,121},{2,10},{3,123},{4,12},{5,125},{6,14},{7,127},{8,16},... | collective-permute-start | bytes 1032200 | tf_op jit(solution)/shard_map/ppermute | solution.py:214
  34.3 10.8 %collective-permute-start.4 = (bf16[64,2688]{1,0:T(8,128)(2,1)S(1)}, bf16[64,2688]{1,0:T(8,128)(2,1)S(1)}, u32[]{:S(2)}, u32[]{:S(2)}) collective-permute-start(bf16[64,2688]{1,0:T(8,128)(2,1)S(1)} %get-tuple-element.35), channel_id=1, source_target_pairs={{0,120},{1,9},{2,122},{3,11},{4,124},{5,13},{6,126},{7,15},{8,0},{... | collective-permute-start | bytes 1032200 | tf_op jit(solution)/shard_map/ppermute | solution.py:214
  36.3 15.3 %collective-permute-start.5 = (bf16[64,2688]{1,0:T(8,128)(2,1)S(1)}, bf16[64,2688]{1,0:T(8,128)(2,1)S(1)}, u32[]{:S(2)}, u32[]{:S(2)}) collective-permute-start(bf16[64,2688]{1,0:T(8,128)(2,1)S(1)} %get-tuple-element.36), channel_id=1, source_target_pairs={{0,112},{1,17},{2,114},{3,19},{4,116},{5,21},{6,118},{7,23},{8,120... | collective-permute-start | bytes 1032200 | tf_op jit(solution)/shard_map/ppermute | solution.py:214
  52.0 19.0 %collective-permute-start.6 = (bf16[16,2688]{1,0:T(8,128)(2,1)S(1)}, bf16[16,2688]{1,0:T(8,128)(2,1)S(1)}, u32[]{:S(2)}, u32[]{:S(2)}) collective-permute-start(bf16[16,2688]{1,0:T(8,128)(2,1)S(1)} %get-tuple-element.38), channel_id=1, source_target_pairs={{0,64},{1,65},{2,66},{3,67},{4,68},{5,69},{6,70},{7,71},{8,72},{9,... | collective-permute-start | bytes 258056 | tf_op jit(solution)/shard_map/ppermute | solution.py:214
  59.7 14.0 %collective-permute-start.7 = (bf16[16,2688]{1,0:T(8,128)(2,1)S(1)}, bf16[16,2688]{1,0:T(8,128)(2,1)S(1)}, u32[]{:S(2)}, u32[]{:S(2)}) collective-permute-start(bf16[16,2688]{1,0:T(8,128)(2,1)S(1)} %get-tuple-element.39), channel_id=1, source_target_pairs={{0,32},{1,97},{2,34},{3,99},{4,36},{5,101},{6,38},{7,103},{8,40},{... | collective-permute-start | bytes 258056 | tf_op jit(solution)/shard_map/ppermute | solution.py:214
  61.7 12.1 %collective-permute-start.8 = (bf16[16,2688]{1,0:T(8,128)(2,1)S(1)}, bf16[16,2688]{1,0:T(8,128)(2,1)S(1)}, u32[]{:S(2)}, u32[]{:S(2)}) collective-permute-start(bf16[16,2688]{1,0:T(8,128)(2,1)S(1)} %get-tuple-element.40), channel_id=1, source_target_pairs={{0,96},{1,33},{2,98},{3,35},{4,100},{5,37},{6,102},{7,39},{8,104},... | collective-permute-start | bytes 258056 | tf_op jit(solution)/shard_map/ppermute | solution.py:214
  92.6 14.3 %collective-permute-start.11 = (bf16[64,2688]{1,0:T(8,128)(2,1)S(1)}, bf16[64,2688]{1,0:T(8,128)(2,1)S(1)}, u32[]{:S(2)}, u32[]{:S(2)}) collective-permute-start(bf16[64,2688]{1,0:T(8,128)(2,1)S(1)} %all_gather.3.c0), channel_id=1, source_target_pairs={{0,16},{1,113},{2,18},{3,115},{4,20},{5,117},{6,22},{7,119},{8,24}... | collective-permute-start | bytes 1032200 | tf_op jit(solution)/shard_map/ppermute | solution.py:214
  99.1 16.9 %collective-permute-start.10 = (bf16[64,2688]{1,0:T(8,128)(2,1)S(1)}, bf16[64,2688]{1,0:T(8,128)(2,1)S(1)}, u32[]{:S(2)}, u32[]{:S(2)}) collective-permute-start(bf16[64,2688]{1,0:T(8,128)(2,1)S(1)} %all_gather.3.c0), channel_id=1, source_target_pairs={{0,120},{1,9},{2,122},{3,11},{4,124},{5,13},{6,126},{7,15},{8,0},{... | collective-permute-start | bytes 1032200 | tf_op jit(solution)/shard_map/ppermute | solution.py:214
  104.0 12.8 %collective-permute-start.9 = (bf16[64,2688]{1,0:T(8,128)(2,1)S(1)}, bf16[64,2688]{1,0:T(8,128)(2,1)S(1)}, u32[]{:S(2)}, u32[]{:S(2)}) collective-permute-start(bf16[64,2688]{1,0:T(8,128)(2,1)S(1)} %all_gather.3.c0), channel_id=1, source_target_pairs={{0,8},{1,121},{2,10},{3,123},{4,12},{5,125},{6,14},{7,127},{8,16},... | collective-permute-start | bytes 1032200 | tf_op jit(solution)/shard_map/ppermute | solution.py:214
  118.2 18.3 %all-to-all-start.1 = ((bf16[16,16,1024]{2,1,0:T(8,128)(2,1)}), bf16[16,16,1024]{2,1,0:T(8,128)(2,1)S(1)}, u32[]{:S(2)}, u32[]{:S(2)}) async-start(bf16[16,16,1024]{2,1,0:T(8,128)(2,1)} %shard_map.98), calls=%async_computation.1 | async-start | bytes 1048576 | tf_op jit(solution)/shard_map/all_to_all | solution.py:222
  124.4 8.9 %collective-permute-start.12 = (bf16[448,512]{1,0:T(8,128)(2,1)S(1)}, bf16[448,512]{1,0:T(8,128)(2,1)S(1)}, u32[]{:S(2)}, u32[]{:S(2)}) collective-permute-start(bf16[448,512]{1,0:T(8,128)(2,1)S(1)} %get-tuple-element.51), channel_id=1, source_target_pairs={{0,1},{1,0},{2,3},{3,2},{4,5},{5,4},{6,7},{7,6},{8,9},{9,8},{10,11... | collective-permute-start | bytes 1376264 | tf_op jit(solution)/shard_map/ppermute | solution.py:219
  129.0 4.4 %collective-permute-start.13 = (bf16[448,512]{1,0:T(8,128)(2,1)S(1)}, bf16[448,512]{1,0:T(8,128)(2,1)S(1)}, u32[]{:S(2)}, u32[]{:S(2)}) collective-permute-start(bf16[448,512]{1,0:T(8,128)(2,1)S(1)} %get-tuple-element.52), channel_id=1, source_target_pairs={{0,1},{1,0},{2,3},{3,2},{4,5},{5,4},{6,7},{7,6},{8,9},{9,8},{10,11... | collective-permute-start | bytes 1376264 | tf_op jit(solution)/shard_map/ppermute | solution.py:219
  130.9 3.8 %collective-permute-start.14 = (bf16[448,512]{1,0:T(8,128)(2,1)S(1)}, bf16[448,512]{1,0:T(8,128)(2,1)S(1)}, u32[]{:S(2)}, u32[]{:S(2)}) collective-permute-start(bf16[448,512]{1,0:T(8,128)(2,1)S(1)} %get-tuple-element.53), channel_id=1, source_target_pairs={{0,1},{1,0},{2,3},{3,2},{4,5},{5,4},{6,7},{7,6},{8,9},{9,8},{10,11... | collective-permute-start | bytes 1376264 | tf_op jit(solution)/shard_map/ppermute | solution.py:219
